TPU v7x, 32 devices: a whole 2x2x4 slice. The times are simulated.
32 devices in a mesh: dp: 16 (over z, y, x), tensor: 2 (over core).
Axes of the slice: x: 2, y: 2, z: 4, core: 2. Of those that a mesh axis runs over, the one named last changes fastest.
Arguments:
- source_tokens: bfloat16 [16384, 768], P('dp'), may hold values from -6 to 6
- target_tokens: bfloat16 [8192, 768], P('dp'), may hold values from -6 to 6
- target_cotangent: bfloat16 [8192, 768], P('dp'), may hold values from -6 to 6
- retrieved: int32 [16, 1024], P('dp'), may hold values from 0 to 8191, as said below
- kept_mask: int32 [16384], P('dp'), may hold values from 0 to 1, as said below
- owner_slots: int32 [504], replicated, may hold values from 0 to 511, as said below
- master: float32 [2, 512, 128, 128], P('tensor', 'dp'), may hold values from -1.299038 to 1.299038
- first_moment: float32 [2, 512, 128, 128], P('tensor', 'dp'), may hold values from -80 to 80
- second_moment: float32 [2, 512, 128, 128], P('tensor', 'dp'), may hold values from 819.2 to 3276.8
- left_stats: float32 [2, 512, 128, 128], P('tensor', 'dp'), may hold values from -491.52 to 419430.4, as said below
- right_stats: float32 [2, 512, 128, 128], P('tensor', 'dp'), may hold values from -491.52 to 419430.4, as said below
- left_basis: float32 [2, 512, 128, 128], P('tensor', 'dp'), may hold values from -1.001 to 1.001, as said below
- right_basis: float32 [2, 512, 128, 128], P('tensor', 'dp'), may hold values from -1.001 to 1.001, as said below
- shared_vectors: float32 [15, 768], P(None, 'dp'), may hold values from -1.8 to 1.8
- shared_first: float32 [15, 768], P(None, 'dp'), may hold values from -80 to 80
- shared_second: float32 [15, 768], P(None, 'dp'), may hold values from 819.2 to 3276.8
- split_vectors: float32 [2, 7, 768], P('tensor', None, 'dp'), may hold values from -4 to 4
- split_first: float32 [2, 7, 768], P('tensor', None, 'dp'), may hold values from -80 to 80
- split_second: float32 [2, 7, 768], P('tensor', None, 'dp'), may hold values from 819.2 to 3276.8
Outputs:
- encoder_states: float32 [16384, 768], P('dp')
- decoder_states: float32 [8192, 768], P('dp')
- source_grad: float32 [16384, 768], P('dp')
- target_grad: float32 [8192, 768], P('dp')
- new_master: float32 [2, 512, 128, 128], P('tensor', 'dp')
- new_first: float32 [2, 512, 128, 128], P('tensor', 'dp')
- new_second: float32 [2, 512, 128, 128], P('tensor', 'dp')
- new_left_stats: float32 [2, 512, 128, 128], P('tensor', 'dp')
- new_right_stats: float32 [2, 512, 128, 128], P('tensor', 'dp')
- new_left_basis: float32 [2, 512, 128, 128], P('tensor', 'dp')
- new_right_basis: float32 [2, 512, 128, 128], P('tensor', 'dp')
- shared_new_first: float32 [15, 768], P(None, 'dp')
- shared_new_second: float32 [15, 768], P(None, 'dp')
- shared_updated: float32 [15, 768], P(None, 'dp')
- split_new_first: float32 [2, 7, 768], P('tensor', None, 'dp')
- split_new_second: float32 [2, 7, 768], P('tensor', None, 'dp')
- split_updated: float32 [2, 7, 768], P('tensor', None, 'dp')
Inputs may be any that keep to these rules, and one draw needn't show every extreme that they name: `retrieved`: in each row, entries j * 64 to (j + 1) * 64 - 1 are distinct datastore rows of j * 512 to (j + 1) * 512 - 1, j from 0. `kept_mask`: in each group the ones form one run of exactly 512 positions; in the first group it starts at the group's start, in the last it ends at the group's end. `owner_slots`: distinct slots. `left_stats`: each block is symmetric positive definite. `right_stats`: each block is symmetric positive definite. `left_basis`: each block is orthogonal up to rounding. `right_basis`: each block is orthogonal up to rounding.
All inputs are finite; a program needn't handle non-finite values.
Results may differ from a plain program's by a relative error of at most 0.035.
Values may be sent and summed in bfloat16 or wider, within the bound.
A program may use at most 384 MiB of HBM per device.

v0:
```python
from functools import partial

import jax
import jax.numpy as jnp
from jax import lax
from jax.sharding import PartitionSpec as P

HD = 64
KEEP = 512
STEP = 10


MATMUL_ACCURACY = lax.Precision.HIGHEST
BETA_ONE = 0.9
BETA_TWO = 0.95
ADAM_EPSILON = 1e-08
MATRIX_RATE = 0.1
VECTOR_RATE = 0.5
WEIGHT_DECAY = 0.01
NORM_EPSILON = 1e-05


def for_sending(x):

    def short(part):
        return part.astype(jnp.bfloat16) if part.dtype == jnp.float32 else part

    return jax.tree.map(short, x)


def matrix_list(model_width, hidden_width, tensor_count):
    half_width = model_width // tensor_count
    hidden_half = hidden_width // tensor_count
    return [
        ("enc_qkv", model_width, 3 * half_width),
        ("enc_out", half_width, model_width),
        ("enc_up", model_width, hidden_half),
        ("enc_down", hidden_half, model_width),
        ("dec_qkv", model_width, 3 * half_width),
        ("dec_out", half_width, model_width),
        ("crs_q", model_width, half_width),
        ("crs_kv", model_width, 2 * half_width),
        ("crs_out", half_width, model_width),
        ("dec_up", model_width, hidden_half),
        ("dec_down", hidden_half, model_width),
    ]


def unpack(blocks, model_width, hidden_width, tensor_count):
    tile_size = blocks.shape[-1]
    matrices = {}
    offset = 0
    for matrix_name, height, breadth in matrix_list(model_width, hidden_width, tensor_count):
        block_count = height // tile_size * (breadth // tile_size)
        pieces = blocks[offset : offset + block_count].reshape(
            height // tile_size, breadth // tile_size, tile_size, tile_size
        )
        matrices[matrix_name] = pieces.transpose(0, 2, 1, 3).reshape(height, breadth)
        offset = offset + block_count
    return matrices


def pack(matrices, model_width, hidden_width, tensor_count, tile_size):
    pieces = []
    for matrix_name, height, breadth in matrix_list(model_width, hidden_width, tensor_count):
        shaped = matrices[matrix_name].reshape(
            height // tile_size, tile_size, breadth // tile_size, tile_size
        )
        pieces.append(shaped.transpose(0, 2, 1, 3).reshape(-1, tile_size, tile_size))
    return jnp.concatenate(pieces, 0)


def split_biases(flat_vector, half_width, hidden_half):
    layout = [
        ("enc_q", half_width),
        ("enc_v", half_width),
        ("enc_up", hidden_half),
        ("dec_q", half_width),
        ("dec_v", half_width),
        ("crs_q", half_width),
        ("crs_v", half_width),
        ("dec_up", hidden_half),
    ]
    result = {}
    offset = 0
    for label_name, length in layout:
        result[label_name] = flat_vector[offset : offset + length]
        offset = offset + length
    return result


def layer_norm(values, gain, shift):
    center = values - jnp.mean(values, -1, keepdims=True)
    spread = jnp.mean(center * center, -1, keepdims=True)
    return center * lax.rsqrt(spread + NORM_EPSILON) * gain + shift


def project(left, right):
    return jnp.dot(left, right, preferred_element_type=jnp.float32)


def inner_rows(left, right):
    return jnp.einsum("sa,sb->ab", left, right, preferred_element_type=jnp.float32)


def times_transposed(left, right):
    return jnp.einsum("sa,ba->sb", left, right, preferred_element_type=jnp.float32)


def tensor_sum(values):
    return lax.psum(values.astype(jnp.bfloat16), "tensor").astype(jnp.float32)


def tensor_back(values):
    return jax.tree.map(
        lambda part: part.astype(jnp.float32), lax.psum(for_sending(values), "tensor")
    )


def raw_scores(query_rows, keys, causal):
    scale = query_rows.shape[-1] ** (-0.5)
    scores = (
        jnp.einsum("bqhe,bkhe->bhqk", query_rows, keys, preferred_element_type=jnp.float32) * scale
    )
    if causal:
        query_pos = lax.broadcasted_iota(jnp.int32, scores.shape, 2)
        key_pos = lax.broadcasted_iota(jnp.int32, scores.shape, 3)
        scores = jnp.where(key_pos <= query_pos, scores, -1000000000.0)
    return scores


def attend_forward(query_rows, keys, values, causal):
    scores = raw_scores(query_rows, keys, causal)
    totals = jax.nn.logsumexp(scores, axis=-1, keepdims=True)
    probs = jnp.exp(scores - totals)
    attended = jnp.einsum(
        "bhqk,bkhe->bqhe", probs.astype(jnp.bfloat16), values, preferred_element_type=jnp.float32
    )
    return (attended.astype(jnp.bfloat16), totals)


def attend_backward(query_rows, keys, values, totals, grad_out, causal):
    scale = query_rows.shape[-1] ** (-0.5)
    probs = jnp.exp(raw_scores(query_rows, keys, causal) - totals)
    grad_values = jnp.einsum(
        "bhqk,bqhe->bkhe", probs.astype(jnp.bfloat16), grad_out, preferred_element_type=jnp.float32
    )
    grad_probs = jnp.einsum("bqhe,bkhe->bhqk", grad_out, values, preferred_element_type=jnp.float32)
    grad_scores = (probs * (grad_probs - jnp.sum(grad_probs * probs, -1, keepdims=True))).astype(
        jnp.bfloat16
    )
    grad_queries = (
        jnp.einsum("bhqk,bkhe->bqhe", grad_scores, keys, preferred_element_type=jnp.float32) * scale
    )
    grad_keys = (
        jnp.einsum("bhqk,bqhe->bkhe", grad_scores, query_rows, preferred_element_type=jnp.float32)
        * scale
    )
    return (grad_queries, grad_keys, grad_values)


def self_forward(inputs_low, weight_qkv, bias_qkv, output_weight, causal):
    length = inputs_low.shape[0]
    part_width = weight_qkv.shape[1] // 3
    blended_output = (project(inputs_low, weight_qkv) + bias_qkv).astype(jnp.bfloat16)
    head_shape = (1, length, part_width // HD, HD)
    query_rows = blended_output[:, :part_width].reshape(head_shape)
    keys = blended_output[:, part_width : 2 * part_width].reshape(head_shape)
    values = blended_output[:, 2 * part_width :].reshape(head_shape)
    attended, totals = attend_forward(query_rows, keys, values, causal)
    combined_heads = attended.reshape(length, part_width)
    return (
        project(combined_heads, output_weight),
        (query_rows, keys, values, totals, combined_heads),
    )


def self_backward(grad_pre, inputs_low, saved, weight_qkv, output_weight, causal):
    query_rows, keys, values, totals, combined_heads = saved
    length = inputs_low.shape[0]
    part_width = combined_heads.shape[1]
    grad_branch = grad_pre.astype(jnp.bfloat16)
    grad_wout = inner_rows(combined_heads, grad_branch)
    grad_merged = (
        times_transposed(grad_branch, output_weight).astype(jnp.bfloat16).reshape(query_rows.shape)
    )
    grad_q, grad_k, grad_v = attend_backward(query_rows, keys, values, totals, grad_merged, causal)
    grad_mixed = jnp.concatenate(
        [
            grad_q.reshape(length, part_width),
            grad_k.reshape(length, part_width),
            grad_v.reshape(length, part_width),
        ],
        1,
    ).astype(jnp.bfloat16)
    grad_wqkv = inner_rows(inputs_low, grad_mixed)
    bias_sums = jnp.sum(grad_mixed.astype(jnp.float32), 0)
    part_input = times_transposed(grad_mixed, weight_qkv)
    return (grad_wqkv, bias_sums[:part_width], bias_sums[2 * part_width :], grad_wout, part_input)


def ffn_forward(hidden_low, weight_up, bias_up, weight_down):
    upward = project(hidden_low, weight_up) + bias_up
    active = jax.nn.gelu(upward, approximate=False).astype(jnp.bfloat16)
    return (project(active, weight_down), (upward, active))


def ffn_backward(grad_pre, hidden_low, saved, weight_up, weight_down):
    upward, active = saved
    grad_down = grad_pre.astype(jnp.bfloat16)
    grad_wdown = inner_rows(active, grad_down)
    grad_active = times_transposed(grad_down, weight_down)
    gelu_back = jax.vjp(partial(jax.nn.gelu, approximate=False), upward)[1]
    grad_up = gelu_back(grad_active)[0].astype(jnp.bfloat16)
    grad_wup = inner_rows(hidden_low, grad_up)
    grad_bias = jnp.sum(grad_up.astype(jnp.float32), 0)
    return (grad_wup, grad_bias, grad_wdown, times_transposed(grad_up, weight_up))


def cross_forward(
    query_inputs,
    retrieved_entries,
    query_weight,
    query_bias_vector,
    key_value_weight,
    bias_v,
    output_weight,
):
    blocks, qrow_count, model_width = query_inputs.shape
    part_width = query_weight.shape[1]
    query_rows = (
        jnp.einsum("kpl,le->kpe", query_inputs, query_weight, preferred_element_type=jnp.float32)
        + query_bias_vector
    )
    query_rows = query_rows.astype(jnp.bfloat16).reshape(blocks, qrow_count, part_width // HD, HD)
    key_value_bias = jnp.concatenate([jnp.zeros((part_width,), jnp.float32), bias_v])
    blended_output = (
        jnp.einsum(
            "uwo,ot->uwt", retrieved_entries, key_value_weight, preferred_element_type=jnp.float32
        )
        + key_value_bias
    ).astype(jnp.bfloat16)
    keys = blended_output[..., :part_width].reshape(blocks, -1, part_width // HD, HD)
    values = blended_output[..., part_width:].reshape(blocks, -1, part_width // HD, HD)
    attended, totals = attend_forward(query_rows, keys, values, False)
    combined_heads = attended.reshape(blocks * qrow_count, part_width)
    return (
        project(combined_heads, output_weight),
        (query_rows, keys, values, totals, combined_heads),
    )


def cross_backward(
    grad_pre, first_low, retrieved_entries, saved, query_weight, key_value_weight, output_weight
):
    query_rows, keys, values, totals, combined_heads = saved
    part_width = combined_heads.shape[1]
    grad_branch = grad_pre.astype(jnp.bfloat16)
    grad_wout = inner_rows(combined_heads, grad_branch)
    grad_merged = (
        times_transposed(grad_branch, output_weight).astype(jnp.bfloat16).reshape(query_rows.shape)
    )
    grad_q, grad_k, grad_v = attend_backward(query_rows, keys, values, totals, grad_merged, False)
    grad_query = grad_q.reshape(-1, part_width).astype(jnp.bfloat16)
    grad_wq = inner_rows(first_low, grad_query)
    grad_bq = jnp.sum(grad_query.astype(jnp.float32), 0)
    grad_kv = jnp.concatenate(
        [grad_k.reshape(-1, part_width), grad_v.reshape(-1, part_width)], 1
    ).astype(jnp.bfloat16)
    fetched_rows = retrieved_entries.reshape(-1, retrieved_entries.shape[-1])
    grad_wkv = inner_rows(fetched_rows, grad_kv)
    grad_bv = jnp.sum(grad_kv[:, part_width:].astype(jnp.float32), 0)
    part_first = times_transposed(grad_query, query_weight)
    part_fetched = times_transposed(grad_kv, key_value_weight).reshape(retrieved_entries.shape)
    return (grad_wq, grad_bq, grad_wkv, grad_bv, grad_wout, part_first, part_fetched)


def orthonormal(matrix):
    gram = jnp.matmul(matrix.T, matrix, precision=MATMUL_ACCURACY)
    factor = jnp.linalg.cholesky(gram)
    return jax.scipy.linalg.solve_triangular(factor, matrix.T, lower=True).T


def soap_update(
    grad_block,
    weight_block,
    first_block,
    second_block,
    left_block,
    right_block,
    left_turn,
    right_turn,
):
    product = partial(jnp.matmul, precision=MATMUL_ACCURACY)
    rotated = product(product(left_turn.T, grad_block), right_turn)
    new_first = BETA_ONE * first_block + (1.0 - BETA_ONE) * grad_block
    new_second = BETA_TWO * second_block + (1.0 - BETA_TWO) * rotated * rotated
    first_rotated = product(product(left_turn.T, new_first), right_turn)
    correct_one = 1.0 - BETA_ONE**STEP
    correct_two = 1.0 - BETA_TWO**STEP
    normed = first_rotated / correct_one / (jnp.sqrt(new_second / correct_two) + ADAM_EPSILON)
    new_weight = (
        weight_block
        - MATRIX_RATE * product(product(left_turn, normed), right_turn.T)
        - MATRIX_RATE * WEIGHT_DECAY * weight_block
    )
    new_left = BETA_TWO * left_block + (1.0 - BETA_TWO) * product(grad_block, grad_block.T)
    new_right = BETA_TWO * right_block + (1.0 - BETA_TWO) * product(grad_block.T, grad_block)
    return (
        new_first,
        new_second,
        new_weight,
        new_left,
        new_right,
        orthonormal(product(new_left, left_turn)),
        orthonormal(product(new_right, right_turn)),
    )


def adam_vector(grad_value, value, first, second):
    new_first = BETA_ONE * first + (1.0 - BETA_ONE) * grad_value
    new_second = BETA_TWO * second + (1.0 - BETA_TWO) * grad_value * grad_value
    correct_one = 1.0 - BETA_ONE**STEP
    correct_two = 1.0 - BETA_TWO**STEP
    updated = value - VECTOR_RATE * (new_first / correct_one) / (
        jnp.sqrt(new_second / correct_two) + ADAM_EPSILON
    )
    return (new_first, new_second, updated)


def local(
    source_tokens,
    target_tokens,
    target_cotangent,
    retrieved,
    kept_mask,
    owner_slots,
    master,
    first_moment,
    second_moment,
    left_stats,
    right_stats,
    left_basis,
    right_basis,
    shared_vectors,
    shared_first,
    shared_second,
    split_vectors,
    split_first,
    split_second,
):
    tensor_count = lax.axis_size("tensor")
    device_count = lax.axis_size("dp")
    model_width = source_tokens.shape[1]
    tile_size = master.shape[2]
    hidden_width = (split_vectors.shape[1] - 3) * model_width
    half_width = model_width // tensor_count
    hidden_half = hidden_width // tensor_count
    qblocks = retrieved.shape[0]
    per_owner = retrieved.shape[1] // device_count
    gathered, shared_whole, split_whole = (
        lax.all_gather(master[0].astype(jnp.bfloat16), "dp", axis=0, tiled=True),
        lax.all_gather(shared_vectors.astype(jnp.bfloat16), "dp", axis=1, tiled=True),
        lax.all_gather(split_vectors[0].astype(jnp.bfloat16), "dp", axis=1, tiled=True),
    )
    weights = unpack(
        jnp.take(gathered, owner_slots, axis=0), model_width, hidden_width, tensor_count
    )
    shared = shared_whole.astype(jnp.float32)
    biases = split_biases(split_whole.astype(jnp.float32).reshape(-1), half_width, hidden_half)
    zero_half = jnp.zeros((half_width,), jnp.float32)
    source_float = source_tokens.astype(jnp.float32)
    enc_bias = jnp.concatenate([biases["enc_q"], zero_half, biases["enc_v"]])
    enc_branch, enc_saved = self_forward(
        source_tokens, weights["enc_qkv"], enc_bias, weights["enc_out"], False
    )
    pre_one = source_float + tensor_sum(enc_branch) + shared[0]
    hidden_one, norm_one_back = jax.vjp(layer_norm, pre_one, shared[1], shared[2])
    hidden_low = hidden_one.astype(jnp.bfloat16)
    enc_feed, enc_feed_saved = ffn_forward(
        hidden_low, weights["enc_up"], biases["enc_up"], weights["enc_down"]
    )
    pre_two = hidden_one + tensor_sum(enc_feed) + shared[3]
    encoder_states, norm_two_back = jax.vjp(layer_norm, pre_two, shared[4], shared[5])
    start_row = jnp.argmax(kept_mask)
    stored = lax.dynamic_slice_in_dim(encoder_states.astype(jnp.bfloat16), start_row, KEEP, 0)
    owner_base = KEEP * lax.broadcasted_iota(jnp.int32, (1, device_count, 1), 1)
    wanted = lax.all_to_all(
        retrieved.reshape(qblocks, device_count, per_owner) - owner_base,
        "dp",
        split_axis=1,
        concat_axis=1,
        tiled=True,
    )
    served = jnp.take(stored, wanted, axis=0)
    retrieved_entries = lax.all_to_all(
        served, "dp", split_axis=1, concat_axis=1, tiled=True
    ).reshape(qblocks, -1, model_width)
    target_float = target_tokens.astype(jnp.float32)
    dec_bias = jnp.concatenate([biases["dec_q"], zero_half, biases["dec_v"]])
    dec_branch, dec_saved = self_forward(
        target_tokens, weights["dec_qkv"], dec_bias, weights["dec_out"], True
    )
    pre_three = target_float + tensor_sum(dec_branch) + shared[6]
    first_dec, norm_three_back = jax.vjp(layer_norm, pre_three, shared[7], shared[8])
    first_low = first_dec.astype(jnp.bfloat16)
    cross_branch, cross_saved = cross_forward(
        first_low.reshape(qblocks, -1, model_width),
        retrieved_entries,
        weights["crs_q"],
        biases["crs_q"],
        weights["crs_kv"],
        biases["crs_v"],
        weights["crs_out"],
    )
    pre_four = first_dec + tensor_sum(cross_branch) + shared[9]
    second_dec, norm_four_back = jax.vjp(layer_norm, pre_four, shared[10], shared[11])
    second_low = second_dec.astype(jnp.bfloat16)
    dec_feed, dec_feed_saved = ffn_forward(
        second_low, weights["dec_up"], biases["dec_up"], weights["dec_down"]
    )
    pre_five = second_dec + tensor_sum(dec_feed) + shared[12]
    decoder_states, norm_five_back = jax.vjp(layer_norm, pre_five, shared[13], shared[14])
    grad_five, grad_gain_five, grad_shift_five = norm_five_back(
        target_cotangent.astype(jnp.float32)
    )
    grad_dec_up, grad_dec_upb, grad_dec_down, part_second = ffn_backward(
        grad_five, second_low, dec_feed_saved, weights["dec_up"], weights["dec_down"]
    )
    grad_second = grad_five + tensor_back(part_second)
    grad_four, grad_gain_four, grad_shift_four = norm_four_back(grad_second)
    grad_crs_q, grad_crs_qb, grad_crs_kv, grad_crs_vb, grad_crs_out, part_first, part_fetched = (
        cross_backward(
            grad_four,
            first_low,
            retrieved_entries,
            cross_saved,
            weights["crs_q"],
            weights["crs_kv"],
            weights["crs_out"],
        )
    )
    summed_first, summed_fetched = tensor_back((part_first, part_fetched))
    grad_first = grad_four + summed_first
    grad_three, grad_gain_three, grad_shift_three = norm_three_back(grad_first)
    grad_dec_qkv, grad_dec_qb, grad_dec_vb, grad_dec_out, part_target = self_backward(
        grad_three, target_tokens, dec_saved, weights["dec_qkv"], weights["dec_out"], True
    )
    target_grad = grad_three + tensor_back(part_target)
    fetched_low = summed_fetched.astype(jnp.bfloat16)
    returned = lax.all_to_all(
        fetched_low.reshape(qblocks, device_count, per_owner, model_width),
        "dp",
        split_axis=1,
        concat_axis=1,
        tiled=True,
    )
    matches = (wanted.reshape(1, -1) == lax.broadcasted_iota(jnp.int32, (KEEP, 1), 0)).astype(
        jnp.bfloat16
    )
    stored_grad = project(matches, returned.reshape(-1, model_width))
    grad_states = lax.dynamic_update_slice_in_dim(
        jnp.zeros_like(encoder_states), stored_grad, start_row, 0
    )
    grad_two, grad_gain_two, grad_shift_two = norm_two_back(grad_states)
    grad_enc_up, grad_enc_upb, grad_enc_down, part_hidden = ffn_backward(
        grad_two, hidden_low, enc_feed_saved, weights["enc_up"], weights["enc_down"]
    )
    grad_hidden = grad_two + tensor_back(part_hidden)
    grad_one, grad_gain_one, grad_shift_one = norm_one_back(grad_hidden)
    grad_enc_qkv, grad_enc_qb, grad_enc_vb, grad_enc_out, part_source = self_backward(
        grad_one, source_tokens, enc_saved, weights["enc_qkv"], weights["enc_out"], False
    )
    source_grad = grad_one + tensor_back(part_source)
    shared_grad = jnp.stack(
        [
            jnp.sum(grad_one, 0),
            grad_gain_one,
            grad_shift_one,
            jnp.sum(grad_two, 0),
            grad_gain_two,
            grad_shift_two,
            jnp.sum(grad_three, 0),
            grad_gain_three,
            grad_shift_three,
            jnp.sum(grad_four, 0),
            grad_gain_four,
            grad_shift_four,
            jnp.sum(grad_five, 0),
            grad_gain_five,
            grad_shift_five,
        ]
    )
    split_grad = jnp.concatenate(
        [
            grad_enc_qb,
            grad_enc_vb,
            grad_enc_upb,
            grad_dec_qb,
            grad_dec_vb,
            grad_crs_qb,
            grad_crs_vb,
            grad_dec_upb,
        ]
    ).reshape(-1, model_width)
    matrix_grads = {
        "enc_qkv": grad_enc_qkv,
        "enc_out": grad_enc_out,
        "enc_up": grad_enc_up,
        "enc_down": grad_enc_down,
        "dec_qkv": grad_dec_qkv,
        "dec_out": grad_dec_out,
        "crs_q": grad_crs_q,
        "crs_kv": grad_crs_kv,
        "crs_out": grad_crs_out,
        "dec_up": grad_dec_up,
        "dec_down": grad_dec_down,
    }
    packed = pack(matrix_grads, model_width, hidden_width, tensor_count, tile_size)
    slot_grads = (
        jnp.zeros((gathered.shape[0], tile_size, tile_size), jnp.float32)
        .at[owner_slots]
        .set(packed)
    )
    owned_grads, shared_owned, split_owned = (
        lax.psum_scatter(slot_grads, "dp", scatter_dimension=0, tiled=True),
        lax.psum_scatter(shared_grad, "dp", scatter_dimension=1, tiled=True),
        lax.psum_scatter(split_grad, "dp", scatter_dimension=1, tiled=True),
    )
    results = jax.vmap(soap_update)(
        owned_grads,
        master[0],
        first_moment[0],
        second_moment[0],
        left_stats[0],
        right_stats[0],
        left_basis[0],
        right_basis[0],
    )
    new_first, new_second, new_master, new_left, new_right, new_lbasis, new_rbasis = results
    shared_new_first, shared_new_second, shared_updated = adam_vector(
        shared_owned, shared_vectors, shared_first, shared_second
    )
    split_new_first, split_new_second, split_updated = adam_vector(
        split_owned, split_vectors[0], split_first[0], split_second[0]
    )
    return (
        encoder_states,
        decoder_states,
        source_grad,
        target_grad,
        new_master[None],
        new_first[None],
        new_second[None],
        new_left[None],
        new_right[None],
        new_lbasis[None],
        new_rbasis[None],
        shared_new_first,
        shared_new_second,
        shared_updated,
        split_new_first[None],
        split_new_second[None],
        split_updated[None],
    )


def solution(mesh):
    placed = (
        P("dp", None),
        P("dp", None),
        P("dp", None),
        P("dp", None),
        P("dp"),
        P(),
        P("tensor", "dp", None, None),
        P("tensor", "dp", None, None),
        P("tensor", "dp", None, None),
        P("tensor", "dp", None, None),
        P("tensor", "dp", None, None),
        P("tensor", "dp", None, None),
        P("tensor", "dp", None, None),
        P(None, "dp"),
        P(None, "dp"),
        P(None, "dp"),
        P("tensor", None, "dp"),
        P("tensor", None, "dp"),
        P("tensor", None, "dp"),
    )
    return jax.shard_map(
        local,
        mesh=mesh,
        in_specs=placed,
        out_specs=(
            P("dp", None),
            P("dp", None),
            P("dp", None),
            P("dp", None),
            P("tensor", "dp", None, None),
            P("tensor", "dp", None, None),
            P("tensor", "dp", None, None),
            P("tensor", "dp", None, None),
            P("tensor", "dp", None, None),
            P("tensor", "dp", None, None),
            P("tensor", "dp", None, None),
            P(None, "dp"),
            P(None, "dp"),
            P(None, "dp"),
            P("tensor", None, "dp"),
            P("tensor", None, "dp"),
            P("tensor", None, "dp"),
        ),
        check_vma=False,
    )
```

profile of v0, /device:TPU:0, one launch (start us, length us, event | category | flops | bytes accessed | tf_op | source)
XLA Modules:
  0.0 3265.2 jit_solution(118683469960141808)
XLA Ops:
  10.2 43.4 %all-gather = bf16[16,48,7]{1,2,0:T(8,128)(2,1)S(1)} all-gather(bf16[1,48,7]{1,2,0:T(8,128)(2,1)S(1)} %bitcast.665), channel_id=1, replica_groups=mesh['dp'=16,'tensor'=2] {'dp'}, dimensions={0}, use_global_device_ids=true | all-gather | bytes 11424 | tf_op jit(solution)/shard_map/all_gather | solution.py:364
  53.8 37.1 %all-gather.1 = bf16[16,48,15]{1,2,0:T(8,128)(2,1)S(1)} all-gather(bf16[1,48,15]{1,2,0:T(8,128)(2,1)S(1)} %convert_bitcast_fusion), channel_id=1, replica_groups=mesh['dp'=16,'tensor'=2] {'dp'}, dimensions={0}, use_global_device_ids=true | all-gather | bytes 24480 | tf_op jit(solution)/shard_map/all_gather | solution.py:363
  93.0 114.0 %all-gather.4.cloned.1.call-done = bf16[512,128,128]{2,1,0:T(8,128)(2,1)} async-done(((bf16[32,128,128]{2,1,0:T(8,128)(2,1)}), bf16[512,128,128]{2,1,0:T(8,128)(2,1)}) %all-gather.4.cloned.1.call-update) | async-done | bytes 16777232 | tf_op jit(solution)/shard_map/all_gather | solution.py:362
  207.0 19.6 gather_fusion
  226.6 8.8 broadcast_select_fusion
  254.0 10.1 multiply_reduce_fusion.1
  264.2 10.5 exponential_reduce_fusion
  275.2 10.9 fusion.119
  313.8 19.2 multiply_convert_fusion.3
  340.5 5.1 all-to-all-start
  352.9 6.6 all-reduce.27.cloned.1.call-done
  366.5 5.2 gather_fusion.1
  374.5 7.0 all-to-all-start.1
  388.0 27.8 all-to-all-done.1
  430.9 5.1 copy.304
  439.5 13.1 all-reduce.15.cloned.1.call-done
  456.1 10.2 multiply_convert_fusion.4
  470.1 20.3 all-reduce.17.cloned.1.call-done
  504.5 20.5 all-reduce.19.cloned.1.call-done
  530.9 10.7 multiply_reduce_fusion.2
  544.2 6.5 multiply_convert_fusion.1
  556.0 21.7 all-reduce.21.cloned.1.call-done
  577.8 6.8 all-to-all-start.2
  591.9 5.6 fusion.207
  597.5 6.7 reshape.869
  604.2 6.5 copy.322
  614.3 6.6 reshape.871
  620.9 5.8 copy.323
  626.7 5.0 convert_reduce_fusion.6
  638.6 5.0 dynamic_update_slice.3
  650.1 8.9 convert_reduce_fusion
  671.5 4.6 fusion.200
  676.1 6.6 reshape.861
  682.8 6.6 copy.316
  689.5 4.6 fusion.204
  694.1 6.7 reshape.859
  700.8 6.4 copy.315
  707.2 5.0 multiply_reduce_fusion.6
  718.3 16.2 multiply_reduce_fusion
  734.4 17.3 multiply_convert_fusion
  759.6 9.4 multiply_convert_fusion.5
  769.0 13.7 fusion.122
  810.2 5.2 reshape.863
  815.4 5.5 copy.317
  820.9 6.0 convolution_bitcast_fusion.1
  826.9 4.8 reshape.856
  831.7 5.5 copy.313
  844.5 5.2 add_reduce_fusion
  882.4 11.7 broadcast_in_dim.147
  894.1 92.3 %scatter_fusion = f32[512,128,128]{2,1,0:T(8,128)} fusion(f32[512,128,128]{2,1,0:T(8,128)} %broadcast_in_dim.147, s32[504]{0:T(512)S(1)} %copy-done.145, f32[504,128,128]{2,1,0:T(8,128)} %constant_dynamic-update-slice_fusion), kind=kCustom, calls=%fused_computation.2 | custom fusion | bytes 99092448 | tf_op jit(solution)/shard_map/scatter | solution.py:523
  989.2 103.2 %reduce-scatter.10.cloned.1.call-done = f32[48,15]{1,0:T(8,128)} async-done(((f32[768,15]{1,0:T(8,128)}), f32[48,15]{1,0:T(8,128)}) %reduce-scatter.10.cloned.1.call-update) | async-done | bytes 2896
  1093.9 683.3 %reduce-scatter.8.cloned.1.call-done = f32[32,128,128]{2,1,0:T(8,128)} async-done(((f32[512,128,128]{2,1,0:T(8,128)}), f32[32,128,128]{2,1,0:T(8,128)}) %reduce-scatter.8.cloned.1.call-update) | async-done | bytes 2097168 | tf_op jit(solution)/shard_map/reduce_scatter | solution.py:526
  1777.2 7.4 bitcast_add_fusion.3
  1788.1 5.0 fusion.241
  1800.0 376.8 %custom-call.8 = f32[32,128,128]{2,1,0:T(8,128)} custom-call(f32[32,128,128]{2,1,0:T(8,128)} %fusion.48), custom_call_target="Cholesky" | custom-call | tf_op jit(solution)/shard_map/vmap(jit(cholesky))/cholesky | solution.py:280
  2176.7 6.5 bitcast_add_fusion.2
  2186.9 5.0 fusion.242
  2198.7 376.8 %custom-call.10 = f32[32,128,128]{2,1,0:T(8,128)} custom-call(f32[32,128,128]{2,1,0:T(8,128)} %fusion.44), custom_call_target="Cholesky" | custom-call | tf_op jit(solution)/shard_map/vmap(jit(cholesky))/cholesky | solution.py:280
  2581.6 315.8 %custom-call.11 = f32[32,1,128,128]{2,3,1,0:T(8,128)} custom-call(f32[32,1,128,128]{3,2,1,0:T(8,128)} %get-tuple-element.222), custom_call_target="InvertDiagBlocksLowerTriangular" | custom-call | tf_op jit(solution)/shard_map/vmap(jit(_solve_triangular))/triangular_solve | solution.py:281
  2897.4 7.0 fusion.111
  2907.3 316.2 %custom-call.9 = f32[32,1,128,128]{2,3,1,0:T(8,128)} custom-call(f32[32,1,128,128]{3,2,1,0:T(8,128)} %get-tuple-element.223), custom_call_target="InvertDiagBlocksLowerTriangular" | custom-call | tf_op jit(solution)/shard_map/vmap(jit(_solve_triangular))/triangular_solve | solution.py:281
  3223.5 7.0 fusion.106
  3233.4 5.7 fusion.63
  3250.3 6.0 fusion.66
  (628 shorter events, 300.9 us)
Async XLA Ops:
  7.2 1777.4 %copy-start = (f32[1,32,128,128]{3,2,1,0:T(8,128)S(1)}, f32[1,32,128,128]{3,2,1,0:T(8,128)}, u32[]{:S(2)}) copy-start(f32[1,32,128,128]{3,2,1,0:T(8,128)} %param.33) | copy-start | bytes 6291460
  7.2 46.6 %copy-start.138 = (f32[15,48]{1,0:T(8,128)S(1)}, f32[15,48]{1,0:T(8,128)}, u32[]{:S(2)}) copy-start(f32[15,48]{1,0:T(8,128)} %param.35) | copy-start | bytes 8644
  7.2 84.4 %copy-start.162 = (s32[504]{0:T(512)S(1)}, s32[504]{0:T(512)}, u32[]{:S(2)}) copy-start(s32[504]{0:T(512)} %param.27) | copy-start | bytes 6052
  7.2 199.8 %all-gather.4.cloned.1.call-start = ((), (), s32[]{:S(2)}) async-start(), calls=%async_computation.6 | async-start | bytes 17825792 | tf_op jit(solution)/shard_map/all_gather | solution.py:362
  10.2 299.9 %all-reduce.13.cloned.1.call-start = ((), (), s32[]{:S(2)}) async-start(), calls=%async_computation.7 | async-start | bytes 3145728 | tf_op jit(solution)/shard_map/psum | solution.py:111
  91.7 135.0 %copy-start.144 = (s32[504]{0:T(512)}, s32[504]{0:T(512)S(1)}, u32[]{:S(2)}) copy-start(s32[504]{0:T(512)S(1)} %compare_select_fusion.1) | copy-start | bytes 6052
  93.0 266.5 %copy-start.118 = (f32[768]{0:T(1024)}, f32[768]{0:T(1024)S(1)}, u32[]{:S(2)}) copy-start(f32[768]{0:T(1024)S(1)} %get-tuple-element.155) | copy-start | bytes 9220
  93.0 266.5 %copy-start.126 = (f32[768]{0:T(1024)}, f32[768]{0:T(1024)S(1)}, u32[]{:S(2)}) copy-start(f32[768]{0:T(1024)S(1)} %get-tuple-element.154) | copy-start | bytes 9220
  93.0 266.5 %copy-start.148 = (f32[768]{0:T(1024)}, f32[768]{0:T(1024)S(1)}, u32[]{:S(2)}) copy-start(f32[768]{0:T(1024)S(1)} %get-tuple-element.153) | copy-start | bytes 9220
  235.5 10.0 copy-start.8
  254.0 10.1 copy-start.41
  254.0 10.1 copy-start.43
  254.0 21.1 copy-start.51
  274.7 11.4 copy-start.104
  275.2 11.0 copy-start.110
  289.2 70.3 %all-reduce.27.cloned.1.call-start = ((), (), s32[]{:S(2)}) async-start(), calls=%async_computation.17 | async-start | bytes 4718592 | tf_op jit(solution)/shard_map/psum | solution.py:111
  296.5 10.2 copy-start.64
  312.9 46.6 %copy-start.122 = (f32[1024]{0:T(1024)}, f32[1024]{0:T(1024)S(1)}, u32[]{:S(2)}) copy-start(f32[1024]{0:T(1024)S(1)} %broadcast_multiply_fusion.1) | copy-start | bytes 12292
  313.7 19.3 copy-start.133
  313.8 45.7 %copy-start.124 = (f32[1024]{0:T(1024)}, f32[1024]{0:T(1024)S(1)}, u32[]{:S(2)}) copy-start(f32[1024]{0:T(1024)S(1)} %fusion.180) | copy-start | bytes 12292
  313.8 21.0 copy-start.74
  334.8 10.7 copy-start.164
  340.5 12.3 all-to-all-start
  371.7 9.8 copy-start.161
  374.5 9.4 slice-start.5
  374.5 41.3 %all-to-all-start.1 = ((bf16[1,16,64,768]{3,2,0,1:T(8,128)(2,1)}), bf16[1,16,64,768]{3,2,0,1:T(8,128)(2,1)}, u32[]{:S(2)}, u32[]{:S(2)}) async-start(bf16[1,16,64,768]{3,2,0,1:T(8,128)(2,1)} %broadcast_select_fusion.1), calls=%async_computation.1 | async-start | bytes 3145728 | tf_op jit(solution)/shard_map/all_to_all | solution.py:396
  381.5 71.1 %all-reduce.15.cloned.1.call-start = ((), (), s32[]{:S(2)}) async-start(), calls=%async_computation.8 | async-start | bytes 1572864 | tf_op jit(solution)/shard_map/psum | solution.py:111
  386.3 42.1 %copy-start.114 = (bf16[3,6,128,128]{3,1,2,0:T(8,128)(2,1)}, bf16[3,6,128,128]{3,1,2,0:T(8,128)(2,1)S(1)}, u32[]{:S(2)}) copy-start(bf16[3,6,128,128]{3,1,2,0:T(8,128)(2,1)S(1)} %copy.303) | copy-start | bytes 1769476
  386.7 65.9 %copy-start.131 = (f32[512]{0:T(512)}, f32[512]{0:T(512)S(1)}, u32[]{:S(2)}) copy-start(f32[512]{0:T(512)S(1)} %broadcast_multiply_fusion.4) | copy-start | bytes 6148
  387.1 32.0 copy-start.146
  387.1 65.5 %copy-start.136 = (f32[512]{0:T(512)}, f32[512]{0:T(512)S(1)}, u32[]{:S(2)}) copy-start(f32[512]{0:T(512)S(1)} %fusion.183) | copy-start | bytes 6148
  430.7 59.7 %all-reduce.17.cloned.1.call-start = ((), (), s32[]{:S(2)}) async-start(), calls=%async_computation.9 | async-start | bytes 1572864 | tf_op jit(solution)/shard_map/psum | solution.py:111
  436.0 16.6 copy-start.30
  436.0 16.6 copy-start.152
  455.8 10.6 copy-start.9
  456.1 11.4 copy-start.78
  467.5 22.9 copy-start.151
  469.8 23.2 copy-start.80
  469.8 23.2 copy-start.135
  469.8 55.1 %all-reduce.19.cloned.1.call-start = ((), (), s32[]{:S(2)}) async-start(), calls=%async_computation.10 | async-start | bytes 1572864 | tf_op jit(solution)/shard_map/psum | solution.py:116
  504.4 73.3 %all-reduce.21.cloned.1.call-start = ((), (), s32[]{:S(2)}) async-start(), calls=%async_computation.11 | async-start | bytes 3145728 | tf_op jit(solution)/shard_map/psum | solution.py:116
  529.1 12.4 copy-start.142
  530.2 11.3 slice-start
  530.8 10.7 slice-start.1
  530.8 10.7 slice-start.2
  577.8 55.4 %all-to-all-start.2 = ((bf16[1,16,64,768]{3,2,0,1:T(8,128)(2,1)}), bf16[1,16,64,768]{3,2,0,1:T(8,128)(2,1)}, u32[]{:S(2)}, u32[]{:S(2)}) async-start(bf16[1,16,64,768]{3,2,0,1:T(8,128)(2,1)} %all-reduce.21.cloned.1.call-done), calls=%async_computation.2 | async-start | bytes 3145728 | tf_op jit(solution)/shard_map/all_to_all | solution.py:451
  584.6 122.6 %all-reduce.25.cloned.1.call-start = ((), (), s32[]{:S(2)}) async-start(), calls=%async_computation.16 | async-start | bytes 4718592 | tf_op jit(solution)/shard_map/psum | solution.py:116
  649.7 9.3 copy-start.21
  650.1 10.5 copy-start.73
  664.4 180.1 %all-reduce.23.cloned.1.call-start = ((), (), s32[]{:S(2)}) async-start(), calls=%async_computation.15 | async-start | bytes 4718592 | tf_op jit(solution)/shard_map/psum | solution.py:116
  734.4 21.9 copy-start.44
  768.9 13.8 copy-start.31
  768.9 13.8 copy-start.121
  768.9 13.8 copy-start.129
  768.9 13.8 copy-start.132
  768.9 13.8 copy-start.137
  769.0 13.8 copy-start.143
  803.4 183.2 %reduce-scatter.12.cloned.1.call-start = ((), (), s32[]{:S(2)}) async-start(), calls=%async_computation.14 | async-start | bytes 417792
  842.9 249.5 %reduce-scatter.10.cloned.1.call-start = ((), (), s32[]{:S(2)}) async-start(), calls=%async_computation.13 | async-start | bytes 417792
  856.1 921.1 %reduce-scatter.8.cloned.1.call-start = ((), (), s32[]{:S(2)}) async-start(), calls=%async_computation.12 | async-start | bytes 35651584 | tf_op jit(solution)/shard_map/reduce_scatter | solution.py:526
  882.4 11.7 copy-start.145
  986.5 106.7 %copy-start.139 = (f32[15,48]{1,0:T(8,128)S(1)}, f32[15,48]{1,0:T(8,128)}, u32[]{:S(2)}) copy-start(f32[15,48]{1,0:T(8,128)} %param.35) | copy-start | bytes 8644
  986.5 106.7 %copy-start.159 = (f32[15,48]{1,0:T(8,128)S(1)}, f32[15,48]{1,0:T(8,128)}, u32[]{:S(2)}) copy-start(f32[15,48]{1,0:T(8,128)} %param.37) | copy-start | bytes 8644
  986.5 106.7 %copy-start.160 = (f32[15,48]{1,0:T(8,128)S(1)}, f32[15,48]{1,0:T(8,128)}, u32[]{:S(2)}) copy-start(f32[15,48]{1,0:T(8,128)} %param.36) | copy-start | bytes 8644
  (141 other events, 500.0 us)
Sparse Core Ops, SparseCore 0:
  11.4 195.5 all-gather.3
  289.4 18.5 all-reduce.12
  338.6 20.7 all-reduce.26
  430.8 21.7 all-reduce.14
  469.9 20.3 all-reduce.16
  504.5 20.3 all-reduce.18
  556.1 21.5 all-reduce.20
  664.5 22.9 all-reduce.24
  803.6 22.9 all-reduce.22
  843.1 122.8 reduce-scatter.11
  971.9 120.4 reduce-scatter.9
  1094.6 682.5 reduce-scatter.7
where the time goes:
time: 3280 us; the launch traced here: 3270 us
  other arithmetic  1510 us (46%)
  waiting for transfers between devices  1020 us (31%)
  local copies, waits for them, and re-layouts  339 us (10%)
  matrix products  284 us (9%)
  blocking collectives  80.5 us (2%)
    another operation x5, other arithmetic, orthonormal(): factor = jnp.linalg.cholesky(gram)  757 us
    reduce_scatter x1, waiting for transfers between devices, local(): lax.psum_scatter(slot_grads, 'dp', scatter_dimension=0, tiled=True)  683 us
    another operation x4, other arithmetic, orthonormal(): return jax.scipy.linalg.solve_triangular(factor, matrix.T, lower=True).T  634 us
    all_gather x1, waiting for transfers between devices, local(): lax.all_gather(master[0].astype(jnp.bfloat16), 'dp', axis=0, tiled=True)  114 us
    unnamed x14, waiting for transfers between devices  103 us
    scatter x1, local copies, waits for them, and re-layouts, local(): slot_grads = jnp.zeros((gathered.shape[0], tile_size, tile_size), jnp.flo...  92.3 us
    unnamed x406, local copies, waits for them, and re-layouts  69.6 us
  transfers between devices with their start and end apart: 15, of which 10 were waited for; matrix products, arithmetic and copies ran while one was open for 10% of the time, Pallas kernels for 0%

commit v1 on v0

--- a/solution.py
+++ b/solution.py
@@ -1,8 +1,11 @@
+import functools
 from functools import partial
 
 import jax
 import jax.numpy as jnp
 from jax import lax
+from jax.experimental import pallas as pl
+from jax.experimental.pallas import tpu as pltpu
 from jax.sharding import PartitionSpec as P
 
 HD = 64
@@ -10,7 +13,6 @@
 STEP = 10
 
 
-MATMUL_ACCURACY = lax.Precision.HIGHEST
 BETA_ONE = 0.9
 BETA_TWO = 0.95
 ADAM_EPSILON = 1e-08
@@ -18,6 +20,8 @@
 VECTOR_RATE = 0.5
 WEIGHT_DECAY = 0.01
 NORM_EPSILON = 1e-05
+TILE = 128
+PANEL = 32
 
 
 def for_sending(x):
@@ -44,30 +48,6 @@
         ("dec_up", model_width, hidden_half),
         ("dec_down", hidden_half, model_width),
     ]
-
-
-def unpack(blocks, model_width, hidden_width, tensor_count):
-    tile_size = blocks.shape[-1]
-    matrices = {}
-    offset = 0
-    for matrix_name, height, breadth in matrix_list(model_width, hidden_width, tensor_count):
-        block_count = height // tile_size * (breadth // tile_size)
-        pieces = blocks[offset : offset + block_count].reshape(
-            height // tile_size, breadth // tile_size, tile_size, tile_size
-        )
-        matrices[matrix_name] = pieces.transpose(0, 2, 1, 3).reshape(height, breadth)
-        offset = offset + block_count
-    return matrices
-
-
-def pack(matrices, model_width, hidden_width, tensor_count, tile_size):
-    pieces = []
-    for matrix_name, height, breadth in matrix_list(model_width, hidden_width, tensor_count):
-        shaped = matrices[matrix_name].reshape(
-            height // tile_size, tile_size, breadth // tile_size, tile_size
-        )
-        pieces.append(shaped.transpose(0, 2, 1, 3).reshape(-1, tile_size, tile_size))
-    return jnp.concatenate(pieces, 0)
 
 
 def split_biases(flat_vector, half_width, hidden_half):
@@ -275,46 +255,557 @@
     return (grad_wq, grad_bq, grad_wkv, grad_bv, grad_wout, part_first, part_fetched)
 
 
-def orthonormal(matrix):
-    gram = jnp.matmul(matrix.T, matrix, precision=MATMUL_ACCURACY)
-    factor = jnp.linalg.cholesky(gram)
-    return jax.scipy.linalg.solve_triangular(factor, matrix.T, lower=True).T
-
-
-def soap_update(
-    grad_block,
-    weight_block,
-    first_block,
-    second_block,
-    left_block,
-    right_block,
-    left_turn,
-    right_turn,
-):
-    product = partial(jnp.matmul, precision=MATMUL_ACCURACY)
-    rotated = product(product(left_turn.T, grad_block), right_turn)
-    new_first = BETA_ONE * first_block + (1.0 - BETA_ONE) * grad_block
-    new_second = BETA_TWO * second_block + (1.0 - BETA_TWO) * rotated * rotated
-    first_rotated = product(product(left_turn.T, new_first), right_turn)
-    correct_one = 1.0 - BETA_ONE**STEP
-    correct_two = 1.0 - BETA_TWO**STEP
-    normed = first_rotated / correct_one / (jnp.sqrt(new_second / correct_two) + ADAM_EPSILON)
-    new_weight = (
-        weight_block
-        - MATRIX_RATE * product(product(left_turn, normed), right_turn.T)
-        - MATRIX_RATE * WEIGHT_DECAY * weight_block
-    )
-    new_left = BETA_TWO * left_block + (1.0 - BETA_TWO) * product(grad_block, grad_block.T)
-    new_right = BETA_TWO * right_block + (1.0 - BETA_TWO) * product(grad_block.T, grad_block)
+def halves(x):
+    hi = x.astype(jnp.bfloat16)
+    return hi, (x - hi.astype(jnp.float32)).astype(jnp.bfloat16)
+
+def mm(a, b, dims=((1,), (0,)), passes=3):
+    dot = functools.partial(lax.dot_general, dimension_numbers=(dims, ((), ())), preferred_element_type=jnp.float32)
+    if passes == 6:
+        return dot(a, b, precision=lax.Precision.HIGHEST)
+    if passes == 1:
+        return dot(a.astype(jnp.bfloat16), b.astype(jnp.bfloat16))
+    ah, al = halves(a); bh, bl = halves(b)
+    return dot(ah, bh) + (dot(ah, bl) + dot(al, bh))
+
+NN=((1,),(0,)); NT=((1,),(1,)); TN=((0,),(0,))
+
+def soap_kernel(passes, used_ref, g_ref, w_ref, m_ref, v_ref, l_ref, r_ref, ql_ref, qr_ref,
+                nw_ref, nm_ref, nv_ref, nl_ref, nr_ref, nql_ref, nqr_ref, sa_ref):
+    nb = g_ref.shape[0]
+    p_rot, p_orth, p_chol = passes
+    c1 = 1.0 - BETA_ONE**STEP
+    c2 = 1.0 - BETA_TWO**STEP
+
+    def one(i, carry):
+        used = used_ref[pl.program_id(0) * nb + i] > 0
+        g = jnp.where(used, g_ref[i], 0.0)
+        ql = ql_ref[i]
+        qr = qr_ref[i]
+        gt = g.T
+        nm = BETA_ONE * m_ref[i] + (1.0 - BETA_ONE) * g
+        nm_ref[i] = nm
+        qlt = ql.T
+        side = mm(jnp.concatenate([g, nm], 0), qr, NN, p_rot)
+        both = mm(qlt, jnp.concatenate([side[:TILE], side[TILE:]], 1), NN, p_rot)
+        rotated, first = both[:, :TILE], both[:, TILE:]
+        nv = BETA_TWO * v_ref[i] + (1.0 - BETA_TWO) * rotated * rotated
+        nv_ref[i] = nv
+        normed = first / c1 / (jnp.sqrt(nv / c2) + ADAM_EPSILON)
+        step = mm(mm(ql, normed, NN, p_rot), qr, NT, p_rot)
+        w = w_ref[i]
+        nw_ref[i] = w - MATRIX_RATE * step - MATRIX_RATE * WEIGHT_DECAY * w
+        nl = BETA_TWO * l_ref[i] + (1.0 - BETA_TWO) * mm(g, gt, NN, p_rot)
+        nr = BETA_TWO * r_ref[i] + (1.0 - BETA_TWO) * mm(gt, g, NN, p_rot)
+        nl_ref[i] = nl
+        nr_ref[i] = nr
+        for k, (stat, turn) in enumerate(((nl, ql), (nr, qr))):
+            a = mm(stat, turn, NN, p_orth)
+            at = a.T
+            sa_ref[2 * i + k, :, :TILE] = mm(at, a, NN, p_orth)
+            sa_ref[2 * i + k, :, TILE:] = at
+        return carry
+
+    lax.fori_loop(0, nb, one, 0, unroll=2)
+
+    count = 2 * nb
+    per = TILE // (2 * PANEL)
+    rows = count // per * PANEL
+    lane = lax.broadcasted_iota(jnp.int32, (rows, TILE), 1)
+    start = lane // (2 * PANEL) * (2 * PANEL)
+    sub = lax.broadcasted_iota(jnp.int32, (count // per, PANEL, TILE), 1)
+    lane1 = lax.broadcasted_iota(jnp.int32, (PANEL, 2 * PANEL), 1)
+    sub1 = lax.broadcasted_iota(jnp.int32, (PANEL, 2 * PANEL), 0)
+    eye = (lane1[:, :PANEL] == sub1[:, :PANEL]).astype(jnp.float32)
+    for p in range(TILE // PANEL):
+        r0 = p * PANEL
+        packs = []
+        for q in range(count // per):
+            pieces = []
+            for k in range(per):
+                pieces += [sa_ref[q * per + k, r0:r0 + PANEL, r0:r0 + PANEL], eye]
+            packs.append(jnp.concatenate(pieces, 1)[None])
+        x = jnp.concatenate(packs, 0)
+        piv = jnp.ones_like(x)
+        for j in range(PANEL):
+            col = jnp.take_along_axis(x.reshape(rows, TILE), start + j, axis=1).reshape(x.shape)
+            row = x[:, j:j + 1, :]
+            pivot = col[:, j:j + 1, :]
+            piv = jnp.where(sub == j, pivot, piv)
+            if j < PANEL - 1:
+                x = x - jnp.where(sub > j, col, 0.0) * (row * (1.0 / pivot))
+        x = x * lax.rsqrt(piv)
+        for q in range(count // per):
+            for k in range(per):
+                i = q * per + k
+                wmat = x[q, :, 2 * PANEL * k + PANEL:2 * PANEL * (k + 1)]
+                u = mm(wmat, sa_ref[i, r0:r0 + PANEL, :], NN, p_chol)
+                sa_ref[i, r0:r0 + PANEL, TILE:] = u[:, TILE:]
+                if p < TILE // PANEL - 1:
+                    ut = u[:, :TILE].T
+                    sa_ref[i, r0 + PANEL:, :] -= mm(ut[r0 + PANEL:, :], u, NN, p_chol)
+    def fin(i, carry):
+        nql_ref[i] = sa_ref[2 * i, :, TILE:].T
+        nqr_ref[i] = sa_ref[2 * i + 1, :, TILE:].T
+        return carry
+    lax.fori_loop(0, nb, fin, 0)
+
+def soap_all(used, g, w, m, v, l, r, ql, qr, nb=16, passes=(3, 3, 3)):
+    s = g.shape[0]
+    nb = min(nb, s)
+    spec = pl.BlockSpec((nb, TILE, TILE), lambda i: (i, 0, 0))
+    return pl.pallas_call(
+        functools.partial(soap_kernel, passes),
+        grid=(s // nb,),
+        out_shape=[jax.ShapeDtypeStruct(g.shape, jnp.float32)] * 7,
+        in_specs=[pl.BlockSpec(memory_space=pltpu.SMEM)] + [spec] * 8,
+        out_specs=[spec] * 7,
+        scratch_shapes=[pltpu.VMEM((2 * nb, TILE, 2 * TILE), jnp.float32)],
+        compiler_params=pltpu.CompilerParams(vmem_limit_bytes=48 << 20),
+        name="soap",
+    )(used, g, w, m, v, l, r, ql, qr)
+
+
+MESH = pl.DeviceIdType.MESH
+ANY = pl.BlockSpec(memory_space=pl.ANY)
+
+
+def chip_grid(device_count):
+    if device_count == 16:
+        return 4, 2, 2
+    side = round(device_count ** (1 / 3))
+    if side**3 == device_count:
+        return side, side, side
+    return 1, 1, device_count
+
+
+def place(grid):
+    zs, ys, xs = grid
+    me = lax.axis_index("dp")
+    return me // (ys * xs), lax.rem(me // xs, ys), lax.rem(me, xs)
+
+
+def peers(grid):
+    zs, ys, xs = grid
+    z, y, x = place(grid)
+
+    def device(zz, yy, xx):
+        return {"dp": (zz * ys + yy) * xs + xx}
+
     return (
-        new_first,
-        new_second,
-        new_weight,
-        new_left,
-        new_right,
-        orthonormal(product(new_left, left_turn)),
-        orthonormal(product(new_right, right_turn)),
-    )
+        lambda k: device(lax.rem(z + k, zs), y, x),
+        lambda k: device(z, lax.rem(y + k, ys), x),
+        lambda k: device(z, y, lax.rem(x + k, xs)),
+    )
+
+
+def greet(grid):
+    barrier = pltpu.get_barrier_semaphore()
+    count = 0
+    for size, peer in zip(grid, peers(grid)):
+        for k in range(1, size):
+            pl.semaphore_signal(barrier, inc=1, device_id=peer(k), device_id_type=MESH)
+            count += 1
+    pl.semaphore_wait(barrier, count)
+
+
+def remote(src, dst, send, recv, device):
+    return pltpu.make_async_remote_copy(
+        src_ref=src, dst_ref=dst, send_sem=send, recv_sem=recv, device_id=device, device_id_type=MESH
+    )
+
+
+def chunking(slots):
+    half = slots // 2
+    chunks = min(16, half)
+    return half, chunks, half // chunks
+
+
+def rs_kernel(grid, *refs):
+    zs, ys, xs = grid
+    n = 0
+    in_ref, small_ref, out_ref, small_out_ref = refs[:4]
+    (own0, own1, ra0, ra1, rb0, rb1, rc0, rc1, total, rs_z, rs_y, rs_x, load_sem,
+     as0, as1, ar0, ar1, bs0, bs1, br0, br1, cs0, cs1, cr0, cr1,
+     ssz, ssy, ssx, srz, sry, srx) = refs[4:]
+    own, rec_a, rec_b, rec_c = (own0, own1), (ra0, ra1), (rb0, rb1), (rc0, rc1)
+    a_send, a_recv, b_send, b_recv, c_send, c_recv = (as0, as1), (ar0, ar1), (bs0, bs1), (br0, br1), (cs0, cs1), (cr0, cr1)
+    rec_s, s_send, s_recv = (rs_z, rs_y, rs_x), (ssz, ssy, ssx), (srz, sry, srx)
+
+    z, y, x = place(grid)
+    tos = peers(grid)
+    to_z, to_y, to_x = tos
+    slots = out_ref.shape[0]
+    half, chunks, size = chunking(slots)
+    first = ((xs, x, to_x), (ys, y, to_y))
+    second = ((ys, y, to_y), (xs, x, to_x))
+
+    def source(g, c, other):
+        span = pl.ds(g * half + c * size, size)
+        return in_ref.at[:, :, other, span] if g == 0 else in_ref.at[:, other, :, span]
+
+    def load(g, c):
+        return pltpu.make_async_copy(source(g, c, first[g][1]), own[g].at[c], load_sem.at[g, c])
+
+    def send_a(g, c, k):
+        count, mine, to = first[g]
+        return remote(source(g, c, lax.rem(mine + k, count)), rec_a[g].at[c, k - 1],
+                      a_send[g].at[c, k - 1], a_recv[g].at[c, k - 1], to(k))
+
+    def send_b(g, c, k):
+        count, mine, to = second[g]
+        return remote(own[g].at[c, :, lax.rem(mine + k, count)], rec_b[g].at[c, k - 1],
+                      b_send[g].at[c, k - 1], b_recv[g].at[c, k - 1], to(k))
+
+    def send_c(g, c, k):
+        return remote(own[g].at[c, lax.rem(z + k, zs), second[g][1]], rec_c[g].at[c, k - 1],
+                      c_send[g].at[c, k - 1], c_recv[g].at[c, k - 1], to_z(k))
+
+    def start_a(c):
+        for g in range(2):
+            for k in range(1, first[g][0]):
+                send_a(g, c, k).start()
+
+    def send_s(axis, k):
+        return remote(total.at[2 - axis], rec_s[axis].at[k - 1],
+                      s_send[axis].at[k - 1], s_recv[axis].at[k - 1], tos[axis](k))
+
+    def small_start(axis):
+        for k in range(1, grid[axis]):
+            send_s(axis, k).start()
+
+    def small_add(axis):
+        value = total[2 - axis]
+        for k in range(1, grid[axis]):
+            send_s(axis, k).wait_recv()
+            value += rec_s[axis][k - 1]
+        return value
+
+    for c in range(chunks):
+        for g in range(2):
+            load(g, c).start()
+    total[0] = small_ref[...]
+    greet(grid)
+    small_start(2)
+    start_a(0)
+    if chunks > 1:
+        start_a(1)
+    total[1] = small_add(2)
+    small_start(1)
+    total[2] = small_add(1)
+    small_start(0)
+
+    def step_a(c):
+        for g in range(2):
+            load(g, c).wait()
+            for k in range(1, first[g][0]):
+                send_a(g, c, k).wait_recv()
+        if c + 2 < chunks:
+            start_a(c + 2)
+        for g in range(2):
+            n2 = second[g][0]
+
+            def add(e, carry):
+                a, b = e // n2, lax.rem(e, n2)
+                value = own[g][c, a, b].astype(jnp.float32)
+                for k in range(1, first[g][0]):
+                    value += rec_a[g][c, k - 1, a, b].astype(jnp.float32)
+                own[g][c, a, b] = value.astype(jnp.bfloat16)
+                return carry
+
+            lax.fori_loop(0, zs * n2, add, 0)
+            for k in range(1, n2):
+                send_b(g, c, k).start()
+
+    def step_b(c):
+        for g in range(2):
+            n2, mine = second[g][0], second[g][1]
+            for k in range(1, n2):
+                send_b(g, c, k).wait_recv()
+
+            def add(a, carry):
+                value = own[g][c, a, mine].astype(jnp.float32)
+                for k in range(1, n2):
+                    value += rec_b[g][c, k - 1, a].astype(jnp.float32)
+                own[g][c, a, mine] = value.astype(jnp.bfloat16)
+                return carry
+
+            lax.fori_loop(0, zs, add, 0)
+            for k in range(1, zs):
+                send_c(g, c, k).start()
+
+    def step_c(c):
+        for g in range(2):
+            for k in range(1, zs):
+                send_c(g, c, k).wait_recv()
+            mine = second[g][1]
+
+            def add(e, carry):
+                value = own[g][c, z, mine, e].astype(jnp.float32)
+                for k in range(1, zs):
+                    value += rec_c[g][c, k - 1, e].astype(jnp.float32)
+                out_ref[g * half + c * size + e] = value
+                return carry
+
+            lax.fori_loop(0, size, add, 0)
+
+    for t in range(chunks + 2):
+        if t < chunks:
+            step_a(t)
+        if 1 <= t <= chunks:
+            step_b(t - 1)
+        if t >= 2:
+            step_c(t - 2)
+    small_out_ref[...] = small_add(0)
+    for axis in range(3):
+        for k in range(1, grid[axis]):
+            send_s(axis, k).wait_send()
+    for c in range(chunks):
+        for g in range(2):
+            for k in range(1, first[g][0]):
+                send_a(g, c, k).wait_send()
+            for k in range(1, second[g][0]):
+                send_b(g, c, k).wait_send()
+            for k in range(1, zs):
+                send_c(g, c, k).wait_send()
+
+
+def some(shape):
+    return tuple(max(1, s) for s in shape)
+
+
+def reduce_to_owners(slot_grads, small, device_count):
+    grid = chip_grid(device_count)
+    zs, ys, xs = grid
+    slots = slot_grads.shape[0] // device_count
+    half, chunks, size = chunking(slots)
+    block = (size, TILE, TILE)
+    bf = jnp.bfloat16
+    dma = pltpu.SemaphoreType.DMA
+    firsts, seconds = (xs, ys), (ys, xs)
+    scratch = (
+        [pltpu.VMEM((chunks, zs, seconds[g]) + block, bf) for g in range(2)]
+        + [pltpu.VMEM(some((chunks, firsts[g] - 1, zs, seconds[g])) + block, bf) for g in range(2)]
+        + [pltpu.VMEM(some((chunks, seconds[g] - 1, zs)) + block, bf) for g in range(2)]
+        + [pltpu.VMEM(some((chunks, zs - 1)) + block, bf) for g in range(2)]
+        + [pltpu.VMEM((3,) + small.shape, jnp.float32)]
+        + [pltpu.VMEM((max(1, n - 1),) + small.shape, jnp.float32) for n in grid]
+        + [dma((2, chunks))]
+        + [dma(some((chunks, firsts[g] - 1))) for g in range(2)] * 2
+        + [dma(some((chunks, seconds[g] - 1))) for g in range(2)] * 2
+        + [dma(some((chunks, zs - 1))) for g in range(2)] * 2
+        + [dma((max(1, n - 1),)) for n in grid] * 2
+    )
+    return pl.pallas_call(
+        functools.partial(rs_kernel, grid),
+        out_shape=[jax.ShapeDtypeStruct((slots, TILE, TILE), jnp.float32), jax.ShapeDtypeStruct(small.shape, jnp.float32)],
+        in_specs=[ANY, pl.BlockSpec(memory_space=pltpu.VMEM)],
+        out_specs=[pl.BlockSpec(memory_space=pltpu.VMEM)] * 2,
+        scratch_shapes=scratch,
+        compiler_params=pltpu.CompilerParams(collective_id=1, has_side_effects=True, vmem_limit_bytes=48 << 20),
+        name="reduce_to_owners",
+    )(slot_grads.reshape(zs, ys, xs, slots, TILE, TILE), small)
+
+
+def ag_kernel(grid, own_ref, small_ref, out_ref, small_out_ref,
+              load_sem, z_send, z_recv, b_send0, b_send1, b_recv0, b_recv1, a_send0, a_send1, a_recv0, a_recv1,
+              s_load, ssz, ssy, ssx, srz, sry, srx):
+    zs, ys, xs = grid
+    z, y, x = place(grid)
+    tos = peers(grid)
+    to_z, to_y, to_x = tos
+    slots = own_ref.shape[0]
+    half, chunks, size = chunking(slots)
+    first = ((xs, to_x), (ys, to_y))
+    second = ((ys, to_y), (xs, to_x))
+    b_send, b_recv, a_send, a_recv = (b_send0, b_send1), (b_recv0, b_recv1), (a_send0, a_send1), (a_recv0, a_recv1)
+    s_send, s_recv = (ssz, ssy, ssx), (srz, sry, srx)
+
+    def span(g, c):
+        return pl.ds(g * half + c * size, size)
+
+    def send_z(g, c, k):
+        return remote(own_ref.at[span(g, c)], out_ref.at[z, y, x, span(g, c)],
+                      z_send.at[g, c, k - 1], z_recv.at[g, c, k - 1], to_z(k))
+
+    def send_b(g, c, k):
+        part = out_ref.at[:, y, x, span(g, c)]
+        return remote(part, part, b_send[g].at[c, k - 1], b_recv[g].at[c, k - 1], second[g][1](k))
+
+    def send_a(g, c, k):
+        part = out_ref.at[:, :, x, span(g, c)] if g == 0 else out_ref.at[:, y, :, span(g, c)]
+        return remote(part, part, a_send[g].at[c, k - 1], a_recv[g].at[c, k - 1], first[g][1](k))
+
+    def send_s(axis, k):
+        if axis == 0:
+            source, target = small_ref, small_out_ref.at[z, y, x]
+        else:
+            source = target = small_out_ref.at[:, y, x] if axis == 1 else small_out_ref.at[:, :, x]
+        return remote(source, target, s_send[axis].at[k - 1], s_recv[axis].at[k - 1], tos[axis](k))
+
+    keep = pltpu.make_async_copy(own_ref, out_ref.at[z, y, x], load_sem)
+    keep_small = pltpu.make_async_copy(small_ref, small_out_ref.at[z, y, x], s_load)
+    keep.start()
+    keep_small.start()
+    greet(grid)
+
+    for k in range(1, grid[0]):
+        send_s(0, k).start()
+    def start_z(c):
+        for g in range(2):
+            for k in range(1, zs):
+                send_z(g, c, k).start()
+
+    def small_wait(axis):
+        for k in range(1, grid[axis]):
+            send_s(axis, k).wait_recv()
+
+    def small_start(axis):
+        for k in range(1, grid[axis]):
+            send_s(axis, k).start()
+
+    start_z(0)
+    for t in range(chunks + 1):
+        if t < chunks:
+            for g in range(2):
+                for k in range(1, zs):
+                    send_z(g, t, k).wait_recv()
+            if t == 0:
+                keep.wait()
+                keep_small.wait()
+                small_wait(0)
+                small_start(1)
+            if t + 1 < chunks:
+                start_z(t + 1)
+            for g in range(2):
+                for k in range(1, second[g][0]):
+                    send_b(g, t, k).start()
+        if t >= 1:
+            for g in range(2):
+                for k in range(1, second[g][0]):
+                    send_b(g, t - 1, k).wait_recv()
+                for k in range(1, first[g][0]):
+                    send_a(g, t - 1, k).start()
+        if t == 1:
+            small_wait(1)
+            small_start(2)
+    small_wait(2)
+    for c in range(chunks):
+        for g in range(2):
+            for k in range(1, first[g][0]):
+                send_a(g, c, k).wait_recv()
+    for axis in range(3):
+        for k in range(1, grid[axis]):
+            send_s(axis, k).wait_send()
+    for c in range(chunks):
+        for g in range(2):
+            for k in range(1, zs):
+                send_z(g, c, k).wait_send()
+            for k in range(1, second[g][0]):
+                send_b(g, c, k).wait_send()
+            for k in range(1, first[g][0]):
+                send_a(g, c, k).wait_send()
+
+
+def gather_all(own, small, device_count):
+    grid = chip_grid(device_count)
+    zs, ys, xs = grid
+    slots = own.shape[0]
+    half, chunks, size = chunking(slots)
+    dma = pltpu.SemaphoreType.DMA
+    firsts, seconds = (xs, ys), (ys, xs)
+    scratch = (
+        [dma, dma(some((2, chunks, zs - 1))), dma(some((2, chunks, zs - 1)))]
+        + [dma(some((chunks, seconds[g] - 1))) for g in range(2)] * 2
+        + [dma(some((chunks, firsts[g] - 1))) for g in range(2)] * 2
+        + [dma]
+        + [dma((max(1, n - 1),)) for n in grid] * 2
+    )
+    blocks, smalls = pl.pallas_call(
+        functools.partial(ag_kernel, grid),
+        out_shape=[jax.ShapeDtypeStruct(grid + own.shape, own.dtype), jax.ShapeDtypeStruct(grid + small.shape, small.dtype)],
+        in_specs=[pl.BlockSpec(memory_space=pltpu.VMEM)] * 2,
+        out_specs=[ANY, ANY],
+        scratch_shapes=scratch,
+        compiler_params=pltpu.CompilerParams(collective_id=2, has_side_effects=True),
+        name="gather_all",
+    )(own, small)
+    return blocks.reshape((-1,) + own.shape[1:]), smalls.reshape((-1,) + small.shape)
+
+
+def move_tiles_kernel(shapes, unpacking, slots_ref, *refs):
+    count = len(shapes)
+    if unpacking:
+        packed, mats, held, sems = refs[0], refs[1:1 + count], refs[1 + count:-1], refs[-1]
+    else:
+        mats, packed, held, sems = refs[:count], refs[count], refs[count + 1:-1], refs[-1]
+
+    def whole(index):
+        if unpacking:
+            return pltpu.make_async_copy(held[index], mats[index], sems.at[1, index])
+        return pltpu.make_async_copy(mats[index], held[index], sems.at[0, index])
+
+    def tiles(index, offset):
+        height, breadth = shapes[index]
+        down, across = height // TILE, breadth // TILE
+        stage = 0 if unpacking else 1
+
+        def start(i, carry):
+            for j in range(across):
+                tile = held[index].at[pl.ds(pl.multiple_of(i * TILE, TILE), TILE), j * TILE:(j + 1) * TILE]
+                slot = packed.at[slots_ref[offset + i * across + j]]
+                ends = (slot, tile) if unpacking else (tile, slot)
+                pltpu.make_async_copy(*ends, sems.at[stage, index]).start()
+            return carry
+
+        lax.fori_loop(0, down, start, 0)
+        return offset + down * across
+
+    def wait_tiles(index):
+        stage = 0 if unpacking else 1
+        pltpu.make_async_copy(held[index], held[index], sems.at[stage, index]).wait()
+
+    offset = 0
+    if unpacking:
+        for index in range(count):
+            offset = tiles(index, offset)
+        for index in range(count):
+            wait_tiles(index)
+            whole(index).start()
+        for index in range(count):
+            whole(index).wait()
+    else:
+        for index in range(count):
+            whole(index).start()
+        for index in range(count):
+            whole(index).wait()
+            offset = tiles(index, offset)
+        for index in range(count):
+            wait_tiles(index)
+
+
+def unpack_tiles(packed, slots, shapes):
+    return pl.pallas_call(
+        functools.partial(move_tiles_kernel, shapes, True),
+        out_shape=[jax.ShapeDtypeStruct(s, packed.dtype) for s in shapes],
+        in_specs=[pl.BlockSpec(memory_space=pltpu.SMEM), ANY],
+        out_specs=[ANY] * len(shapes),
+        scratch_shapes=[pltpu.VMEM(s, packed.dtype) for s in shapes] + [pltpu.SemaphoreType.DMA((2, len(shapes)))],
+        compiler_params=pltpu.CompilerParams(vmem_limit_bytes=24 << 20),
+        name="unpack_tiles",
+    )(slots, packed)
+
+
+def pack_tiles(mats, slots, slot_count):
+    return pl.pallas_call(
+        functools.partial(move_tiles_kernel, [m.shape for m in mats], False),
+        out_shape=jax.ShapeDtypeStruct((slot_count, TILE, TILE), mats[0].dtype),
+        in_specs=[pl.BlockSpec(memory_space=pltpu.SMEM)] + [ANY] * len(mats),
+        out_specs=ANY,
+        scratch_shapes=[pltpu.VMEM(m.shape, m.dtype) for m in mats] + [pltpu.SemaphoreType.DMA((2, len(mats)))],
+        compiler_params=pltpu.CompilerParams(vmem_limit_bytes=24 << 20),
+        name="pack_tiles",
+    )(slots, *mats)
 
 
 def adam_vector(grad_value, value, first, second):
@@ -358,14 +849,29 @@
     hidden_half = hidden_width // tensor_count
     qblocks = retrieved.shape[0]
     per_owner = retrieved.shape[1] // device_count
-    gathered, shared_whole, split_whole = (
-        lax.all_gather(master[0].astype(jnp.bfloat16), "dp", axis=0, tiled=True),
-        lax.all_gather(shared_vectors.astype(jnp.bfloat16), "dp", axis=1, tiled=True),
-        lax.all_gather(split_vectors[0].astype(jnp.bfloat16), "dp", axis=1, tiled=True),
-    )
-    weights = unpack(
-        jnp.take(gathered, owner_slots, axis=0), model_width, hidden_width, tensor_count
-    )
+    me = lax.axis_index("dp")
+    vectors = jnp.concatenate([shared_vectors, split_vectors[0]], 0)
+    vector_count, vector_width = vectors.shape
+    padded = -(-vector_count // 8) * 8
+    small = jnp.concatenate(
+        [
+            jnp.pad(vectors, ((0, padded - vector_count), (0, TILE - vector_width))),
+            retrieved.astype(jnp.float32).reshape(-1, TILE),
+        ],
+        0,
+    )
+    gathered, smalls = gather_all(master[0].astype(jnp.bfloat16), small, device_count)
+    whole = (
+        smalls[:, :vector_count, :vector_width]
+        .transpose(1, 0, 2)
+        .reshape(vector_count, model_width)
+        .astype(jnp.bfloat16)
+    )
+    shared_count = shared_vectors.shape[0]
+    shared_whole, split_whole = whole[:shared_count], whole[shared_count:]
+    shapes = [s[1:] for s in matrix_list(model_width, hidden_width, tensor_count)]
+    names = [s[0] for s in matrix_list(model_width, hidden_width, tensor_count)]
+    weights = dict(zip(names, unpack_tiles(gathered, owner_slots, shapes)))
     shared = shared_whole.astype(jnp.float32)
     biases = split_biases(split_whole.astype(jnp.float32).reshape(-1), half_width, hidden_half)
     zero_half = jnp.zeros((half_width,), jnp.float32)
@@ -384,13 +890,11 @@
     encoder_states, norm_two_back = jax.vjp(layer_norm, pre_two, shared[4], shared[5])
     start_row = jnp.argmax(kept_mask)
     stored = lax.dynamic_slice_in_dim(encoder_states.astype(jnp.bfloat16), start_row, KEEP, 0)
-    owner_base = KEEP * lax.broadcasted_iota(jnp.int32, (1, device_count, 1), 1)
-    wanted = lax.all_to_all(
-        retrieved.reshape(qblocks, device_count, per_owner) - owner_base,
-        "dp",
-        split_axis=1,
-        concat_axis=1,
-        tiled=True,
+    wanted = (
+        smalls[:, padded:].reshape(device_count, qblocks, device_count, per_owner)[:, :, me]
+        .transpose(1, 0, 2)
+        .astype(jnp.int32)
+        - KEEP * me
     )
     served = jnp.take(stored, wanted, axis=0)
     retrieved_entries = lax.all_to_all(
@@ -516,18 +1020,22 @@
         "dec_up": grad_dec_up,
         "dec_down": grad_dec_down,
     }
-    packed = pack(matrix_grads, model_width, hidden_width, tensor_count, tile_size)
-    slot_grads = (
-        jnp.zeros((gathered.shape[0], tile_size, tile_size), jnp.float32)
-        .at[owner_slots]
-        .set(packed)
-    )
-    owned_grads, shared_owned, split_owned = (
-        lax.psum_scatter(slot_grads, "dp", scatter_dimension=0, tiled=True),
-        lax.psum_scatter(shared_grad, "dp", scatter_dimension=1, tiled=True),
-        lax.psum_scatter(split_grad, "dp", scatter_dimension=1, tiled=True),
-    )
-    results = jax.vmap(soap_update)(
+    slot_grads = pack_tiles(
+        [matrix_grads[name].astype(jnp.bfloat16) for name in names], owner_slots, gathered.shape[0]
+    )
+    vector_grads = jnp.pad(
+        jnp.concatenate([shared_grad, split_grad], 0), ((0, padded - vector_count), (0, 0))
+    )
+    owned_grads, vector_sums = reduce_to_owners(slot_grads, vector_grads, device_count)
+    vector_owned = lax.dynamic_slice_in_dim(vector_sums, me * vector_width, vector_width, 1)
+    shared_owned = vector_owned[:shared_count]
+    split_owned = vector_owned[shared_count:vector_count]
+    owned_slots = me * owned_grads.shape[0] + lax.broadcasted_iota(
+        jnp.int32, (owned_grads.shape[0], 1), 0
+    )
+    used = jnp.any(owned_slots == owner_slots[None, :], 1).astype(jnp.int32)
+    results = soap_all(
+        used,
         owned_grads,
         master[0],
         first_moment[0],
@@ -537,7 +1045,7 @@
         left_basis[0],
         right_basis[0],
     )
-    new_first, new_second, new_master, new_left, new_right, new_lbasis, new_rbasis = results
+    new_master, new_first, new_second, new_left, new_right, new_lbasis, new_rbasis = results
     shared_new_first, shared_new_second, shared_updated = adam_vector(
         shared_owned, shared_vectors, shared_first, shared_second
     )

time: 3280 us -> 1030 us (0.31)
  other arithmetic: 1510 us -> 112 us
  waiting for transfers between devices: 1020 us -> 149 us
  Pallas kernels: 0 us -> 428 us
  local copies, waits for them, and re-layouts: 339 us -> 83.5 us
  blocking collectives: 80.5 us -> 0 us
  matrix products: 284 us -> 218 us
    another operation x9 -> x0, other arithmetic: 1390 us -> none  [the longest x5 757 us: orthonormal(): factor = jnp.linalg.cholesky(gram)]
    reduce_scatter x1 -> x0, waiting for transfers between devices: 683 us -> none  [local(): lax.psum_scatter(slot_grads, 'dp', scatter_dimension=0, tiled=True)]
    pallas_call x0 -> x5, Pallas kernels: none -> 428 us  [the longest x1 159 us: gather_all(): pl.pallas_call(functools.partial(ag_kernel, grid), out_shape=[jax.ShapeDt...]
    all_gather x1 -> x0, waiting for transfers between devices: 114 us -> none  [local(): lax.all_gather(master[0].astype(jnp.bfloat16), 'dp', axis=0, tiled=True)]
    unnamed x14 -> x8, waiting for transfers between devices: 103 us -> 0.13 us
    scatter x1 -> x0, local copies, waits for them, and re-layouts: 92.3 us -> none  [local(): slot_grads = jnp.zeros((gathered.shape[0], tile_size, tile_size), jnp.flo...]
    all_gather x2 -> x0, blocking collectives: 80.5 us -> none  [the longest x1 43.4 us: local(): lax.all_gather(split_vectors[0].astype(jnp.bfloat16), 'dp', axis=1, tiled...]
    reshape x18 -> x1, local copies, waits for them, and re-layouts: 66 us -> 0.08 us  [local(): smalls[:, padded:].reshape(device_count, qblocks, device_count, per_owner)]
  transfers between devices with their start and end apart: 15 -> 10, of which waited for: 10 -> 9; matrix products, arithmetic and copies ran while one was open for 10% -> 9% of each run, Pallas kernels for 0% -> 1%
where the time goes in v1:
time: 1030 us; the launch traced here: 1020 us
  Pallas kernels  428 us (42%)
  matrix products  218 us (21%)
  waiting for transfers between devices  149 us (14%)
  other arithmetic  112 us (11%)
  local copies, waits for them, and re-layouts  83.5 us (8%)
  between operations  19 us (2%)
  starting transfers between devices  14.9 us (1%)
    pallas_call x1, Pallas kernels, gather_all(): pl.pallas_call(functools.partial(ag_kernel, grid), out_shape=[jax.ShapeDt...  159 us
    pallas_call x1, Pallas kernels, reduce_to_owners(): pl.pallas_call(functools.partial(rs_kernel, grid), out_shape=[jax.ShapeDt...  158 us
    pallas_call x1, Pallas kernels, soap_all(): pl.pallas_call(functools.partial(soap_kernel, passes), grid=(s // nb,), o...  95.7 us
    psum x4, waiting for transfers between devices, tensor_sum(): return lax.psum(values.astype(jnp.bfloat16), 'tensor').astype(jnp.float32)  55.7 us
    dot_general x10, matrix products, project(): return jnp.dot(left, right, preferred_element_type=jnp.float32)  46.4 us
    psum x4, waiting for transfers between devices, tensor_back(): lax.psum(for_sending(values), 'tensor')  43.5 us
    unnamed x452, local copies, waits for them, and re-layouts  39 us
    dot_general x11, matrix products, times_transposed(): jnp.einsum('sa,ba->sb', left, right, preferred_element_type=jnp.float32)  33.4 us
  transfers between devices with their start and end apart: 10, of which 9 were waited for; matrix products, arithmetic and copies ran while one was open for 9% of the time, Pallas kernels for 1%

profile of v1, /device:TPU:0, one launch (start us, length us, event | category | flops | bytes accessed | tf_op | source)
XLA Modules:
  0.0 1024.3 jit_solution(8574736997976792501)
XLA Ops:
  7.3 2.7 bitcast_convert_fusion.own_ref
  10.7 158.8 %gather_all.1 = (bf16[4,2,2,32,128,128]{5,4,3,2,1,0:T(8,128)(2,1)}, f32[4,2,2,32,128]{4,3,2,1,0:T(8,128)}) custom-call(bf16[32,128,128]{2,1,0:T(8,128)(2,1)} %bitcast_convert_fusion.own_ref, f32[32,128]{1,0:T(8,128)} %pad_maximum_fusion.5.small_ref), custom_call_target="tpu_custom_call" | custom-call | tf_op jit(solution)/shard_map/gather_all/pallas_call | solution.py:724
  171.2 6.6 unpack_tiles.1
  183.4 10.2 multiply_reduce_fusion.1
  193.7 10.6 %exponential_reduce_fusion = f32[6,1024]{1,0:T(8,128)S(1)} fusion(f32[6,1024,1024]{1,2,0:T(8,128)} %get-tuple-element.222, f32[6,1024]{1,0:T(8,128)S(1)} %is-finite_select_fusion), kind=kLoop, calls=%fused_computation.4 | loop fusion | flops 18868224 | bytes 25214976 | tf_op jit(solution)/shard_map/reduce_sum | solution.py:114
  204.3 10.5 %fusion.33 = bf16[6,64,1024]{2,1,0:T(8,128)(2,1)S(1)} fusion(bf16[1024,6,64]{0,2,1:T(8,128)(2,1)S(1)} %bitcast.240, f32[6,1024,1024]{1,2,0:T(8,128)} %get-tuple-element.222, f32[6,1024]{1,0:T(8,128)S(1)} %log_add_fusion), kind=kOutput, calls=%fused_computation.140 | convolution fusion | flops 824573952 | bytes 26763264 | tf_op jit(solution)/shard_map/bhqk,bkhe->bqhe/dot_general | solution.py:116
  222.9 3.8 fusion.103
  227.6 4.0 exponential_reduce_fusion.2
  236.9 3.9 all-reduce.15.cloned.1.call-done
  245.4 17.9 %multiply_convert_fusion.3 = (bf16[1024,1536]{1,0:T(8,128)(2,1)S(1)}, f32[1024,1536]{1,0:T(8,128)}, f32[1024,1536]{1,0:T(8,128)}) fusion(f32[1536]{0:T(1024)S(1)} %add.373, bf16[768,1536]{1,0:T(8,128)(2,1)S(1)} %copy-done.12, f32[768]{0:T(1024)S(1)} %add.370, f32[768]{0:T(1024)S(1)} %mul.510, f32[1024]{0:T(1024)S(1)} %fusion.57, ...), kind=kOutput, calls=%fused_computation.23 | convolution fusion | flops 2526806016 | bytes 21257216 | tf_op jit(solution)/shard_map/dot_general | solution.py:79
  265.0 3.7 convolution_convert_fusion.10
  272.6 19.1 %all-reduce.29.cloned.1.call-done = (bf16[1024,768]{1,0:T(8,128)(2,1)}, bf16[512,768]{1,0:T(8,128)(2,1)}) async-done(((bf16[1024,768]{1,0:T(8,128)(2,1)}, bf16[512,768]{1,0:T(8,128)(2,1)}), (bf16[1024,768]{1,0:T(8,128)(2,1)}, bf16[512,768]{1,0:T(8,128)(2,1)})) %all-reduce.29.cloned.1.call-update) | async-done | bytes 2359312 | tf_op jit(solution)/shard_map/psum | solution.py:91
  291.7 3.2 fusion.95
  298.4 5.2 gather_fusion
  303.7 2.9 broadcast_select_fusion
  306.6 6.8 all-to-all-start
  320.1 27.6 %all-to-all-done = bf16[1,16,64,768]{3,2,0,1:T(8,128)(2,1)} async-done(((bf16[1,16,64,768]{3,2,0,1:T(8,128)(2,1)}), bf16[1,16,64,768]{3,2,0,1:T(8,128)(2,1)}, u32[]{:S(2)}, u32[]{:S(2)}) %all-to-all-start) | async-done | bytes 1572896 | tf_op jit(solution)/shard_map/all_to_all | solution.py:900
  347.7 2.9 fusion.32
  352.7 11.3 %exponential_reduce_fusion.1 = f32[6,512]{1,0:T(8,128)S(1)} fusion(f32[6,512,1024]{2,1,0:T(8,128)S(1)} %get-tuple-element.227, f32[6,512]{1,0:T(8,128)S(1)} %is-finite_select_fusion.1), kind=kLoop, calls=%fused_computation.10 | loop fusion | flops 9434112 | bytes 12607488 | tf_op jit(solution)/shard_map/reduce_sum | solution.py:114
  364.1 2.8 convolution_convert_fusion.27
  374.9 16.2 %all-reduce.17.cloned.1.call-done = bf16[512,768]{1,0:T(8,128)(2,1)} async-done(((bf16[512,768]{1,0:T(8,128)(2,1)}), bf16[512,768]{1,0:T(8,128)(2,1)}) %all-reduce.17.cloned.1.call-update) | async-done | bytes 786448 | tf_op jit(solution)/shard_map/psum | solution.py:91
  391.1 2.4 fusion.94
  394.6 9.4 multiply_convert_fusion.4
  411.6 16.4 %all-reduce.19.cloned.1.call-done = bf16[512,768]{1,0:T(8,128)(2,1)} async-done(((bf16[512,768]{1,0:T(8,128)(2,1)}), bf16[512,768]{1,0:T(8,128)(2,1)}) %all-reduce.19.cloned.1.call-update) | async-done | bytes 786448 | tf_op jit(solution)/shard_map/psum | solution.py:91
  428.0 2.3 fusion.92
  435.6 2.9 convert_reduce_fusion.2
  442.3 20.3 %all-reduce.21.cloned.1.call-done = bf16[512,768]{1,0:T(8,128)(2,1)} async-done(((bf16[512,768]{1,0:T(8,128)(2,1)}), bf16[512,768]{1,0:T(8,128)(2,1)}) %all-reduce.21.cloned.1.call-update) | async-done | bytes 786448 | tf_op jit(solution)/shard_map/psum | solution.py:96
  462.6 3.8 multiply_reduce_fusion.11
  468.5 10.8 %multiply_reduce_fusion.2 = (f32[6,512]{1,0:T(8,128)S(1)}, f32[6,512,1024]{2,1,0:T(8,128)}) fusion(f32[6,512,1024]{2,1,0:T(8,128)} %copy-done.30, f32[6,512]{1,0:T(8,128)S(1)} %copy-done.105, bf16[512,6,64]{0,2,1:T(8,128)(2,1)S(1)} %bitcast.291, bf16[1024,6,64]{0,2,1:T(8,128)(2,1)S(1)} %bitcast.242), kind=kOutput, calls=%fused_computation.8 | convolution fusion | flops 415233024 | bytes 26370048 | tf_op jit(solution)/shard_map/bqhe,bkhe->bhqk/dot_general | solution.py:128
  479.4 2.6 convolution_convert_fusion.13
  482.0 6.8 multiply_convert_fusion.1
  491.4 2.6 convolution_convert_fusion.9
  494.0 21.7 %all-reduce.23.cloned.1.call-done = bf16[1,16,64,768]{3,2,0,1:T(8,128)(2,1)} async-done(((bf16[1,16,64,768]{3,2,0,1:T(8,128)(2,1)}), bf16[1,16,64,768]{3,2,0,1:T(8,128)(2,1)}) %all-reduce.23.cloned.1.call-update) | async-done | bytes 1572880 | tf_op jit(solution)/shard_map/psum | solution.py:96
  515.8 6.8 all-to-all-start.1
  524.6 3.5 convolution_convert_fusion.2.refs_10_
  528.2 3.1 convolution_convert_fusion.3.refs_9_
  534.9 22.1 %all-to-all-done.1 = bf16[1,16,64,768]{3,2,0,1:T(8,128)(2,1)} async-done(((bf16[1,16,64,768]{3,2,0,1:T(8,128)(2,1)}), bf16[1,16,64,768]{3,2,0,1:T(8,128)(2,1)}, u32[]{:S(2)}, u32[]{:S(2)}) %all-to-all-start.1) | async-done | bytes 1572896 | tf_op jit(solution)/shard_map/all_to_all | solution.py:955
  556.9 3.6 fusion.23
  562.4 5.0 dynamic_update_slice.3
  567.4 4.3 multiply_reduce_fusion.5
  573.8 9.3 convert_reduce_fusion
  584.8 3.7 convolution_convert_fusion.8
  595.0 2.4 convolution_convert_fusion.22.refs_6_
  597.4 4.0 convolution_convert_fusion.11.refs_7_
  602.7 4.5 convolution_convert_fusion.refs_3_
  607.2 4.2 convolution_convert_fusion.1.refs_2_
  613.0 3.9 multiply_reduce_fusion.12
  622.3 2.5 fusion.45
  629.6 2.9 multiply_reduce_fusion.6
  632.5 2.4 fusion.88
  636.9 20.6 %multiply_reduce_fusion = (f32[6,1024]{1,0:T(8,128)}, f32[6,1024,1024]{1,2,0:T(8,128)}) fusion(f32[6,1024,1024]{1,2,0:T(8,128)} %get-tuple-element.222, f32[6,1024]{1,0:T(8,128)} %copy-done.101, bf16[1024,6,64]{0,2,1:T(8,128)(2,1)} %bitcast.255, bf16[1024,6,64]{0,2,1:T(8,128)(2,1)} %bitcast.239), kind=kOutput, calls=%fused_computation.2 | convolution fusion | flops 830466048 | bytes 51953664 | tf_op jit(solution)/shard_map/bqhe,bkhe->bhqk/dot_general | solution.py:128
  657.5 17.0 %multiply_convert_fusion = bf16[6,1024,1024]{1,2,0:T(8,128)(2,1)S(1)} fusion(f32[6,1024,1024]{1,2,0:T(8,128)} %get-tuple-element.232, f32[6,1024,1024]{1,2,0:T(8,128)} %get-tuple-element.222, f32[6,1024]{1,0:T(8,128)} %get-tuple-element.231, f32[6,1024]{1,0:T(8,128)} %copy-done.101), kind=kLoop, calls=%fused_computation.1 | loop fusion | flops 31457280 | bytes 62963712 | tf_op jit(solution)/shard_map/convert_element_type | solution.py:129
  674.5 4.5 copy-done.32
  679.0 3.2 multiply_convert_fusion.6
  682.2 9.4 multiply_convert_fusion.5
  691.6 13.6 %fusion.36 = bf16[6,64,1024]{2,1,0:T(8,128)(2,1)} fusion(bf16[1024,6,64]{0,2,1:T(8,128)(2,1)} %bitcast.256, f32[6,1024,1024]{1,2,0:T(8,128)} %get-tuple-element.222, f32[6,1024]{1,0:T(8,128)} %copy-done.101), kind=kOutput, calls=%fused_computation.141 | convolution fusion | flops 824573952 | bytes 26763264 | tf_op jit(solution)/shard_map/bhqk,bqhe->bkhe/dot_general | solution.py:125
  707.3 5.7 convolution_convert_fusion.7
  735.0 2.9 fusion.17.refs_4_
  741.0 2.3 fusion.16.refs_0_
  744.3 8.5 pack_tiles.1
  752.9 3.2 add_reduce_fusion.2
  756.2 3.6 add_reduce_fusion
  760.3 158.4 %reduce_to_owners.1 = (f32[32,128,128]{2,1,0:T(8,128)S(1)}, f32[24,768]{1,0:T(8,128)S(1)}) custom-call(bf16[4,2,2,32,128,128]{5,4,3,2,1,0:T(8,128)(2,1)} %bitcast.233, f32[24,768]{1,0:T(8,128)S(1)} %pad.10.refs_1_), custom_call_target="tpu_custom_call" | custom-call | tf_op jit(solution)/shard_map/reduce_to_owners/pallas_call | solution.py:599
  921.3 95.7 %soap.1 = (f32[32,128,128]{2,1,0:T(8,128)}, f32[32,128,128]{2,1,0:T(8,128)}, f32[32,128,128]{2,1,0:T(8,128)}, f32[32,128,128]{2,1,0:T(8,128)}, f32[32,128,128]{2...) custom-call(s32[32]{0:T(128)S(1)} %convert_element_type.405.used_ref, ...), custom_call_target="tpu_custom_call" | custom-call | tf_op jit(solution)/shard_map/soap/pallas_call | solution.py:357
  (608 shorter events, 135.5 us)
Async XLA Ops:
  7.2 262.6 %copy-start = (s32[1024]{0:T(1024)S(1)}, s32[1024]{0:T(1024)}, u32[]{:S(2)}) copy-start(s32[1024]{0:T(1024)} %param.23) | copy-start | bytes 12292
  7.2 164.0 %copy-start.9 = (s32[504]{0:T(512)S(1)}, s32[504]{0:T(512)}, u32[]{:S(2)}) copy-start(s32[504]{0:T(512)} %slots_ref.3) | copy-start | bytes 6052
  7.3 233.6 %all-reduce.15.cloned.1.call-start = ((), (), s32[]{:S(2)}) async-start(), calls=%async_computation.2 | async-start | bytes 3145728 | tf_op jit(solution)/shard_map/psum | solution.py:91
  177.9 37.0 %copy-start.28 = (bf16[384,768]{1,0:T(8,128)(2,1)}, bf16[384,768]{1,0:T(8,128)(2,1)S(1)}, u32[]{:S(2)}) copy-start(bf16[384,768]{1,0:T(8,128)(2,1)S(1)} %get-tuple-element.43) | copy-start | bytes 1769476
  177.9 41.2 %copy-start.22 = (bf16[768,1152]{1,0:T(8,128)(2,1)}, bf16[768,1152]{1,0:T(8,128)(2,1)S(1)}, u32[]{:S(2)}) copy-start(bf16[768,1152]{1,0:T(8,128)(2,1)S(1)} %get-tuple-element.46) | copy-start | bytes 5308420
  177.9 56.8 %copy-start.7 = (bf16[384,768]{1,0:T(8,128)(2,1)}, bf16[384,768]{1,0:T(8,128)(2,1)S(1)}, u32[]{:S(2)}) copy-start(bf16[384,768]{1,0:T(8,128)(2,1)S(1)} %get-tuple-element.47) | copy-start | bytes 1769476
  193.7 10.7 %copy-start.68 = (bf16[1024,384]{0,1:T(8,128)(2,1)S(1)}, bf16[1024,384]{0,1:T(8,128)(2,1)}, u32[]{:S(2)}) copy-start(bf16[1024,384]{0,1:T(8,128)(2,1)} %get-tuple-element.184) | copy-start | bytes 2359300
  204.3 10.5 %copy-start.101 = (f32[6,1024]{1,0:T(8,128)}, f32[6,1024]{1,0:T(8,128)S(1)}, u32[]{:S(2)}) copy-start(f32[6,1024]{1,0:T(8,128)S(1)} %log_add_fusion) | copy-start | bytes 73732
  217.9 73.8 %all-reduce.29.cloned.1.call-start = ((), (), s32[]{:S(2)}) async-start(), calls=%async_computation.9 | async-start | bytes 4718592 | tf_op jit(solution)/shard_map/psum | solution.py:91
  227.5 64.2 %copy-start.116 = (f32[768]{0:T(1024)}, f32[768]{0:T(1024)S(1)}, u32[]{:S(2)}) copy-start(f32[768]{0:T(1024)S(1)} %mul.510) | copy-start | bytes 9220
  227.5 64.2 %copy-start.165 = (f32[768]{0:T(1024)}, f32[768]{0:T(1024)S(1)}, u32[]{:S(2)}) copy-start(f32[768]{0:T(1024)S(1)} %add.370) | copy-start | bytes 9220
  227.6 17.8 %copy-start.197 = (f32[1536]{0:T(1024)}, f32[1536]{0:T(1024)S(1)}, u32[]{:S(2)}) copy-start(f32[1536]{0:T(1024)S(1)} %add.373) | copy-start | bytes 18436
  245.4 17.9 %copy-start.139 = (f32[1024]{0:T(1024)}, f32[1024]{0:T(1024)S(1)}, u32[]{:S(2)}) copy-start(f32[1024]{0:T(1024)S(1)} %multiply_reduce_fusion.10) | copy-start | bytes 12292
  245.4 46.3 %copy-start.119 = (f32[1024]{0:T(1024)}, f32[1024]{0:T(1024)S(1)}, u32[]{:S(2)}) copy-start(f32[1024]{0:T(1024)S(1)} %fusion.57) | copy-start | bytes 12292
  245.4 19.6 %copy-start.15 = (bf16[1536,768]{1,0:T(8,128)(2,1)S(1)}, bf16[1536,768]{1,0:T(8,128)(2,1)}, u32[]{:S(2)}) copy-start(bf16[1536,768]{1,0:T(8,128)(2,1)} %copy-done.14) | copy-start | bytes 7077892
  269.7 25.8 %copy-start.122 = (f32[768]{0:T(1024)}, f32[768]{0:T(1024)S(1)}, u32[]{:S(2)}) copy-start(f32[768]{0:T(1024)S(1)} %mul.519) | copy-start | bytes 9220
  271.9 23.1 %copy-start.114 = (s32[16,1,1,64]{3,0,2,1:T(8,128)}, s32[16,1,1,64]{3,0,2,1:T(8,128)S(1)}, u32[]{:S(2)}) copy-start(s32[16,1,1,64]{3,0,2,1:T(8,128)S(1)} %get-tuple-element.175) | copy-start | bytes 12292
  303.7 11.2 %copy-start.200 = (f32[384]{0:T(512)S(1)}, f32[384]{0:T(512)}, u32[]{:S(2)}) copy-start(f32[384]{0:T(512)} %get-tuple-element.214) | copy-start | bytes 4612
  303.7 11.8 %copy-start.53 = (bf16[512,768]{1,0:T(8,128)(2,1)S(1)}, bf16[512,768]{1,0:T(8,128)(2,1)}, u32[]{:S(2)}) copy-start(bf16[512,768]{1,0:T(8,128)(2,1)} %param.20) | copy-start | bytes 2359300
  303.7 11.8 %copy-start.55 = (bf16[512,768]{1,0:T(8,128)(2,1)S(1)}, bf16[512,768]{1,0:T(8,128)(2,1)}, u32[]{:S(2)}) copy-start(bf16[512,768]{1,0:T(8,128)(2,1)} %get-tuple-element.154) | copy-start | bytes 2359300
  306.6 41.2 %all-to-all-start = ((bf16[1,16,64,768]{3,2,0,1:T(8,128)(2,1)}), bf16[1,16,64,768]{3,2,0,1:T(8,128)(2,1)}, u32[]{:S(2)}, u32[]{:S(2)}) async-start(bf16[1,16,64,768]{3,2,0,1:T(8,128)(2,1)} %broadcast_select_fusion), calls=%async_computation | async-start | bytes 3145728 | tf_op jit(solution)/shard_map/all_to_all | solution.py:900
  313.4 77.7 %all-reduce.17.cloned.1.call-start = ((), (), s32[]{:S(2)}) async-start(), calls=%async_computation.3 | async-start | bytes 1572864 | tf_op jit(solution)/shard_map/psum | solution.py:91
  315.8 31.9 %copy-start.26 = (bf16[768,768]{1,0:T(8,128)(2,1)S(1)}, bf16[768,768]{1,0:T(8,128)(2,1)}, u32[]{:S(2)}) copy-start(bf16[768,768]{1,0:T(8,128)(2,1)} %copy-done.25) | copy-start | bytes 3538948
  320.1 30.7 %copy-start.88 = (bf16[512,384]{0,1:T(8,128)(2,1)}, bf16[512,384]{0,1:T(8,128)(2,1)S(1)}, u32[]{:S(2)}) copy-start(bf16[512,384]{0,1:T(8,128)(2,1)S(1)} %fusion.43) | copy-start | bytes 1179652
  350.7 13.3 %copy-start.69 = (bf16[1,1024,384]{1,2,0:T(8,128)(2,1)}, bf16[1,1024,384]{1,2,0:T(8,128)(2,1)S(1)}, u32[]{:S(2)}) copy-start(bf16[1,1024,384]{1,2,0:T(8,128)(2,1)S(1)} %get-tuple-element.189) | copy-start | bytes 2359300
  352.7 11.4 %copy-start.30 = (f32[6,512,1024]{2,1,0:T(8,128)}, f32[6,512,1024]{2,1,0:T(8,128)S(1)}, u32[]{:S(2)}) copy-start(f32[6,512,1024]{2,1,0:T(8,128)S(1)} %get-tuple-element.227) | copy-start | bytes 37748740
  369.1 25.4 %copy-start.18 = (bf16[768,1536]{1,0:T(8,128)(2,1)S(1)}, bf16[768,1536]{1,0:T(8,128)(2,1)}, u32[]{:S(2)}) copy-start(bf16[768,1536]{1,0:T(8,128)(2,1)} %copy-done.17) | copy-start | bytes 7077892
  369.2 58.8 %all-reduce.19.cloned.1.call-start = ((), (), s32[]{:S(2)}) async-start(), calls=%async_computation.4 | async-start | bytes 1572864 | tf_op jit(solution)/shard_map/psum | solution.py:91
  393.5 10.5 %copy-start.36 = (f32[512,768]{1,0:T(8,128)}, f32[512,768]{1,0:T(8,128)S(1)}, u32[]{:S(2)}) copy-start(f32[512,768]{1,0:T(8,128)S(1)} %get-tuple-element.173) | copy-start | bytes 4718596
  394.6 10.5 %copy-start.20 = (bf16[1536,768]{1,0:T(8,128)(2,1)S(1)}, bf16[1536,768]{1,0:T(8,128)(2,1)}, u32[]{:S(2)}) copy-start(bf16[1536,768]{1,0:T(8,128)(2,1)} %copy-done.19) | copy-start | bytes 7077892
  407.4 55.2 %all-reduce.21.cloned.1.call-start = ((), (), s32[]{:S(2)}) async-start(), calls=%async_computation.5 | async-start | bytes 1572864 | tf_op jit(solution)/shard_map/psum | solution.py:96
  442.0 24.4 %copy-start.160 = (f32[512]{0:T(512)S(1)}, f32[512]{0:T(512)}, u32[]{:S(2)}) copy-start(f32[512]{0:T(512)} %copy-done.159) | copy-start | bytes 6148
  442.0 24.4 %copy-start.37 = (f32[512,768]{1,0:T(8,128)S(1)}, f32[512,768]{1,0:T(8,128)}, u32[]{:S(2)}) copy-start(f32[512,768]{1,0:T(8,128)} %copy-done.36) | copy-start | bytes 4718596
  442.0 24.4 %copy-start.129 = (f32[768]{0:T(1024)S(1)}, f32[768]{0:T(1024)}, u32[]{:S(2)}) copy-start(f32[768]{0:T(1024)} %mul.533) | copy-start | bytes 9220
  442.0 24.4 %copy-start.134 = (f32[512]{0:T(512)S(1)}, f32[512]{0:T(512)}, u32[]{:S(2)}) copy-start(f32[512]{0:T(512)} %copy-done.133) | copy-start | bytes 6148
  442.0 24.5 %copy-start.147 = (f32[512]{0:T(512)S(1)}, f32[512]{0:T(512)}, u32[]{:S(2)}) copy-start(f32[512]{0:T(512)} %copy-done.146) | copy-start | bytes 6148
  442.0 24.4 %copy-start.155 = (f32[512]{0:T(512)S(1)}, f32[512]{0:T(512)}, u32[]{:S(2)}) copy-start(f32[512]{0:T(512)} %copy-done.154) | copy-start | bytes 6148
  442.0 73.7 %all-reduce.23.cloned.1.call-start = ((), (), s32[]{:S(2)}) async-start(), calls=%async_computation.6 | async-start | bytes 3145728 | tf_op jit(solution)/shard_map/psum | solution.py:96
  467.4 12.0 %copy-start.149 = (f32[512]{0:T(512)}, f32[512]{0:T(512)S(1)}, u32[]{:S(2)}) copy-start(f32[512]{0:T(512)S(1)} %negate_multiply_fusion.5) | copy-start | bytes 6148
  467.4 12.0 %slice-start = ((s8[12582912]{0:T(1024)(128)(4,1)}), s8[4194304]{0:T(1024)(128)(4,1)S(1)}, s32[]{:S(2)}) async-start(s8[12582912]{0:T(1024)(128)(4,1)} %bitcast.227), calls=%async_computation.10 | async-start | bytes 8388608
  468.5 10.8 %slice-start.1 = ((s8[12582912]{0:T(1024)(128)(4,1)}), s8[4194304]{0:T(1024)(128)(4,1)S(1)}, s32[]{:S(2)}) async-start(s8[12582912]{0:T(1024)(128)(4,1)} %bitcast.227), calls=%async_computation.11 | async-start | bytes 8388608
  468.5 10.8 %slice-start.2 = ((s8[12582912]{0:T(1024)(128)(4,1)}), s8[4194304]{0:T(1024)(128)(4,1)S(1)}, s32[]{:S(2)}) async-start(s8[12582912]{0:T(1024)(128)(4,1)} %bitcast.227), calls=%async_computation.12 | async-start | bytes 8388608
  494.0 29.1 %copy-start.115 = (s32[16,1,1,64]{3,0,2,1:T(8,128)S(1)}, s32[16,1,1,64]{3,0,2,1:T(8,128)}, u32[]{:S(2)}) copy-start(s32[16,1,1,64]{3,0,2,1:T(8,128)} %copy-done.114) | copy-start | bytes 12292
  494.0 29.4 %copy-start.170 = (f32[768]{0:T(1024)S(1)}, f32[768]{0:T(1024)}, u32[]{:S(2)}) copy-start(f32[768]{0:T(1024)} %get-tuple-element.142) | copy-start | bytes 9220
  494.0 29.9 %copy-start.169 = (f32[768]{0:T(1024)S(1)}, f32[768]{0:T(1024)}, u32[]{:S(2)}) copy-start(f32[768]{0:T(1024)} %get-tuple-element.148) | copy-start | bytes 9220
  494.0 30.5 %copy-start.156 = (f32[512]{0:T(512)S(1)}, f32[512]{0:T(512)}, u32[]{:S(2)}) copy-start(f32[512]{0:T(512)} %copy-done.154) | copy-start | bytes 6148
  515.8 41.2 %all-to-all-start.1 = ((bf16[1,16,64,768]{3,2,0,1:T(8,128)(2,1)}), bf16[1,16,64,768]{3,2,0,1:T(8,128)(2,1)}, u32[]{:S(2)}, u32[]{:S(2)}) async-start(bf16[1,16,64,768]{3,2,0,1:T(8,128)(2,1)} %all-reduce.23.cloned.1.call-done), calls=%async_computation.1 | async-start | bytes 3145728 | tf_op jit(solution)/shard_map/all_to_all | solution.py:955
  522.6 90.3 %all-reduce.27.cloned.1.call-start = ((), (), s32[]{:S(2)}) async-start(), calls=%async_computation.8 | async-start | bytes 4718592 | tf_op jit(solution)/shard_map/psum | solution.py:96
  533.4 27.2 %copy-start.90 = (bf16[6,64,512]{2,1,0:T(8,128)(2,1)}, bf16[6,64,512]{2,1,0:T(8,128)(2,1)S(1)}, u32[]{:S(2)}) copy-start(bf16[6,64,512]{2,1,0:T(8,128)(2,1)S(1)} %get-tuple-element.238) | copy-start | bytes 1179652
  573.8 11.0 %copy-start.13 = (bf16[768,1536]{1,0:T(8,128)(2,1)S(1)}, bf16[768,1536]{1,0:T(8,128)(2,1)}, u32[]{:S(2)}) copy-start(bf16[768,1536]{1,0:T(8,128)(2,1)} %copy-done.11) | copy-start | bytes 7077892
  588.5 164.3 %all-reduce.25.cloned.1.call-start = ((), (), s32[]{:S(2)}) async-start(), calls=%async_computation.7 | async-start | bytes 4718592 | tf_op jit(solution)/shard_map/psum | solution.py:96
  635.0 22.5 %copy-start.173 = (f32[1024]{0:T(1024)}, f32[1024]{0:T(1024)S(1)}, u32[]{:S(2)}) copy-start(f32[1024]{0:T(1024)S(1)} %negate_multiply_fusion.2) | copy-start | bytes 12292
  657.5 21.5 %copy-start.67 = (bf16[1024,384]{0,1:T(8,128)(2,1)S(1)}, bf16[1024,384]{0,1:T(8,128)(2,1)}, u32[]{:S(2)}) copy-start(bf16[1024,384]{0,1:T(8,128)(2,1)} %copy-done.66) | copy-start | bytes 2359300
  717.9 15.9 %copy-start.164 = (f32[768]{0:T(1024)S(1)}, f32[768]{0:T(1024)}, u32[]{:S(2)}) copy-start(f32[768]{0:T(1024)} %get-tuple-element.135) | copy-start | bytes 9220
  717.9 16.5 %copy-start.163 = (f32[768]{0:T(1024)S(1)}, f32[768]{0:T(1024)}, u32[]{:S(2)}) copy-start(f32[768]{0:T(1024)} %get-tuple-element.140) | copy-start | bytes 9220
  719.4 18.5 %copy-start.162 = (f32[512]{0:T(512)S(1)}, f32[512]{0:T(512)}, u32[]{:S(2)}) copy-start(f32[512]{0:T(512)} %copy-done.161) | copy-start | bytes 6148
  760.2 158.5 %copy-start.181 = (f32[1,7,48]{2,0,1:T(1,128)S(1)}, f32[1,7,48]{2,0,1:T(1,128)}, u32[]{:S(2)}) copy-start(f32[1,7,48]{2,0,1:T(1,128)} %param.35) | copy-start | bytes 4036
  760.2 158.5 %copy-start.202 = (f32[1,7,48]{2,0,1:T(1,128)S(1)}, f32[1,7,48]{2,0,1:T(1,128)}, u32[]{:S(2)}) copy-start(f32[1,7,48]{2,0,1:T(1,128)} %param.36) | copy-start | bytes 4036
  760.2 158.5 %copy-start.203 = (f32[1,7,48]{2,0,1:T(1,128)S(1)}, f32[1,7,48]{2,0,1:T(1,128)}, u32[]{:S(2)}) copy-start(f32[1,7,48]{2,0,1:T(1,128)} %param.37) | copy-start | bytes 4036
  760.2 160.4 %copy-start.153 = (f32[15,48]{1,0:T(8,128)S(1)}, f32[15,48]{1,0:T(8,128)}, u32[]{:S(2)}) copy-start(f32[15,48]{1,0:T(8,128)} %param.32) | copy-start | bytes 8644
  760.2 160.4 %copy-start.195 = (f32[15,48]{1,0:T(8,128)S(1)}, f32[15,48]{1,0:T(8,128)}, u32[]{:S(2)}) copy-start(f32[15,48]{1,0:T(8,128)} %param.34) | copy-start | bytes 8644
  760.2 160.4 %copy-start.196 = (f32[15,48]{1,0:T(8,128)S(1)}, f32[15,48]{1,0:T(8,128)}, u32[]{:S(2)}) copy-start(f32[15,48]{1,0:T(8,128)} %param.33) | copy-start | bytes 8644
  760.2 161.0 %copy-start.2 = (f32[1,32,128,128]{3,2,1,0:T(8,128)S(1)}, f32[1,32,128,128]{3,2,1,0:T(8,128)}, u32[]{:S(2)}) copy-start(f32[1,32,128,128]{3,2,1,0:T(8,128)} %param.25) | copy-start | bytes 6291460
  921.3 95.7 %copy-start.1 = (s32[1024]{0:T(1024)S(1)}, s32[1024]{0:T(1024)}, u32[]{:S(2)}) copy-start(s32[1024]{0:T(1024)} %param.23) | copy-start | bytes 12292
  (166 other events, 630.5 us)
Sparse Core Ops, SparseCore 0:
  218.0 22.7 all-reduce.14
  268.8 22.8 all-reduce.28
  369.3 21.7 all-reduce.16
  407.5 20.3 all-reduce.18
  442.2 20.4 all-reduce.20
  494.1 21.5 all-reduce.22
  588.7 24.2 all-reduce.26
  718.1 23.3 all-reduce.24

commit v2 on v1

v2 whole, which is shorter than its diff:
```python
import functools
from functools import partial

import jax
import jax.numpy as jnp
from jax import lax
from jax.experimental import pallas as pl
from jax.experimental.pallas import tpu as pltpu
from jax.sharding import PartitionSpec as P

HD = 64
KEEP = 512
STEP = 10


BETA_ONE = 0.9
BETA_TWO = 0.95
ADAM_EPSILON = 1e-08
MATRIX_RATE = 0.1
VECTOR_RATE = 0.5
WEIGHT_DECAY = 0.01
NORM_EPSILON = 1e-05
TILE = 128
PANEL = 32
ROWS = 256
KEYS = 256
PAIR = 2 * HD
NN = ((1,), (0,))
NT = ((1,), (1,))
F32 = jnp.float32
BF16 = jnp.bfloat16
MESH = pl.DeviceIdType.MESH
ANY = pl.BlockSpec(memory_space=pl.ANY)


def matrix_list(model_width, hidden_width, tensor_count):
    half_width = model_width // tensor_count
    hidden_half = hidden_width // tensor_count
    return [
        ("enc_qkv", model_width, 3 * half_width),
        ("enc_out", half_width, model_width),
        ("enc_up", model_width, hidden_half),
        ("enc_down", hidden_half, model_width),
        ("dec_qkv", model_width, 3 * half_width),
        ("dec_out", half_width, model_width),
        ("crs_q", model_width, half_width),
        ("crs_kv", model_width, 2 * half_width),
        ("crs_out", half_width, model_width),
        ("dec_up", model_width, hidden_half),
        ("dec_down", hidden_half, model_width),
    ]


def halves(x):
    high = x.astype(BF16)
    return high, (x - high.astype(F32)).astype(BF16)


def mm(a, b, dims=NN):
    ah, al = halves(a)
    bh, bl = halves(b)
    return times(jnp.concatenate([ah, ah, al], 1), jnp.concatenate([bh, bl, bh], dims[1][0]), dims)


def chip_grid(device_count):
    if device_count == 16:
        return 4, 2, 2
    side = round(device_count ** (1 / 3))
    if side**3 == device_count:
        return side, side, side
    return 1, 1, device_count


def place(grid):
    zs, ys, xs = grid
    me = lax.axis_index("dp")
    return me // (ys * xs), lax.rem(me // xs, ys), lax.rem(me, xs)


def peers(grid):
    zs, ys, xs = grid
    z, y, x = place(grid)

    def device(zz, yy, xx):
        return {"dp": (zz * ys + yy) * xs + xx}

    return (
        lambda k: device(lax.rem(z + k, zs), y, x),
        lambda k: device(z, lax.rem(y + k, ys), x),
        lambda k: device(z, y, lax.rem(x + k, xs)),
    )


def greet(grid):
    barrier = pltpu.get_barrier_semaphore()
    count = 0
    for size, peer in zip(grid, peers(grid)):
        for k in range(1, size):
            pl.semaphore_signal(barrier, inc=1, device_id=peer(k), device_id_type=MESH)
            count += 1
    pl.semaphore_wait(barrier, count)


def remote(src, dst, send, recv, device):
    return pltpu.make_async_remote_copy(
        src_ref=src, dst_ref=dst, send_sem=send, recv_sem=recv, device_id=device, device_id_type=MESH
    )


def chunking(slots):
    half = slots // 2
    chunks = min(16, half)
    return half, chunks, half // chunks


def owner_kernel(grid, *refs):
    zs, ys, xs = grid
    used_ref, in_ref, small_ref = refs[:3]
    state_in, state_out, small_out_ref, work_out_ref = refs[3:10], refs[10:17], refs[17], refs[18]
    state, rest = refs[19:26], refs[26:]
    (own0, own1, ra0, ra1, rb0, rb1, rc0, rc1, total, rs_z, rs_y, rs_x, work, load_sem,
     as0, as1, ar0, ar1, bs0, bs1, br0, br1, cs0, cs1, cr0, cr1,
     ssz, ssy, ssx, srz, sry, srx, state_sem) = rest
    own, rec_a, rec_b, rec_c = (own0, own1), (ra0, ra1), (rb0, rb1), (rc0, rc1)
    a_send, a_recv, b_send, b_recv, c_send, c_recv = (as0, as1), (ar0, ar1), (bs0, bs1), (br0, br1), (cs0, cs1), (cr0, cr1)
    rec_s, s_send, s_recv = (rs_z, rs_y, rs_x), (ssz, ssy, ssx), (srz, sry, srx)

    z, y, x = place(grid)
    tos = peers(grid)
    to_z, to_y, to_x = tos
    slots = state[0].shape[0]
    half = slots // 2
    first = ((xs, x, to_x), (ys, y, to_y))
    second = ((ys, y, to_y), (xs, x, to_x))

    def source(g, c, other):
        slot = g * half + c
        return in_ref.at[:, :, other, slot] if g == 0 else in_ref.at[:, other, :, slot]

    def load(g, c):
        return pltpu.make_async_copy(source(g, c, first[g][1]), own[g].at[c], load_sem.at[g, c])

    def send_a(g, c, k):
        count, mine, to = first[g]
        return remote(source(g, c, lax.rem(mine + k, count)), rec_a[g].at[c, k - 1],
                      a_send[g].at[c, k - 1], a_recv[g].at[c, k - 1], to(k))

    def send_b(g, c, k):
        count, mine, to = second[g]
        return remote(own[g].at[c, :, lax.rem(mine + k, count)], rec_b[g].at[c, k - 1],
                      b_send[g].at[c, k - 1], b_recv[g].at[c, k - 1], to(k))

    def send_c(g, c, k):
        return remote(own[g].at[c, lax.rem(z + k, zs), second[g][1]], rec_c[g].at[c, k - 1],
                      c_send[g].at[c, k - 1], c_recv[g].at[c, k - 1], to_z(k))

    def start_a(c):
        for g in range(2):
            for k in range(1, first[g][0]):
                send_a(g, c, k).start()

    def send_s(axis, k):
        return remote(total.at[2 - axis], rec_s[axis].at[k - 1],
                      s_send[axis].at[k - 1], s_recv[axis].at[k - 1], tos[axis](k))

    def small_start(axis):
        for k in range(1, grid[axis]):
            send_s(axis, k).start()

    def small_add(axis):
        value = total[2 - axis]
        for k in range(1, grid[axis]):
            send_s(axis, k).wait_recv()
            value += rec_s[axis][k - 1]
        return value

    def each(count, action):
        def go(c, carry):
            action(c)
            return carry

        lax.fori_loop(0, count, go, 0)

    def load_all(c):
        for g in range(2):
            load(g, c).start()

    each(half, load_all)
    for i in range(7):
        pltpu.make_async_copy(state_in[i], state[i], state_sem.at[0, i]).start()
    total[0] = small_ref[...]
    greet(grid)
    small_start(2)
    start_a(0)
    total[1] = small_add(2)
    small_start(1)
    total[2] = small_add(1)
    small_start(0)
    for i in range(7):
        pltpu.make_async_copy(state_in[i], state[i], state_sem.at[0, i]).wait()

    def step_a(c):
        for g in range(2):
            load(g, c).wait()
            for k in range(1, first[g][0]):
                send_a(g, c, k).wait_recv()

        @pl.when(c + 1 < half)
        def _():
            start_a(c + 1)

        for g in range(2):
            n2 = second[g][0]

            def add(e, carry, g=g, n2=n2):
                a, b = e // n2, lax.rem(e, n2)
                value = own[g][c, a, b].astype(F32)
                for k in range(1, first[g][0]):
                    value += rec_a[g][c, k - 1, a, b].astype(F32)
                own[g][c, a, b] = value.astype(BF16)
                return carry

            lax.fori_loop(0, zs * n2, add, 0)
            for k in range(1, n2):
                send_b(g, c, k).start()

    def step_b(c):
        for g in range(2):
            n2, mine = second[g][0], second[g][1]
            for k in range(1, n2):
                send_b(g, c, k).wait_recv()

            def add(a, carry, g=g, n2=n2, mine=mine):
                value = own[g][c, a, mine].astype(F32)
                for k in range(1, n2):
                    value += rec_b[g][c, k - 1, a].astype(F32)
                own[g][c, a, mine] = value.astype(BF16)
                return carry

            lax.fori_loop(0, zs, add, 0)
            for k in range(1, zs):
                send_c(g, c, k).start()

    def step_c(c):
        batch = lax.rem(c // 4, 2)
        for g in range(2):
            for k in range(1, zs):
                send_c(g, c, k).wait_recv()
        for g in range(2):
            value = own[g][c, z, second[g][1]].astype(F32)
            for k in range(1, zs):
                value += rec_c[g][c, k - 1].astype(F32)
            slot = g * half + c
            value = jnp.where(used_ref[slot] > 0, value, 0.0)
            soap_products(value, slot, state, work, batch, 2 * (4 * g + lax.rem(c, 4)))

    def finish(b):
        batch = lax.rem(b, 2)
        place_bases(work, batch, state[5], state[6], 4 * b)
        emit(b)

    def emit(b):
        for g in range(2):
            span = pl.ds(g * half + 4 * b, 4)
            for i in range(7):
                pltpu.make_async_copy(state[i].at[span], state_out[i].at[span], state_sem.at[1, i]).start()

    def round_of(r, carry):
        for s in range(4):
            t = 4 * r + s

            @pl.when(t < half)
            def _(t=t):
                step_a(t)

            @pl.when((t >= 1) & (t <= half))
            def _(t=t):
                step_b(t - 1)

            @pl.when((t >= 2) & (t < half + 2))
            def _(t=t):
                step_c(t - 2)

            if s >= 1:

                @pl.when((r >= 1) & (r < half // 4))
                def _(s=s):
                    b = r - 1
                    for p in ((0,), (1,), (2, 3))[s - 1]:
                        panel_step(work, lax.rem(b, 2), p)
                    if s == 3:
                        finish(b)

        return carry

    lax.fori_loop(0, half // 4 + 1, round_of, 0)
    emit(half // 4 - 1)
    work_out_ref[...] = work[(half // 4 - 1) % 2]
    small_out_ref[...] = small_add(0)
    for axis in range(3):
        for k in range(1, grid[axis]):
            send_s(axis, k).wait_send()

    def end(c):
        for g in range(2):
            for k in range(1, first[g][0]):
                send_a(g, c, k).wait_send()
            for k in range(1, second[g][0]):
                send_b(g, c, k).wait_send()
            for k in range(1, zs):
                send_c(g, c, k).wait_send()

    each(half, end)
    for i in range(7):
        pltpu.make_async_copy(state[i], state_out[i], state_sem.at[1, i]).wait()


def place_bases(work, batch, left_ref, right_ref, at):
    half = left_ref.shape[0] // 2
    for g in range(2):
        for e in range(4):
            left_ref[g * half + at + e] = work[batch, 2 * (4 * g + e), :, TILE:].T
            right_ref[g * half + at + e] = work[batch, 2 * (4 * g + e) + 1, :, TILE:].T


def last_bases_kernel(work_ref, *refs):
    state_in, state_out, state, work, sems = refs[:7], refs[7:14], refs[14:21], refs[21], refs[22]
    half = state[0].shape[0] // 2

    def copy_in(i):
        return pltpu.make_async_copy(state_in[i], state[i], sems.at[0, i])

    def copy_out(i):
        return pltpu.make_async_copy(state[i], state_out[i], sems.at[1, i])

    for i in range(7):
        copy_in(i).start()
    work[0] = work_ref[...]
    panel_step(work, 0, 0)
    for i in range(7):
        copy_in(i).wait()
        if i < 5:
            copy_out(i).start()
    for p in range(1, TILE // PANEL):
        panel_step(work, 0, p)
    place_bases(work, 0, state[5], state[6], half - 4)
    for i in range(5, 7):
        copy_out(i).start()
    for i in range(7):
        copy_out(i).wait()


def last_bases(work, state):
    whole = state[0].shape
    return pl.pallas_call(
        last_bases_kernel,
        out_shape=[jax.ShapeDtypeStruct(whole, F32)] * 7,
        in_specs=[pl.BlockSpec(memory_space=pltpu.VMEM)] + [ANY] * 7,
        out_specs=[ANY] * 7,
        scratch_shapes=[pltpu.VMEM(whole, F32)] * 7
        + [pltpu.VMEM((1,) + work.shape, F32), pltpu.SemaphoreType.DMA((2, 7))],
        compiler_params=pltpu.CompilerParams(vmem_limit_bytes=56 << 20),
        name="last_bases",
    )(work, *state)


def soap_products(g, i, state, work, batch, at):
    w_ref, m_ref, v_ref, l_ref, r_ref, ql_ref, qr_ref = state
    c1 = 1.0 - BETA_ONE**STEP
    c2 = 1.0 - BETA_TWO**STEP
    ql = ql_ref[i]
    qr = qr_ref[i]
    gt = g.T
    nm = BETA_ONE * m_ref[i] + (1.0 - BETA_ONE) * g
    m_ref[i] = nm
    side = mm(jnp.concatenate([g, nm], 0), qr)
    both = mm(ql.T, jnp.concatenate([side[:TILE], side[TILE:]], 1))
    rotated, rotated_first = both[:, :TILE], both[:, TILE:]
    nv = BETA_TWO * v_ref[i] + (1.0 - BETA_TWO) * rotated * rotated
    v_ref[i] = nv
    normed = rotated_first / c1 / (jnp.sqrt(nv / c2) + ADAM_EPSILON)
    step = mm(mm(ql, normed), qr, NT)
    w = w_ref[i]
    w_ref[i] = w - MATRIX_RATE * step - MATRIX_RATE * WEIGHT_DECAY * w
    for k, (ref, turn, left, right) in enumerate(((l_ref, ql, g, gt), (r_ref, qr, gt, g))):
        stat = BETA_TWO * ref[i] + (1.0 - BETA_TWO) * mm(left, right)
        ref[i] = stat
        a = mm(stat, turn)
        at_turned = a.T
        work[batch, at + k, :, :TILE] = mm(at_turned, a)
        work[batch, at + k, :, TILE:] = at_turned


def panel_step(work, batch, p):
    count = work.shape[1]
    per = TILE // (2 * PANEL)
    r0 = p * PANEL
    rows = count // per * 8
    lane = lax.broadcasted_iota(jnp.int32, (rows, TILE), 1)
    start = lane // (2 * PANEL) * (2 * PANEL)
    row = lax.rem(lax.broadcasted_iota(jnp.int32, (rows, TILE), 0), 8)
    sub = lax.broadcasted_iota(jnp.int32, (count // per, 8, TILE), 1)
    eye = (
        lax.broadcasted_iota(jnp.int32, (PANEL, PANEL), 0) == lax.broadcasted_iota(jnp.int32, (PANEL, PANEL), 1)
    ).astype(F32)
    packs = []
    for q in range(count // per):
        pieces = []
        for k in range(per):
            pieces += [work[batch, q * per + k, r0:r0 + PANEL, r0:r0 + PANEL], eye]
        packs.append(jnp.concatenate(pieces, 1)[None])
    x = jnp.concatenate(packs, 0)
    strips = [x[:, 8 * e:8 * e + 8, :] for e in range(PANEL // 8)]

    def segment(strip, index):
        return jnp.take_along_axis(strip.reshape(-1, TILE), index, axis=1).reshape(strip.shape)

    for j in range(0, PANEL, 2):
        e0, here = j // 8, j % 8
        one = [segment(strip, start + j) for strip in strips[e0:]]
        two = [segment(strip, start + j + 1) for strip in strips[e0:]]
        corner = one[0][:, here:here + 1, :]
        side = one[0][:, here + 1:here + 2, :]
        inverse = 1.0 / corner
        inverse_two = corner * (1.0 / (corner * two[0][:, here + 1:here + 2, :] - side * side))
        shift = side * inverse
        ratio = strips[e0][:, here:here + 1, :] * inverse
        next_off = side * ratio
        ratio_two = (strips[e0][:, here + 1:here + 2, :] - next_off) * inverse_two
        ratio_one = ratio - shift * ratio_two
        for e in range(e0, PANEL // 8):
            change = one[e - e0] * ratio_one + two[e - e0] * ratio_two
            if e == e0:
                change = jnp.where(sub > here + 1, change, jnp.where(sub == here + 1, next_off, 0.0))
            strips[e] = strips[e] - change
    for e in range(PANEL // 8):
        strips[e] = strips[e] * lax.rsqrt(segment(strips[e], start + 8 * e + row))
    x = jnp.concatenate(strips, 1)
    for q in range(count // per):
        for k in range(per):
            i = q * per + k
            inverse = x[q, :, 2 * PANEL * k + PANEL:2 * PANEL * (k + 1)]
            u = mm(inverse, work[batch, i, r0:r0 + PANEL, :])
            work[batch, i, r0:r0 + PANEL, TILE:] = u[:, TILE:]
            if r0 + PANEL < TILE:
                high, low = halves(u)
                left = jnp.concatenate([u[:, :TILE], u[:, :TILE], low[:, :TILE].astype(F32)], 0).T
                work[batch, i, r0 + PANEL:, :] -= times(
                    left[r0 + PANEL:, :].astype(BF16), jnp.concatenate([high, low, high], 0)
                )


def some(shape):
    return tuple(max(1, s) for s in shape)


def owner_update(used, slot_grads, small, state, device_count):
    grid = chip_grid(device_count)
    zs, ys, xs = grid
    slots = slot_grads.shape[0] // device_count
    half = slots // 2
    block = (TILE, TILE)
    dma = pltpu.SemaphoreType.DMA
    firsts, seconds = (xs, ys), (ys, xs)
    whole = (slots,) + block
    scratch = (
        [pltpu.VMEM(whole, F32)] * 7
        + [pltpu.VMEM((half, zs, seconds[g]) + block, BF16) for g in range(2)]
        + [pltpu.VMEM(some((half, firsts[g] - 1, zs, seconds[g])) + block, BF16) for g in range(2)]
        + [pltpu.VMEM(some((half, seconds[g] - 1, zs)) + block, BF16) for g in range(2)]
        + [pltpu.VMEM(some((half, zs - 1)) + block, BF16) for g in range(2)]
        + [pltpu.VMEM((3,) + small.shape, F32)]
        + [pltpu.VMEM((max(1, n - 1),) + small.shape, F32) for n in grid]
        + [pltpu.VMEM((2, 16, TILE, 2 * TILE), F32)]
        + [dma((2, half))]
        + [dma(some((half, firsts[g] - 1))) for g in range(2)] * 2
        + [dma(some((half, seconds[g] - 1))) for g in range(2)] * 2
        + [dma(some((half, zs - 1))) for g in range(2)] * 2
        + [dma((max(1, n - 1),)) for n in grid] * 2
        + [dma((2, 7))]
    )
    results = pl.pallas_call(
        functools.partial(owner_kernel, grid),
        out_shape=[jax.ShapeDtypeStruct(whole, F32)] * 7
        + [jax.ShapeDtypeStruct(small.shape, F32), jax.ShapeDtypeStruct((16, TILE, 2 * TILE), F32)],
        in_specs=[pl.BlockSpec(memory_space=pltpu.SMEM), ANY, pl.BlockSpec(memory_space=pltpu.VMEM)] + [ANY] * 7,
        out_specs=[ANY] * 7 + [pl.BlockSpec(memory_space=pltpu.VMEM)] * 2,
        scratch_shapes=scratch,
        compiler_params=pltpu.CompilerParams(collective_id=1, has_side_effects=True, vmem_limit_bytes=56 << 20),
        name="owner_update",
    )(used, slot_grads.reshape(zs, ys, xs, slots, TILE, TILE), small, *state)
    return last_bases(results[8], results[:7]), results[7]


def ag_kernel(grid, own_ref, small_ref, out_ref, small_out_ref,
              load_sem, z_send, z_recv, b_send0, b_send1, b_recv0, b_recv1, a_send0, a_send1, a_recv0, a_recv1,
              s_load, ssz, ssy, ssx, srz, sry, srx):
    zs, ys, xs = grid
    z, y, x = place(grid)
    tos = peers(grid)
    to_z, to_y, to_x = tos
    slots = own_ref.shape[0]
    half, chunks, size = chunking(slots)
    first = ((xs, to_x), (ys, to_y))
    second = ((ys, to_y), (xs, to_x))
    b_send, b_recv, a_send, a_recv = (b_send0, b_send1), (b_recv0, b_recv1), (a_send0, a_send1), (a_recv0, a_recv1)
    s_send, s_recv = (ssz, ssy, ssx), (srz, sry, srx)

    def span(g, c):
        return pl.ds(g * half + c * size, size)

    def send_z(g, c, k):
        return remote(own_ref.at[span(g, c)], out_ref.at[z, y, x, span(g, c)],
                      z_send.at[g, c, k - 1], z_recv.at[g, c, k - 1], to_z(k))

    def send_b(g, c, k):
        part = out_ref.at[:, y, x, span(g, c)]
        return remote(part, part, b_send[g].at[c, k - 1], b_recv[g].at[c, k - 1], second[g][1](k))

    def send_a(g, c, k):
        part = out_ref.at[:, :, x, span(g, c)] if g == 0 else out_ref.at[:, y, :, span(g, c)]
        return remote(part, part, a_send[g].at[c, k - 1], a_recv[g].at[c, k - 1], first[g][1](k))

    def send_s(axis, k):
        if axis == 0:
            source, target = small_ref, small_out_ref.at[z, y, x]
        else:
            source = target = small_out_ref.at[:, y, x] if axis == 1 else small_out_ref.at[:, :, x]
        return remote(source, target, s_send[axis].at[k - 1], s_recv[axis].at[k - 1], tos[axis](k))

    keep = pltpu.make_async_copy(own_ref, out_ref.at[z, y, x], load_sem)
    keep_small = pltpu.make_async_copy(small_ref, small_out_ref.at[z, y, x], s_load)
    keep.start()
    keep_small.start()
    greet(grid)

    for k in range(1, grid[0]):
        send_s(0, k).start()
    def start_z(c):
        for g in range(2):
            for k in range(1, zs):
                send_z(g, c, k).start()

    def small_wait(axis):
        for k in range(1, grid[axis]):
            send_s(axis, k).wait_recv()

    def small_start(axis):
        for k in range(1, grid[axis]):
            send_s(axis, k).start()

    start_z(0)
    for t in range(chunks + 1):
        if t < chunks:
            for g in range(2):
                for k in range(1, zs):
                    send_z(g, t, k).wait_recv()
            if t == 0:
                keep.wait()
                keep_small.wait()
                small_wait(0)
                small_start(1)
            if t + 1 < chunks:
                start_z(t + 1)
            for g in range(2):
                for k in range(1, second[g][0]):
                    send_b(g, t, k).start()
        if t >= 1:
            for g in range(2):
                for k in range(1, second[g][0]):
                    send_b(g, t - 1, k).wait_recv()
                for k in range(1, first[g][0]):
                    send_a(g, t - 1, k).start()
        if t == 1:
            small_wait(1)
            small_start(2)
    small_wait(2)
    for c in range(chunks):
        for g in range(2):
            for k in range(1, first[g][0]):
                send_a(g, c, k).wait_recv()
    for axis in range(3):
        for k in range(1, grid[axis]):
            send_s(axis, k).wait_send()
    for c in range(chunks):
        for g in range(2):
            for k in range(1, zs):
                send_z(g, c, k).wait_send()
            for k in range(1, second[g][0]):
                send_b(g, c, k).wait_send()
            for k in range(1, first[g][0]):
                send_a(g, c, k).wait_send()


def gather_all(own, small, device_count):
    grid = chip_grid(device_count)
    zs, ys, xs = grid
    slots = own.shape[0]
    half, chunks, size = chunking(slots)
    dma = pltpu.SemaphoreType.DMA
    firsts, seconds = (xs, ys), (ys, xs)
    scratch = (
        [dma, dma(some((2, chunks, zs - 1))), dma(some((2, chunks, zs - 1)))]
        + [dma(some((chunks, seconds[g] - 1))) for g in range(2)] * 2
        + [dma(some((chunks, firsts[g] - 1))) for g in range(2)] * 2
        + [dma]
        + [dma((max(1, n - 1),)) for n in grid] * 2
    )
    blocks, smalls = pl.pallas_call(
        functools.partial(ag_kernel, grid),
        out_shape=[jax.ShapeDtypeStruct(grid + own.shape, own.dtype), jax.ShapeDtypeStruct(grid + small.shape, small.dtype)],
        in_specs=[pl.BlockSpec(memory_space=pltpu.VMEM)] * 2,
        out_specs=[ANY, ANY],
        scratch_shapes=scratch,
        compiler_params=pltpu.CompilerParams(collective_id=2, has_side_effects=True),
        name="gather_all",
    )(own, small)
    return blocks.reshape((-1,) + own.shape[1:]), smalls.reshape((-1,) + small.shape)


def unpack_kernel(shapes, slots_ref, packed, *refs):
    count = len(shapes)
    mats, held, sems = refs[:count], refs[count:-1], refs[-1]

    def whole(index):
        return pltpu.make_async_copy(held[index], mats[index], sems.at[1, index])

    offset = 0
    for index, (height, breadth) in enumerate(shapes):
        down, across = height // TILE, breadth // TILE

        def start(i, carry, index=index, offset=offset, across=across):
            for j in range(across):
                tile = held[index].at[pl.ds(pl.multiple_of(i * TILE, TILE), TILE), j * TILE:(j + 1) * TILE]
                slot = packed.at[slots_ref[offset + i * across + j]]
                pltpu.make_async_copy(slot, tile, sems.at[0, index]).start()
            return carry

        lax.fori_loop(0, down, start, 0)
        offset += down * across
    for index in range(count):
        pltpu.make_async_copy(held[index], held[index], sems.at[0, index]).wait()
        whole(index).start()
    for index in range(count):
        whole(index).wait()


def unpack_tiles(packed, slots, shapes):
    return pl.pallas_call(
        functools.partial(unpack_kernel, shapes),
        out_shape=[jax.ShapeDtypeStruct(s, packed.dtype) for s in shapes],
        in_specs=[pl.BlockSpec(memory_space=pltpu.SMEM), ANY],
        out_specs=[ANY] * len(shapes),
        scratch_shapes=[pltpu.VMEM(s, packed.dtype) for s in shapes] + [pltpu.SemaphoreType.DMA((2, len(shapes)))],
        compiler_params=pltpu.CompilerParams(vmem_limit_bytes=56 << 20),
        name="unpack_tiles",
    )(slots, packed)


def weight_grads_kernel(plan, used, vectors, passed, slots_ref, *refs):
    arrays, refs = refs[:used], refs[used:]
    given, refs = refs[:len(vectors)], refs[len(vectors):]
    refs = refs[passed:]
    packed, refs = refs[0], refs[1:]
    if vectors:
        rows_ref, refs = refs[0], refs[1:]
    held, refs = refs[:used], refs[used:]
    turned, refs = refs[0], refs[1:]
    results, sems = refs[:len(plan)], refs[len(plan):]
    load_sem, store_sem = sems

    def load(i):
        return pltpu.make_async_copy(arrays[i], held[i], load_sem.at[i])

    order = []
    for left, tokens, right, *rest in plan:
        for i in (left, right):
            if i not in order:
                order.append(i)
    for i in order:
        load(i).start()
    if vectors:
        width = rows_ref.shape[1]
        rows_ref[...] = jnp.zeros_like(rows_ref)
        for source, (at, pieces) in zip(given, vectors):
            if pieces is None:
                rows_ref[at:at + 3, :] = source[0:3, :]
                continue
            for begin, end in pieces:
                while begin < end:
                    lane = at % width
                    size = min(end - begin, width - lane)
                    rows_ref[at // width:at // width + 1, lane:lane + size] = source[:, begin:begin + size]
                    begin, at = begin + size, at + size
    ready = set()
    last = None
    for index, (left, tokens, right, offset, stride, down, across) in enumerate(plan):
        for i in (left, right):
            if i not in ready:
                ready.add(i)
                load(i).wait()
        height = down * TILE
        if last != (left, tokens):
            for j in range(down):
                turned[j * TILE:(j + 1) * TILE, :tokens] = (
                    held[left][:tokens, j * TILE:(j + 1) * TILE].astype(F32).T.astype(BF16)
                )
            last = (left, tokens)
        result = results[index]
        group = 3 if across % 3 == 0 else 1

        def columns(n, carry, right=right, tokens=tokens, height=height, result=result, offset=offset,
                    stride=stride, down=down, group=group, index=index):
            lanes = pl.ds(pl.multiple_of(n * group * TILE, TILE), group * TILE)
            result[:, lanes] = times(turned[:height, :tokens], held[right][:tokens, lanes]).astype(BF16)

            def send(i, carry):
                for j in range(group):
                    tile = result.at[
                        pl.ds(pl.multiple_of(i * TILE, TILE), TILE),
                        pl.ds(pl.multiple_of((n * group + j) * TILE, TILE), TILE),
                    ]
                    slot = packed.at[slots_ref[offset + i * stride + n * group + j]]
                    pltpu.make_async_copy(tile, slot, store_sem.at[index]).start()
                return carry

            lax.fori_loop(0, down, send, 0)
            return carry

        lax.fori_loop(0, across // group, columns, 0)
    for index in range(len(plan)):
        pltpu.make_async_copy(results[index], results[index], store_sem.at[index]).wait()


def weight_grads(matrices, slots, slot_count, packed=None, vectors=None):
    arrays, plan, results = [], [], []

    def index_of(array):
        for i, other in enumerate(arrays):
            if other is array:
                return i
        arrays.append(array)
        return len(arrays) - 1

    for offset, parts in matrices:
        height = parts[0][0].shape[1]
        stride = sum(right.shape[1] for left, right in parts) // TILE
        for left, right in parts:
            across = right.shape[1] // TILE
            plan.append((index_of(left), right.shape[0], index_of(right), offset, stride, height // TILE, across))
            results.append(pltpu.VMEM((height, right.shape[1]), BF16))
            offset += across
    tall = max(entry[5] for entry in plan) * TILE
    long = max(entry[1] for entry in plan)
    out_shape = [jax.ShapeDtypeStruct((slot_count, TILE, TILE), BF16)]
    given, layout = [], []
    if vectors:
        rows, width, items = vectors
        out_shape.append(jax.ShapeDtypeStruct((rows, width), F32))
        given = [item[0] for item in items]
        layout = [item[1:] for item in items]
    passed = [] if packed is None else [packed]
    return pl.pallas_call(
        functools.partial(weight_grads_kernel, plan, len(arrays), layout, len(passed)),
        out_shape=out_shape,
        in_specs=[pl.BlockSpec(memory_space=pltpu.SMEM)] + [ANY] * len(arrays)
        + [pl.BlockSpec(memory_space=pltpu.VMEM)] * len(given) + [ANY] * len(passed),
        out_specs=[ANY] + [pl.BlockSpec(memory_space=pltpu.VMEM)] * (len(out_shape) - 1),
        scratch_shapes=[pltpu.VMEM(a.shape, a.dtype) for a in arrays] + [pltpu.VMEM((tall, long), BF16)] + results
        + [pltpu.SemaphoreType.DMA((len(arrays),)), pltpu.SemaphoreType.DMA((len(plan),))],
        input_output_aliases={} if packed is None else {1 + len(arrays) + len(given): 0},
        compiler_params=pltpu.CompilerParams(vmem_limit_bytes=56 << 20),
        name="weight_grads",
    )(slots, *arrays, *given, *passed)


VM = pl.BlockSpec(memory_space=pltpu.VMEM)


def times(left, right, dims=NN):
    return lax.dot_general(left, right, (dims, ((), ())), preferred_element_type=F32)


def rows_of(t, size=ROWS):
    return pl.ds(pl.multiple_of(t * size, size), size)


class Swap:
    def __init__(self, out, into, send_sem, recv_sem):
        self.out, self.into, self.send_sem, self.recv_sem = out, into, send_sem, recv_sem

    @staticmethod
    def scratch(tiles, width):
        dma = pltpu.SemaphoreType.DMA((tiles,))
        held = pltpu.VMEM((tiles, ROWS, width), BF16)
        return [held, held, dma, dma]

    @staticmethod
    def greet():
        barrier = pltpu.get_barrier_semaphore()
        other = {"tensor": 1 - lax.axis_index("tensor")}
        pl.semaphore_signal(barrier, inc=1, device_id=other, device_id_type=MESH)
        pl.semaphore_wait(barrier, 1)

    def copy(self, t):
        return pltpu.make_async_remote_copy(
            src_ref=self.out.at[t],
            dst_ref=self.into.at[t],
            send_sem=self.send_sem.at[t],
            recv_sem=self.recv_sem.at[t],
            device_id={"tensor": 1 - lax.axis_index("tensor")},
            device_id_type=MESH,
        )

    def give(self, t, value):
        self.out[t] = value.astype(BF16)
        self.copy(t).start()

    def take(self, t):
        self.copy(t).wait()
        return self.out[t].astype(F32) + self.into[t].astype(F32)


class Rows:
    def __init__(self, ref, rows):
        self.ref, self.rows = ref, rows

    def __getitem__(self, index):
        at = self.rows[index[0].start]
        return self.ref[at:at + 1, :]


def bias_places(half, hidden_half):
    places, at = {}, 0
    for name, length in (
        ("enc_q", half), ("enc_v", half), ("enc_up", hidden_half), ("dec_q", half), ("dec_v", half),
        ("crs_q", half), ("crs_v", half), ("dec_up", hidden_half),
    ):
        places[name] = slice(at, at + length)
        at += length
    return places


def bias_row(split_ref, places, names, half):
    zero = jnp.zeros((1, half), F32)
    return jnp.concatenate([zero if name is None else split_ref[:, places[name]] for name in names], 1)


def standardize(values):
    center = values - jnp.mean(values, -1, keepdims=True)
    scale = lax.rsqrt(jnp.mean(center * center, -1, keepdims=True) + NORM_EPSILON)
    return center * scale, scale


def norm_back(grad, unit, scale, gain):
    inner = grad * gain
    return scale * (
        inner - jnp.mean(inner, -1, keepdims=True) - unit * jnp.mean(inner * unit, -1, keepdims=True)
    )


def add_sums(sums_ref, grad_in, grad_out, unit):
    sums_ref[0:1, :] += jnp.sum(grad_in, 0, keepdims=True)
    sums_ref[1:2, :] += jnp.sum(grad_out * unit, 0, keepdims=True)
    sums_ref[2:3, :] += jnp.sum(grad_out, 0, keepdims=True)


def head_mask(shape):
    return lax.broadcasted_iota(jnp.int32, shape, 1) < HD


def attend(query_ref, key_ref, value_ref, attended_ref, totals_ref, score_ref, turned_ref, causal, span):
    queries, keys = query_ref.shape[0], key_ref.shape[0]
    pairs = query_ref.shape[1] // PAIR
    chunks = keys // KEYS
    for j in range(pairs):
        turned_ref[j * PAIR:(j + 1) * PAIR, :] = (
            value_ref[:, j * PAIR:(j + 1) * PAIR].astype(F32).T.astype(BF16)
        )
    for i in range(queries // span):
        mine = slice(i * span, (i + 1) * span)

        def pair(j, carry, i=i, mine=mine):
            lanes = pl.ds(pl.multiple_of(j * PAIR, PAIR), PAIR)
            query = query_ref[mine, lanes] * jnp.asarray(HD**-0.5, BF16)
            first = head_mask(query.shape)
            parts = []
            for h in range(2):
                masked = jnp.where(first if h == 0 else ~first, query, jnp.zeros_like(query))
                top = jnp.full((1, span), -jnp.inf, F32)
                for c in range(chunks):
                    if causal and c * KEYS >= (i + 1) * span:
                        continue
                    scores = times(key_ref[c * KEYS:(c + 1) * KEYS, lanes], masked, NT)
                    if causal and (c + 1) * KEYS > i * span:
                        key_at = c * KEYS + lax.broadcasted_iota(jnp.int32, scores.shape, 0)
                        query_at = i * span + lax.broadcasted_iota(jnp.int32, scores.shape, 1)
                        scores = jnp.where(key_at <= query_at, scores, -1000000000.0)
                    score_ref[h, c * KEYS:(c + 1) * KEYS, :] = scores
                    top = jnp.maximum(top, jnp.max(scores, 0, keepdims=True))
                total = jnp.zeros((1, span), F32)
                mixed = jnp.zeros((HD, span), F32)
                value_rows = pl.ds(pl.multiple_of(j * PAIR + h * HD, HD), HD)
                for c in range(chunks):
                    if causal and c * KEYS >= (i + 1) * span:
                        continue
                    probs = jnp.exp(score_ref[h, c * KEYS:(c + 1) * KEYS, :] - top)
                    total += jnp.sum(probs, 0, keepdims=True)
                    mixed += times(turned_ref[value_rows, c * KEYS:(c + 1) * KEYS], probs.astype(BF16))
                parts.append(mixed * (1.0 / total))
                totals_ref[pl.ds(2 * j + h, 1), mine] = top + jnp.log(total)
            attended_ref[mine, lanes] = jnp.concatenate(parts, 0).T.astype(BF16)
            return carry

        lax.fori_loop(0, pairs, pair, 0)


def attend_back(
    query_ref, key_ref, value_ref, attended_ref, totals_ref, grad_ref,
    grad_query_ref, grad_key_ref, grad_value_ref, turned_ref, causal,
):
    queries, keys = grad_ref.shape[0], key_ref.shape[0]
    pairs = query_ref.shape[1] // PAIR
    chunks = keys // KEYS
    scale = HD**-0.5
    for j in range(pairs):
        turned_ref[j * PAIR:(j + 1) * PAIR, :] = (
            key_ref[:, j * PAIR:(j + 1) * PAIR].astype(F32).T.astype(BF16)
        )

    def pair(j, carry):
        lanes = pl.ds(pl.multiple_of(j * PAIR, PAIR), PAIR)
        query = query_ref[:queries, lanes] * jnp.asarray(scale, BF16)
        grad = grad_ref[:, lanes]
        first = head_mask(query.shape)
        meet = (grad.astype(F32) * attended_ref[:queries, lanes].astype(F32)).T
        masked, grads, deltas, totals = [], [], [], []
        for h in range(2):
            keep = first if h == 0 else ~first
            masked.append(jnp.where(keep, query, jnp.zeros_like(query)))
            grads.append(jnp.where(keep, grad, jnp.zeros_like(grad)))
            deltas.append(jnp.sum(meet[h * HD:(h + 1) * HD], 0, keepdims=True))
            totals.append(totals_ref[pl.ds(2 * j + h, 1), :queries])
        grad_query = [jnp.zeros((HD, queries), F32) for h in range(2)]
        for c in range(chunks):
            some = slice(c * KEYS, (c + 1) * KEYS)
            low = c * KEYS if causal else 0
            grad_key = grad_value = jnp.zeros((KEYS, PAIR), F32)
            for h in range(2):
                scores = times(key_ref[some, lanes], masked[h][low:], NT)
                if causal:
                    key_at = lax.broadcasted_iota(jnp.int32, scores.shape, 0)
                    query_at = lax.broadcasted_iota(jnp.int32, scores.shape, 1)
                    scores = jnp.where(key_at <= query_at, scores, -1000000000.0)
                probs = jnp.exp(scores - totals[h][:, low:])
                grad_probs = times(value_ref[some, lanes], grads[h][low:], NT)
                grad_scores = (probs * (grad_probs - deltas[h][:, low:])).astype(BF16)
                grad_value += times(probs.astype(BF16), grads[h][low:])
                grad_key += times(grad_scores, masked[h][low:])
                key_rows = pl.ds(pl.multiple_of(j * PAIR + h * HD, HD), HD)
                part = times(turned_ref[key_rows, some], grad_scores)
                if low:
                    part = jnp.concatenate([jnp.zeros((HD, low), F32), part], 1)
                grad_query[h] += part
            grad_key_ref[some, lanes] = grad_key.astype(BF16)
            grad_value_ref[some, lanes] = grad_value.astype(BF16)
        grad_query_ref[:, lanes] = (jnp.concatenate(grad_query, 0) * scale).T.astype(BF16)
        return carry

    lax.fori_loop(0, pairs, pair, 0)


def self_forward_kernel(
    causal, span, x_ref, wide_ref, out_weight_ref, bias_ref, vec_ref,
    mixed_ref, attended_ref, totals_ref, unit_ref, scale_ref,
    score_ref, turned_ref, *swap_refs,
):
    swap = Swap(*swap_refs)
    length, width = x_ref.shape
    half = out_weight_ref.shape[0]
    tiles = length // ROWS
    totals_ref[...] = jnp.zeros_like(totals_ref)

    def mix(t, carry):
        mixed_ref[rows_of(t), :] = (times(x_ref[rows_of(t), :], wide_ref[...]) + bias_ref[...]).astype(BF16)
        return carry

    lax.fori_loop(0, tiles, mix, 0)
    attend(
        mixed_ref.at[:, :half], mixed_ref.at[:, half:2 * half], mixed_ref.at[:, 2 * half:],
        attended_ref, totals_ref, score_ref, turned_ref, causal, span,
    )

    def give(t, carry):
        swap.give(t, times(attended_ref[rows_of(t), :], out_weight_ref[...]))
        return carry

    lax.fori_loop(0, tiles, give, 0)

    def take(t, carry):
        rows = rows_of(t)
        unit, scale = standardize(x_ref[rows, :].astype(F32) + swap.take(t) + vec_ref[0:1, :])
        unit_ref[rows, :] = unit
        scale_ref[rows, :] = scale
        return carry

    lax.fori_loop(0, tiles, take, 0)


def shape(*dims, dtype=F32):
    return jax.ShapeDtypeStruct(dims, dtype)


def params(ident, mib=56):
    return pltpu.CompilerParams(collective_id=ident, has_side_effects=True, vmem_limit_bytes=mib << 20)


def cross_forward_kernel(
    span, unit_ref, fetched_ref, query_weight_ref, wide_ref, out_weight_ref, query_bias_ref, bias_ref, vec_ref,
    low_ref, query_ref, mixed_ref, attended_ref, totals_ref, unit_out_ref, scale_ref,
    score_ref, turned_ref, *swap_refs,
):
    swap = Swap(*swap_refs)
    length, width = unit_ref.shape
    half = out_weight_ref.shape[0]
    tiles = length // ROWS
    totals_ref[...] = jnp.zeros_like(totals_ref)

    def ask(t, carry):
        rows = rows_of(t)
        low = (unit_ref[rows, :] * vec_ref[0:1, :] + vec_ref[1:2, :]).astype(BF16)
        low_ref[rows, :] = low
        query_ref[rows, :] = (times(low, query_weight_ref[...]) + query_bias_ref[...]).astype(BF16)
        return carry

    lax.fori_loop(0, tiles, ask, 0)

    def mix(t, carry):
        mixed_ref[rows_of(t), :] = (
            times(fetched_ref[rows_of(t), :], wide_ref[...]) + bias_ref[...]
        ).astype(BF16)
        return carry

    lax.fori_loop(0, fetched_ref.shape[0] // ROWS, mix, 0)
    attend(
        query_ref, mixed_ref.at[:, :half], mixed_ref.at[:, half:],
        attended_ref, totals_ref, score_ref, turned_ref, False, span,
    )

    def give(t, carry):
        swap.give(t, times(attended_ref[rows_of(t), :], out_weight_ref[...]))
        return carry

    lax.fori_loop(0, tiles, give, 0)

    def take(t, carry):
        rows = rows_of(t)
        hidden = unit_ref[rows, :] * vec_ref[0:1, :] + vec_ref[1:2, :]
        unit, scale = standardize(hidden + swap.take(t) + vec_ref[2:3, :])
        unit_out_ref[rows, :] = unit
        scale_ref[rows, :] = scale
        return carry

    lax.fori_loop(0, tiles, take, 0)


def feed_forward_kernel(
    kept, unit_ref, up_ref, down_ref, bias_ref, vec_ref,
    states_ref, states_low_ref, low_ref, active_ref, slope_ref, unit_out_ref, scale_ref, *swap_refs,
):
    swap = Swap(*swap_refs)
    length, width = unit_ref.shape
    hidden_half = up_ref.shape[1]
    tiles, kept_tiles = length // ROWS, kept // ROWS
    step = 512

    def feed(t, carry, keep):
        rows = rows_of(t)
        low = (unit_ref[rows, :] * vec_ref[0:1, :] + vec_ref[1:2, :]).astype(BF16)
        if keep:
            low_ref[rows, :] = low
        total = jnp.zeros((ROWS, width), F32)
        for c in range(0, hidden_half, step):
            upward = times(low, up_ref[:, c:c + step]) + bias_ref[:, c:c + step]
            below = 0.5 * lax.erf(upward * (0.5**0.5)) + 0.5
            active = (upward * below).astype(BF16)
            if keep:
                active_ref[rows, c:c + step] = active
                bell = jnp.exp(-0.5 * upward * upward) * (0.5 / jnp.pi) ** 0.5
                slope_ref[rows, c:c + step] = (below + upward * bell).astype(BF16)
            total += times(active, down_ref[c:c + step, :])
        swap.give(t, total)
        return carry

    lax.fori_loop(0, kept_tiles, functools.partial(feed, keep=True), 0)
    if kept_tiles < tiles:
        lax.fori_loop(kept_tiles, tiles, functools.partial(feed, keep=False), 0)

    def take(t, carry, keep):
        rows = rows_of(t)
        hidden = unit_ref[rows, :] * vec_ref[0:1, :] + vec_ref[1:2, :]
        unit, scale = standardize(hidden + swap.take(t) + vec_ref[2:3, :])
        states = unit * vec_ref[3:4, :] + vec_ref[4:5, :]
        states_ref[rows, :] = states
        if keep:
            states_low_ref[rows, :] = states.astype(BF16)
            unit_out_ref[rows, :] = unit
            scale_ref[rows, :] = scale
        return carry

    lax.fori_loop(0, kept_tiles, functools.partial(take, keep=True), 0)
    if kept_tiles < tiles:
        lax.fori_loop(kept_tiles, tiles, functools.partial(take, keep=False), 0)


def feed_backward_kernel(
    grad_ref, unit_after_ref, scale_after_ref, active_ref, slope_ref, up_ref, down_ref,
    unit_before_ref, scale_before_ref, vec_ref,
    low_ref, grad_up_ref, bias_ref, grad_out_ref, sums_after_ref, sums_before_ref,
    held_ref, *swap_refs,
):
    swap = Swap(*swap_refs)
    length, width = grad_ref.shape
    hidden_half = up_ref.shape[1]
    tiles = length // ROWS
    step = 512
    sums_after_ref[...] = jnp.zeros_like(sums_after_ref)
    sums_before_ref[...] = jnp.zeros_like(sums_before_ref)
    bias_ref[...] = jnp.zeros_like(bias_ref)

    def give(t, carry):
        rows = rows_of(t)
        grad = grad_ref[rows, :].astype(F32)
        unit = unit_after_ref[rows, :]
        inner = norm_back(grad, unit, scale_after_ref[rows, :], vec_ref[0:1, :])
        add_sums(sums_after_ref, inner, grad, unit)
        held_ref[rows, :] = inner
        low = inner.astype(BF16)
        low_ref[rows, :] = low
        total = jnp.zeros((ROWS, width), F32)
        for c in range(0, hidden_half, step):
            grad_active = times(low, down_ref[c:c + step, :], NT)
            grad_up = (grad_active * slope_ref[rows, c:c + step].astype(F32)).astype(BF16)
            grad_up_ref[rows, c:c + step] = grad_up
            bias_ref[:, c:c + step] += jnp.sum(grad_up.astype(F32), 0, keepdims=True)
            total += times(grad_up, up_ref[:, c:c + step], NT)
        swap.give(t, total)
        return carry

    lax.fori_loop(0, tiles, give, 0)

    def take(t, carry):
        rows = rows_of(t)
        grad = held_ref[rows, :] + swap.take(t)
        unit = unit_before_ref[rows, :]
        inner = norm_back(grad, unit, scale_before_ref[rows, :], vec_ref[1:2, :])
        add_sums(sums_before_ref, inner, grad, unit)
        grad_out_ref[rows, :] = inner
        return carry

    lax.fori_loop(0, tiles, take, 0)


def spread(grad_pre_ref, out_weight_ref, low_ref, grad_ref):
    def one(t, carry):
        rows = rows_of(t)
        low = grad_pre_ref[rows, :].astype(BF16)
        low_ref[rows, :] = low
        grad_ref[rows, :] = times(low, out_weight_ref[...], NT).astype(BF16)
        return carry

    lax.fori_loop(0, grad_pre_ref.shape[0] // ROWS, one, 0)


def self_backward_kernel(
    causal, grad_pre_ref, mixed_ref, attended_ref, totals_ref, wide_ref, out_weight_ref,
    low_ref, grad_query_ref, grad_pair_ref, grad_x_ref, sums_ref,
    grad_ref, turned_ref, *swap_refs,
):
    swap = Swap(*swap_refs)
    queries, width = grad_pre_ref.shape
    half = out_weight_ref.shape[0]
    length = mixed_ref.shape[0]
    spread(grad_pre_ref, out_weight_ref, low_ref, grad_ref)
    attend_back(
        mixed_ref.at[:, :half], mixed_ref.at[:, half:2 * half], mixed_ref.at[:, 2 * half:],
        attended_ref, totals_ref, grad_ref,
        grad_query_ref, grad_pair_ref.at[:, :half], grad_pair_ref.at[:, half:], turned_ref, causal,
    )
    sums_ref[...] = jnp.zeros_like(sums_ref)
    first = queries // ROWS

    def give(t, carry, asked):
        rows = rows_of(t)
        pair = grad_pair_ref[rows, :]
        sums_ref[:, half:] += jnp.sum(pair.astype(F32), 0, keepdims=True)
        total = times(pair, wide_ref[:, half:], NT)
        if asked:
            query = grad_query_ref[rows, :]
            sums_ref[:, :half] += jnp.sum(query.astype(F32), 0, keepdims=True)
            total += times(query, wide_ref[:, :half], NT)
        swap.give(t, total)
        return carry

    lax.fori_loop(0, first, functools.partial(give, asked=True), 0)
    if first < length // ROWS:
        lax.fori_loop(first, length // ROWS, functools.partial(give, asked=False), 0)

    def take(t, carry, asked):
        rows = rows_of(t)
        total = swap.take(t)
        grad_x_ref[rows, :] = grad_pre_ref[rows, :] + total if asked else total
        return carry

    lax.fori_loop(0, first, functools.partial(take, asked=True), 0)
    if first < length // ROWS:
        lax.fori_loop(first, length // ROWS, functools.partial(take, asked=False), 0)


def cross_backward_kernel(
    grad_pre_ref, query_ref, mixed_ref, attended_ref, totals_ref, query_weight_ref, wide_ref, out_weight_ref,
    unit_ref, scale_ref, vec_ref,
    low_ref, grad_query_ref, grad_pair_ref, fetched_ref, grad_out_ref, sums_ref, vec_sums_ref,
    grad_ref, turned_ref, *swap_refs,
):
    near, far = Swap(*swap_refs[:4]), Swap(*swap_refs[4:])
    queries, width = grad_pre_ref.shape
    half = out_weight_ref.shape[0]
    keys = mixed_ref.shape[0]
    spread(grad_pre_ref, out_weight_ref, low_ref, grad_ref)
    attend_back(
        query_ref, mixed_ref.at[:, :half], mixed_ref.at[:, half:],
        attended_ref, totals_ref, grad_ref,
        grad_query_ref, grad_pair_ref.at[:, :half], grad_pair_ref.at[:, half:], turned_ref, False,
    )
    sums_ref[...] = jnp.zeros_like(sums_ref)
    vec_sums_ref[...] = jnp.zeros_like(vec_sums_ref)

    def give_far(t, carry):
        pair = grad_pair_ref[rows_of(t), :]
        sums_ref[:, half:] += jnp.sum(pair.astype(F32), 0, keepdims=True)
        far.give(t, times(pair, wide_ref[...], NT))
        return carry

    lax.fori_loop(0, keys // ROWS, give_far, 0)

    def give_near(t, carry):
        query = grad_query_ref[rows_of(t), :]
        sums_ref[:, :half] += jnp.sum(query.astype(F32), 0, keepdims=True)
        near.give(t, times(query, query_weight_ref[...], NT))
        return carry

    lax.fori_loop(0, queries // ROWS, give_near, 0)

    def take_far(t, carry):
        fetched_ref[rows_of(t), :] = far.take(t).astype(BF16)
        return carry

    lax.fori_loop(0, keys // ROWS, take_far, 0)

    def take_near(t, carry):
        rows = rows_of(t)
        grad = grad_pre_ref[rows, :] + near.take(t)
        unit = unit_ref[rows, :]
        inner = norm_back(grad, unit, scale_ref[rows, :], vec_ref[0:1, :])
        add_sums(vec_sums_ref, inner, grad, unit)
        grad_out_ref[rows, :] = inner
        return carry

    lax.fori_loop(0, queries // ROWS, take_near, 0)


def call(name, ident, body, inputs, outputs, scratch):
    return pl.pallas_call(
        body,
        out_shape=outputs,
        in_specs=[VM] * len(inputs),
        out_specs=[VM] * len(outputs),
        scratch_shapes=scratch,
        compiler_params=params(ident),
        name=name,
    )(*inputs)


def held(*dims, dtype=F32):
    return pltpu.VMEM(dims, dtype)


def encoder_forward(ident, x, wide, out_weight, up, down, shared, split, kept):
    length, width = x.shape
    half, hidden_half = out_weight.shape[0], up.shape[1]
    tiles, span = length // ROWS, min(length, 512)
    places = bias_places(half, hidden_half)

    def body(x_ref, wide_ref, out_weight_ref, up_ref, down_ref, shared_ref, split_ref, *refs):
        saved, fed, rest = refs[:5], refs[5:12], refs[12:]
        Swap.greet()
        self_forward_kernel(
            False, span, x_ref, wide_ref, out_weight_ref,
            bias_row(split_ref, places, ("enc_q", None, "enc_v"), half), Rows(shared_ref, (0,)),
            *saved, *rest[:6],
        )
        feed_forward_kernel(
            kept, saved[3], up_ref, down_ref, split_ref.at[:, places["enc_up"]],
            Rows(shared_ref, (1, 2, 3, 4, 5)), *fed, *rest[6:],
        )

    return call(
        "encoder_forward", ident, body, [x, wide, out_weight, up, down, shared, split],
        [
            shape(length, 3 * half, dtype=BF16), shape(length, half, dtype=BF16), shape(8, length),
            shape(length, width), shape(length, 1),
            shape(length, width), shape(kept, width, dtype=BF16), shape(kept, width, dtype=BF16),
            shape(kept, hidden_half, dtype=BF16), shape(kept, hidden_half, dtype=BF16),
            shape(kept, width), shape(kept, 1),
        ],
        [held(2, length, span), held(half, length, dtype=BF16)] + Swap.scratch(tiles, width) * 2,
    )


def decoder_self_forward(ident, x, wide, out_weight, shared, split, hidden_half):
    length, width = x.shape
    half = out_weight.shape[0]
    span = min(length, 512)
    places = bias_places(half, hidden_half)

    def body(x_ref, wide_ref, out_weight_ref, shared_ref, split_ref, *refs):
        Swap.greet()
        self_forward_kernel(
            True, span, x_ref, wide_ref, out_weight_ref,
            bias_row(split_ref, places, ("dec_q", None, "dec_v"), half), Rows(shared_ref, (6,)), *refs,
        )

    return call(
        "decoder_self_forward", ident, body, [x, wide, out_weight, shared, split],
        [
            shape(length, 3 * half, dtype=BF16), shape(length, half, dtype=BF16), shape(8, length),
            shape(length, width), shape(length, 1),
        ],
        [held(2, length, span), held(half, length, dtype=BF16)] + Swap.scratch(length // ROWS, width),
    )


def decoder_core(
    ident, unit, scale, fetched, cotangent, query_weight, wide, out_weight, up, down, shared, split
):
    length, width = unit.shape
    keys = fetched.shape[0]
    half, hidden_half = out_weight.shape[0], up.shape[1]
    tiles, span = length // ROWS, min(length, 512)
    places = bias_places(half, hidden_half)

    def body(
        unit_ref, scale_ref, fetched_ref, cotangent_ref, query_weight_ref, wide_ref, out_weight_ref,
        up_ref, down_ref, shared_ref, split_ref,
        states_ref, low_ref, attended_ref, second_low_ref, active_ref,
        feed_low_ref, grad_up_ref, up_bias_ref, sums_after_ref, sums_before_ref,
        cross_low_ref, grad_query_ref, grad_pair_ref, returned_ref, grad_out_ref, cross_sums_ref, vec_sums_ref,
        query_ref, mixed_ref, totals_ref, unit_four_ref, scale_four_ref, states_low_ref, slope_ref,
        unit_five_ref, scale_five_ref, grad_four_ref, inner_ref, score_ref, turned_ref, grad_ref, *swaps,
    ):
        Swap.greet()
        cross_forward_kernel(
            span, unit_ref, fetched_ref, query_weight_ref, wide_ref, out_weight_ref,
            split_ref.at[:, places["crs_q"]], bias_row(split_ref, places, (None, "crs_v"), half),
            Rows(shared_ref, (7, 8, 9)),
            low_ref, query_ref, mixed_ref, attended_ref, totals_ref, unit_four_ref, scale_four_ref,
            score_ref, turned_ref, *swaps[:4],
        )
        feed_forward_kernel(
            length, unit_four_ref, up_ref, down_ref, split_ref.at[:, places["dec_up"]],
            Rows(shared_ref, (10, 11, 12, 13, 14)),
            states_ref, states_low_ref, second_low_ref, active_ref, slope_ref, unit_five_ref, scale_five_ref,
            *swaps[4:8],
        )
        feed_backward_kernel(
            cotangent_ref, unit_five_ref, scale_five_ref, active_ref, slope_ref, up_ref, down_ref,
            unit_four_ref, scale_four_ref, Rows(shared_ref, (13, 10)),
            feed_low_ref, grad_up_ref, up_bias_ref, grad_four_ref, sums_after_ref, sums_before_ref,
            inner_ref, *swaps[8:12],
        )
        cross_backward_kernel(
            grad_four_ref, query_ref, mixed_ref, attended_ref, totals_ref, query_weight_ref, wide_ref,
            out_weight_ref, unit_ref, scale_ref, Rows(shared_ref, (7,)),
            cross_low_ref, grad_query_ref, grad_pair_ref, returned_ref, grad_out_ref, cross_sums_ref, vec_sums_ref,
            grad_ref, turned_ref, *swaps[12:],
        )

    return call(
        "decoder_core", ident, body,
        [unit, scale, fetched, cotangent, query_weight, wide, out_weight, up, down, shared, split],
        [
            shape(length, width), shape(length, width, dtype=BF16), shape(length, half, dtype=BF16),
            shape(length, width, dtype=BF16), shape(length, hidden_half, dtype=BF16),
            shape(length, width, dtype=BF16), shape(length, hidden_half, dtype=BF16), shape(1, hidden_half),
            shape(8, width), shape(8, width),
            shape(length, width, dtype=BF16), shape(length, half, dtype=BF16), shape(keys, 2 * half, dtype=BF16),
            shape(keys, width, dtype=BF16), shape(length, width), shape(1, 3 * half), shape(8, width),
        ],
        [
            held(length, half, dtype=BF16), held(keys, 2 * half, dtype=BF16), held(8, length),
            held(length, width), held(length, 1), held(length, width, dtype=BF16),
            held(length, hidden_half, dtype=BF16), held(length, width), held(length, 1),
            held(length, width), held(length, width), held(2, keys, span), held(half, keys, dtype=BF16),
            held(length, half, dtype=BF16),
        ]
        + Swap.scratch(tiles, width) * 4 + Swap.scratch(keys // ROWS, width),
    )


def decoder_self_backward(ident, grad_pre, mixed, attended, totals, wide, out_weight):
    queries, width = grad_pre.shape
    length, half = mixed.shape[0], out_weight.shape[0]

    def body(*refs):
        Swap.greet()
        self_backward_kernel(True, *refs)

    return call(
        "decoder_self_backward", ident, body, [grad_pre, mixed, attended, totals, wide, out_weight],
        [
            shape(queries, width, dtype=BF16), shape(queries, half, dtype=BF16), shape(length, 2 * half, dtype=BF16),
            shape(length, width), shape(1, 3 * half),
        ],
        [held(queries, half, dtype=BF16), held(half, length, dtype=BF16)] + Swap.scratch(length // ROWS, width),
    )


def encoder_backward(
    ident, grad, unit_two, scale_two, active, slope, up, down, unit_one, scale_one,
    mixed, attended, totals, wide, out_weight, shared,
):
    queries, width = grad.shape
    length, half, hidden_half = mixed.shape[0], out_weight.shape[0], up.shape[1]

    def body(
        grad_ref, unit_two_ref, scale_two_ref, active_ref, slope_ref, up_ref, down_ref, unit_one_ref, scale_one_ref,
        mixed_ref, attended_ref, totals_ref, wide_ref, out_weight_ref, shared_ref,
        feed_low_ref, grad_up_ref, up_bias_ref, sums_after_ref, sums_before_ref,
        low_ref, grad_query_ref, grad_pair_ref, grad_x_ref, sums_ref,
        grad_one_ref, inner_ref, grad_out_ref, turned_ref, *swaps,
    ):
        Swap.greet()
        feed_backward_kernel(
            grad_ref, unit_two_ref, scale_two_ref, active_ref, slope_ref, up_ref, down_ref,
            unit_one_ref, scale_one_ref, Rows(shared_ref, (4, 1)),
            feed_low_ref, grad_up_ref, up_bias_ref, grad_one_ref, sums_after_ref, sums_before_ref,
            inner_ref, *swaps[:4],
        )
        self_backward_kernel(
            False, grad_one_ref, mixed_ref, attended_ref, totals_ref, wide_ref, out_weight_ref,
            low_ref, grad_query_ref, grad_pair_ref, grad_x_ref, sums_ref, grad_out_ref, turned_ref, *swaps[4:],
        )

    return call(
        "encoder_backward", ident, body,
        [
            grad, unit_two, scale_two, active, slope, up, down, unit_one, scale_one,
            mixed, attended, totals, wide, out_weight, shared,
        ],
        [
            shape(queries, width, dtype=BF16), shape(queries, hidden_half, dtype=BF16), shape(1, hidden_half),
            shape(8, width), shape(8, width),
            shape(queries, width, dtype=BF16), shape(queries, half, dtype=BF16), shape(length, 2 * half, dtype=BF16),
            shape(length, width), shape(1, 3 * half),
        ],
        [
            held(queries, width), held(queries, width), held(queries, half, dtype=BF16),
            held(half, length, dtype=BF16),
        ]
        + Swap.scratch(queries // ROWS, width) + Swap.scratch(length // ROWS, width),
    )


def adam_vector(grad_value, value, first, second):
    new_first = BETA_ONE * first + (1.0 - BETA_ONE) * grad_value
    new_second = BETA_TWO * second + (1.0 - BETA_TWO) * grad_value * grad_value
    correct_one = 1.0 - BETA_ONE**STEP
    correct_two = 1.0 - BETA_TWO**STEP
    updated = value - VECTOR_RATE * (new_first / correct_one) / (
        jnp.sqrt(new_second / correct_two) + ADAM_EPSILON
    )
    return (new_first, new_second, updated)


def local(
    source_tokens,
    target_tokens,
    target_cotangent,
    retrieved,
    kept_mask,
    owner_slots,
    master,
    first_moment,
    second_moment,
    left_stats,
    right_stats,
    left_basis,
    right_basis,
    shared_vectors,
    shared_first,
    shared_second,
    split_vectors,
    split_first,
    split_second,
):
    tensor_count = lax.axis_size("tensor")
    device_count = lax.axis_size("dp")
    model_width = source_tokens.shape[1]
    tile_size = master.shape[2]
    hidden_width = (split_vectors.shape[1] - 3) * model_width
    half_width = model_width // tensor_count
    hidden_half = hidden_width // tensor_count
    qblocks = retrieved.shape[0]
    per_owner = retrieved.shape[1] // device_count
    me = lax.axis_index("dp")
    vectors = jnp.concatenate([shared_vectors, split_vectors[0]], 0)
    vector_count, vector_width = vectors.shape
    padded = -(-vector_count // 8) * 8
    small = jnp.concatenate(
        [
            jnp.pad(vectors, ((0, padded - vector_count), (0, TILE - vector_width))),
            retrieved.astype(jnp.float32).reshape(-1, TILE),
        ],
        0,
    )
    gathered, smalls = gather_all(master[0].astype(jnp.bfloat16), small, device_count)
    whole = (
        smalls[:, :vector_count, :vector_width]
        .transpose(1, 0, 2)
        .reshape(vector_count, model_width)
        .astype(jnp.bfloat16)
    )
    shared_count = shared_vectors.shape[0]
    shared_whole, split_whole = whole[:shared_count], whole[shared_count:]
    shapes = [s[1:] for s in matrix_list(model_width, hidden_width, tensor_count)]
    names = [s[0] for s in matrix_list(model_width, hidden_width, tensor_count)]
    weights = dict(zip(names, unpack_tiles(gathered, owner_slots, shapes)))
    shared = jnp.pad(shared_whole.astype(F32), ((0, 16 - shared_count), (0, 0)))
    split = split_whole.astype(F32).reshape(1, -1)
    start_row = jnp.argmax(kept_mask)
    turned = jnp.roll(source_tokens, -start_row, 0)

    (enc_mixed, enc_attended, enc_totals, unit_one, scale_one,
     states, stored, hidden_low, enc_active, enc_slope, unit_two, scale_two) = encoder_forward(
        10, turned, weights["enc_qkv"], weights["enc_out"], weights["enc_up"], weights["enc_down"],
        shared, split, KEEP,
    )
    encoder_states = jnp.roll(states, start_row, 0)

    wanted = (
        smalls[:, padded:].reshape(device_count, qblocks, device_count, per_owner)[:, :, me]
        .transpose(1, 0, 2)
        .astype(jnp.int32)
        - KEEP * me
    ).reshape(1, -1)
    matches = (wanted == lax.broadcasted_iota(jnp.int32, (KEEP, 1), 0)).astype(BF16)
    served = jnp.einsum("ka,kb->ab", matches, stored, preferred_element_type=F32).astype(BF16)
    fetched = lax.all_to_all(
        served.reshape(qblocks, device_count, per_owner, model_width),
        "dp", split_axis=1, concat_axis=1, tiled=True,
    ).reshape(-1, model_width)

    dec_mixed, dec_attended, dec_totals, unit_three, scale_three = decoder_self_forward(
        12, target_tokens, weights["dec_qkv"], weights["dec_out"], shared, split, hidden_half
    )
    (decoder_states, first_low, crs_attended, second_low, dec_active,
     dec_feed_low, dec_grad_up, dec_up_bias, sums_five, sums_four,
     crs_low, crs_grad_query, crs_grad_pair, fetched_low, grad_three, crs_sums, sums_three) = decoder_core(
        13, unit_three, scale_three, fetched, target_cotangent,
        weights["crs_q"], weights["crs_kv"], weights["crs_out"], weights["dec_up"], weights["dec_down"],
        shared, split,
    )
    returned = lax.all_to_all(
        fetched_low.reshape(qblocks, device_count, per_owner, model_width),
        "dp", split_axis=1, concat_axis=1, tiled=True,
    )
    dec_low, dec_grad_query, dec_grad_pair, target_grad, dec_sums = decoder_self_backward(
        17, grad_three, dec_mixed, dec_attended, dec_totals, weights["dec_qkv"], weights["dec_out"]
    )
    stored_grad = jnp.einsum(
        "ka,ab->kb", matches, returned.reshape(-1, model_width), preferred_element_type=F32
    )
    (enc_feed_low, enc_grad_up, enc_up_bias, sums_two, sums_one,
     enc_low, enc_grad_query, enc_grad_pair, grad_turned, enc_sums) = encoder_backward(
        18, stored_grad, unit_two, scale_two, enc_active, enc_slope, weights["enc_up"], weights["enc_down"],
        unit_one, scale_one, enc_mixed, enc_attended, enc_totals, weights["enc_qkv"], weights["enc_out"], shared,
    )
    source_grad = jnp.roll(grad_turned, start_row, 0)

    first_block, total_blocks = {}, 0
    for name, height, breadth in matrix_list(model_width, hidden_width, tensor_count):
        first_block[name] = total_blocks
        total_blocks += height // TILE * (breadth // TILE)
    three = 3 * half_width
    outer = ((0, half_width), (2 * half_width, three))
    everything = ((0, hidden_half),)
    items = [
        (sums, 3 * i, None) for i, sums in enumerate((sums_one, sums_two, sums_three, sums_four, sums_five))
    ]
    at = shared_count * model_width
    for array, pieces in (
        (enc_sums, outer), (enc_up_bias, everything), (dec_sums, outer), (crs_sums, outer), (dec_up_bias, everything)
    ):
        items.append((array, at, pieces))
        at += sum(end - begin for begin, end in pieces)
    (slot_grads,) = weight_grads(
        [
            (first_block["dec_down"], [(dec_active, dec_feed_low)]),
            (first_block["dec_up"], [(second_low, dec_grad_up)]),
            (first_block["crs_out"], [(crs_attended, crs_low)]),
            (first_block["crs_q"], [(first_low, crs_grad_query)]),
            (first_block["crs_kv"], [(fetched, crs_grad_pair)]),
            (first_block["dec_out"], [(dec_attended, dec_low)]),
            (first_block["dec_qkv"], [(target_tokens, dec_grad_query), (target_tokens, dec_grad_pair)]),
        ],
        owner_slots,
        gathered.shape[0],
    )
    slot_grads, vector_grads = weight_grads(
        [
            (first_block["enc_down"], [(enc_active, enc_feed_low)]),
            (first_block["enc_up"], [(hidden_low, enc_grad_up)]),
            (first_block["enc_out"], [(enc_attended, enc_low)]),
            (first_block["enc_qkv"], [(turned, enc_grad_query), (turned, enc_grad_pair)]),
        ],
        owner_slots,
        gathered.shape[0],
        slot_grads,
        (padded, model_width, items),
    )
    slots = master.shape[1]
    owned_slots = me * slots + lax.broadcasted_iota(jnp.int32, (slots, 1), 0)
    used = jnp.any(owned_slots == owner_slots[None, :], 1).astype(jnp.int32)
    results, vector_sums = owner_update(
        used,
        slot_grads,
        vector_grads,
        [
            array[0]
            for array in (
                master, first_moment, second_moment, left_stats, right_stats, left_basis, right_basis
            )
        ],
        device_count,
    )
    vector_owned = lax.dynamic_slice_in_dim(vector_sums, me * vector_width, vector_width, 1)
    shared_owned = vector_owned[:shared_count]
    split_owned = vector_owned[shared_count:vector_count]
    new_master, new_first, new_second, new_left, new_right, new_lbasis, new_rbasis = results
    shared_new_first, shared_new_second, shared_updated = adam_vector(
        shared_owned, shared_vectors, shared_first, shared_second
    )
    split_new_first, split_new_second, split_updated = adam_vector(
        split_owned, split_vectors[0], split_first[0], split_second[0]
    )
    return (
        encoder_states,
        decoder_states,
        source_grad,
        target_grad,
        new_master[None],
        new_first[None],
        new_second[None],
        new_left[None],
        new_right[None],
        new_lbasis[None],
        new_rbasis[None],
        shared_new_first,
        shared_new_second,
        shared_updated,
        split_new_first[None],
        split_new_second[None],
        split_updated[None],
    )


def solution(mesh):
    placed = (
        P("dp", None),
        P("dp", None),
        P("dp", None),
        P("dp", None),
        P("dp"),
        P(),
        P("tensor", "dp", None, None),
        P("tensor", "dp", None, None),
        P("tensor", "dp", None, None),
        P("tensor", "dp", None, None),
        P("tensor", "dp", None, None),
        P("tensor", "dp", None, None),
        P("tensor", "dp", None, None),
        P(None, "dp"),
        P(None, "dp"),
        P(None, "dp"),
        P("tensor", None, "dp"),
        P("tensor", None, "dp"),
        P("tensor", None, "dp"),
    )
    return jax.shard_map(
        local,
        mesh=mesh,
        in_specs=placed,
        out_specs=(
            P("dp", None),
            P("dp", None),
            P("dp", None),
            P("dp", None),
            P("tensor", "dp", None, None),
            P("tensor", "dp", None, None),
            P("tensor", "dp", None, None),
            P("tensor", "dp", None, None),
            P("tensor", "dp", None, None),
            P("tensor", "dp", None, None),
            P("tensor", "dp", None, None),
            P(None, "dp"),
            P(None, "dp"),
            P(None, "dp"),
            P("tensor", None, "dp"),
            P("tensor", None, "dp"),
            P("tensor", None, "dp"),
        ),
        check_vma=False,
    )
```

time: 1030 us -> 634 us (0.62)
  matrix products: 218 us -> 6.9 us
  waiting for transfers between devices: 149 us -> 23.2 us
  Pallas kernels: 428 us -> 546 us
  other arithmetic: 112 us -> 19.5 us
  local copies, waits for them, and re-layouts: 83.5 us -> 8.86 us
  between operations: 19 us -> 4 us
    dot_general x52 -> x2, matrix products: 218 us -> 6.9 us  [the longest x1 3.59 us: local(): jnp.einsum('ka,ab->kb', matches, returned.reshape(-1, model_width), prefe...]
    pallas_call x4 -> x10, Pallas kernels: 269 us -> 388 us  [the longest x1 173 us: owner_update(): pl.pallas_call(functools.partial(owner_kernel, grid), out_shape=[jax.Shap...]
    psum x8 -> x0, waiting for transfers between devices: 99.2 us -> none  [the longest x4 55.7 us: tensor_sum(): return lax.psum(values.astype(jnp.bfloat16), 'tensor').astype(jnp.float32)]
    reduce_sum x28 -> x0, other arithmetic: 77.3 us -> none  [the longest x3 26 us: attend_forward(): totals = jax.nn.logsumexp(scores, axis=-1, keepdims=True)]
    unnamed x452 -> x37, local copies, waits for them, and re-layouts: 39 us -> 6.08 us
    convert_element_type x5 -> x0, other arithmetic: 26.4 us -> none  [the longest x3 25.5 us: attend_backward(): (probs * (grad_probs - jnp.sum(grad_probs * probs, -1, keepdims=True))).a...]
    all_to_all x1, waiting for transfers between devices: 22.1 us -> 0.1 us  [local(): lax.all_to_all(fetched_low.reshape(qblocks, device_count, per_owner, mode...]
    concatenate x1 -> x3, other arithmetic: 0.01 us -> 11.7 us  [the longest x1 4.79 us: local(): source_grad = jnp.roll(grad_turned, start_row, 0)]
  transfers between devices with their start and end apart: 10 -> 2, of which waited for: 9 -> 2; matrix products, arithmetic and copies ran while one was open for 9% -> 1% of each run, Pallas kernels for 1% -> 6%
where the time goes in v2:
time: 634 us; the launch traced here: 625 us
  Pallas kernels  546 us (86%)
  waiting for transfers between devices  23.2 us (4%)
  other arithmetic  19.5 us (3%)
  starting transfers between devices  16.7 us (3%)
  local copies, waits for them, and re-layouts  8.86 us (1%)
  matrix products  6.9 us (1%)
    pallas_call x1, Pallas kernels, owner_update(): pl.pallas_call(functools.partial(owner_kernel, grid), out_shape=[jax.Shap...  173 us
    pallas_call x1, Pallas kernels, gather_all(): pl.pallas_call(functools.partial(ag_kernel, grid), out_shape=[jax.ShapeDt...  159 us
    pallas_call x5, Pallas kernels, call(): pl.pallas_call(body, out_shape=outputs, in_specs=[VM] * len(inputs), out_...  151 us
    pallas_call x2, Pallas kernels, weight_grads(): pl.pallas_call(functools.partial(weight_grads_kernel, plan, len(arrays),...  30.4 us
    all_to_all x1, waiting for transfers between devices, local(): lax.all_to_all(served.reshape(qblocks, device_count, per_owner, model_wid...  23.1 us
    pallas_call x1, Pallas kernels, last_bases(): pl.pallas_call(last_bases_kernel, out_shape=[jax.ShapeDtypeStruct(whole,...  20.8 us
  transfers between devices with their start and end apart: 2, of which 2 were waited for; matrix products, arithmetic and copies ran while one was open for 1% of the time, Pallas kernels for 6%

profile of v2, /device:TPU:0, one launch (start us, length us, event | category | flops | bytes accessed | tf_op | source)
XLA Modules:
  0.0 625.3 jit_solution(13706076168318047908)
XLA Ops:
  0.7 0.0 copy-start
  0.7 0.0 copy-start.12
  0.7 0.0 copy-start.9
  0.7 0.0 copy-start.7
  0.7 0.0 copy-done
  0.7 0.7 iota_reduce_fusion
  2.7 0.0 copy-start.6
  2.7 2.8 bitcast_convert_fusion.own_ref
  5.5 0.0 copy-done.12
  5.5 0.0 copy-done.9
  5.6 0.0 copy-done.7
  5.6 0.6 pad_maximum_fusion.small_ref
  6.2 158.5 %gather_all.1 = (bf16[4,2,2,32,128,128]{5,4,3,2,1,0:T(8,128)(2,1)}, f32[4,2,2,32,128]{4,3,2,1,0:T(8,128)}) custom-call(bf16[32,128,128]{2,1,0:T(8,128)(2,1)} %bitcast_convert_fusion.own_ref, f32[32,128]{1,0:T(8,128)} %pad_maximum_fusion.small_ref), custom_call_target="tpu_custom_call" | custom-call | tf_op jit(solution)/shard_map/gather_all/pallas_call | solution.py:609
  164.7 0.9 slice.27
  165.7 0.8 slice.30
  166.6 0.1 convert_element_type.41
  166.7 0.6 pad_convert_fusion.shared_ref
  167.3 0.7 reshape.110.split_ref
  168.0 0.1 reshape.103
  168.2 0.1 sub.31
  168.3 0.0 copy-done.6
  168.3 3.7 fusion.5.x_ref.refs_6_
  172.0 12.3 %unpack_tiles.1 = (bf16[768,1152]{1,0:T(8,128)(2,1)}, bf16[384,768]{1,0:T(8,128)(2,1)}, bf16[768,1536]{1,0:T(8,128)(2,1)}, bf16[1536,768]{1,0:T(8,128)(2,1)}, bf...) custom-call(s32[504]{0:T(512)} %slots_ref.5, ...), custom_call_target="tpu_custom_call" | custom-call | tf_op jit(solution)/shard_map/unpack_tiles/pallas_call | solution.py:649
  184.3 36.0 %encoder_forward.1 = (bf16[1024,1152]{1,0:T(8,128)(2,1)}, bf16[1024,384]{1,0:T(8,128)(2,1)}, f32[8,1024]{1,0:T(8,128)}, f32[1024,768]{1,0:T(8,128)}, f32[1024,1]...) custom-call(bf16[1024,768]{1,0:T(8,128)(2,1)} %fusion.5.x_ref.refs_6, ...), custom_call_target="tpu_custom_call" | custom-call | tf_op jit(solution)/shard_map/encoder_forward/pallas_call | solution.py:1274
  220.3 3.3 fusion.4
  223.6 8.3 %all-to-all-start = ((bf16[1,16,64,768]{3,2,0,1:T(8,128)(2,1)}), bf16[1,16,64,768]{3,2,0,1:T(8,128)(2,1)S(1)}, u32[]{:S(2)}, u32[]{:S(2)}) async-start(bf16[1,16,64,768]{3,2,0,1:T(8,128)(2,1)} %bitcast.6), calls=%async_computation | async-start | bytes 3145728 | tf_op jit(solution)/shard_map/all_to_all | solution.py:1559
  232.0 11.1 %decoder_self_forward.1 = (bf16[512,1152]{1,0:T(8,128)(2,1)}, bf16[512,384]{1,0:T(8,128)(2,1)}, f32[8,512]{1,0:T(8,128)}, f32[512,768]{1,0:T(8,128)}, f32[512,1]{1,0:T(8,128)}) custom-call(bf16[512,768]{1,0:T(8,128)(2,1)} %refs_12_.1, bf16[768,1152]{1,0:T(8,128)(2,1)} %get-tuple-element.107.wide_ref.refs_4_, ...), custom_call_target="tpu_custom_call" | custom-call | tf_op jit(solution)/shard_map/decoder_self_forward/pallas_call | solution.py:1274
  243.1 23.1 %all-to-all-done = bf16[1,16,64,768]{3,2,0,1:T(8,128)(2,1)S(1)} async-done(((bf16[1,16,64,768]{3,2,0,1:T(8,128)(2,1)}), bf16[1,16,64,768]{3,2,0,1:T(8,128)(2,1)S(1)}, u32[]{:S(2)}, u32[]{:S(2)}) %all-to-all-start) | async-done | bytes 1572896 | tf_op jit(solution)/shard_map/all_to_all | solution.py:1559
  266.2 1.1 copy-done.2
  267.4 59.2 %decoder_core.1 = (f32[512,768]{1,0:T(8,128)}, bf16[512,768]{1,0:T(8,128)(2,1)}, bf16[512,384]{1,0:T(8,128)(2,1)}, bf16[512,768]{1,0:T(8,128)(2,1)}, bf16[512,15...) custom-call(f32[512,768]{1,0:T(8,128)} %get-tuple-element.109.unit_r, ...), custom_call_target="tpu_custom_call" | custom-call | tf_op jit(solution)/shard_map/decoder_core/pallas_call | solution.py:1274
  326.6 0.0 copy-start.8
  326.6 0.0 copy-start.3
  326.6 8.4 %all-to-all-start.1 = ((bf16[1,16,64,768]{3,2,0,1:T(8,128)(2,1)}), bf16[1,16,64,768]{3,2,0,1:T(8,128)(2,1)}, u32[]{:S(2)}, u32[]{:S(2)}) async-start(bf16[1,16,64,768]{3,2,0,1:T(8,128)(2,1)} %bitcast.66), calls=%async_computation.1 | async-start | bytes 3145728 | tf_op jit(solution)/shard_map/all_to_all | solution.py:1574
  336.3 0.0 copy-done.8
  336.4 0.2 compare_reduce_fusion
  336.5 0.5 convert_element_type.44.refs_0_
  337.1 0.0 copy-done.3
  337.1 3.2 fusion.1
  340.3 12.5 %decoder_self_backward.1 = (bf16[512,768]{1,0:T(8,128)(2,1)}, bf16[512,384]{1,0:T(8,128)(2,1)}, bf16[512,768]{1,0:T(8,128)(2,1)}, f32[512,768]{1,0:T(8,128)}, f32[1,1152]{1,0:T(1,128)}) custom-call(f32[512,768]{1,0:T(8,128)} %get-tuple-element.129.refs_0_, bf16[512,1152]{1,0:T(8,128)(2,1)} %get-tuple-element.130.refs_1_, ...), custom_call_target="tpu_custom_call" | custom-call | tf_op jit(solution)/shard_map/decoder_self_backward/pallas_call | solution.py:1274
  352.8 16.4 %weight_grads.2.refs_19_ = bf16[512,128,128]{2,1,0:T(8,128)(2,1)} custom-call(s32[504]{0:T(512)} %slots_ref.5, bf16[512,1536]{1,0:T(8,128)(2,1)} %get-tuple-element.150.refs_0_, bf16[512,768]{1,0:T(8,128)(2,1)} %get-tuple-element.151.refs_1_, bf16[512,768]{1,0:T(8,128)(2,1)} %get-tuple-element.152.refs_2_, bf16[512,1536]{1,0:T(8,128)(2,1)} %get-tuple-element.153.refs_3_, ...), custom_call_target="tpu_custom_call" | custom-call | tf_op jit(solution)/shard_map/weight_grads/pallas_call | solution.py:763
  369.2 0.1 all-to-all-done.1
  369.3 3.6 fusion.2.grad_ref
  372.9 31.7 %encoder_backward.1 = (bf16[512,768]{1,0:T(8,128)(2,1)}, bf16[512,1536]{1,0:T(8,128)(2,1)}, f32[1,1536]{1,0:T(1,128)}, f32[8,768]{1,0:T(8,128)}, f32[8,768]{1,0:...) custom-call(f32[512,768]{1,0:T(8,128)} %fusion.2.grad_ref, ...), custom_call_target="tpu_custom_call" | custom-call | tf_op jit(solution)/shard_map/encoder_backward/pallas_call | solution.py:1274
  404.6 4.8 fusion
  409.4 14.1 %weight_grads.3 = (bf16[512,128,128]{2,1,0:T(8,128)(2,1)}, f32[24,768]{1,0:T(8,128)}) custom-call(s32[504]{0:T(512)} %slots_ref.5, bf16[512,1536]{1,0:T(8,128)(2,1)} %get-tuple-element.121.active_ref.refs_0_, bf16[512,768]{1,0:T(8,128)(2,1)} %get-tuple-element.134.refs_1_, ...), custom_call_target="tpu_custom_call", output_to_operand_aliasing={{0}: (20, {})} | custom-call | tf_op jit(solution)/shard_map/weight_grads/pallas_call | solution.py:763
  423.5 0.0 copy-start.13
  423.5 0.0 copy-start.14
  423.5 0.0 copy-start.10
  423.5 0.0 copy-start.11
  423.5 173.4 %owner_update.1 = (f32[32,128,128]{2,1,0:T(8,128)}, f32[32,128,128]{2,1,0:T(8,128)}, f32[32,128,128]{2,1,0:T(8,128)}, f32[32,128,128]{2,1,0:T(8,128)}, f32[32,12...) custom-call(s32[32]{0:T(128)} %convert_element_type.44.refs_0_, ...), custom_call_target="tpu_custom_call" | custom-call | tf_op jit(solution)/shard_map/owner_update/pallas_call | solution.py:482
  596.9 0.0 copy-done.13
  596.9 0.0 copy-done.14
  597.0 0.8 subtract_bitcast_fusion
  597.8 0.6 copy.56
  598.4 0.6 copy.57
  599.0 0.6 copy.58
  599.5 0.0 copy-done.10
  599.5 0.0 copy-done.11
  599.5 1.4 divide_subtract_fusion
  601.0 20.8 %last_bases.1 = (f32[32,128,128]{2,1,0:T(8,128)}, f32[32,128,128]{2,1,0:T(8,128)}, f32[32,128,128]{2,1,0:T(8,128)}, f32[32,128,128]{2,1,0:T(8,128)}, f32[32,128,...) custom-call(f32[16,128,256]{2,1,0:T(8,128)} %get-tuple-element.164.work_ref, ...), custom_call_target="tpu_custom_call" | custom-call | tf_op jit(solution)/shard_map/last_bases/pallas_call | solution.py:355
  621.8 0.0 copy-start.1
  621.8 1.1 copy.86
  622.9 0.8 copy-done.5
  623.7 1.1 copy.87
  (13 shorter events, 0.1 us)
Async XLA Ops:
  0.7 4.9 copy-start.12
  0.7 4.9 copy-start.9
  0.7 4.9 copy-start.7
  2.7 165.6 %copy-start.6 = (bf16[1024,768]{1,0:T(8,128)(2,1)S(1)}, bf16[1024,768]{1,0:T(8,128)(2,1)}, u32[]{:S(2)}) copy-start(bf16[1024,768]{1,0:T(8,128)(2,1)} %param.21) | copy-start | bytes 4718596
  223.6 42.6 %all-to-all-start = ((bf16[1,16,64,768]{3,2,0,1:T(8,128)(2,1)}), bf16[1,16,64,768]{3,2,0,1:T(8,128)(2,1)S(1)}, u32[]{:S(2)}, u32[]{:S(2)}) async-start(bf16[1,16,64,768]{3,2,0,1:T(8,128)(2,1)} %bitcast.6), calls=%async_computation | async-start | bytes 3145728 | tf_op jit(solution)/shard_map/all_to_all | solution.py:1559
  266.2 1.1 copy-start.2
  326.6 9.8 %copy-start.8 = (s32[504]{0:T(512)S(1)}, s32[504]{0:T(512)}, u32[]{:S(2)}) copy-start(s32[504]{0:T(512)} %slots_ref.5) | copy-start | bytes 6052
  326.6 10.5 %copy-start.3 = (f32[1024,768]{1,0:T(8,128)S(1)}, f32[1024,768]{1,0:T(8,128)}, u32[]{:S(2)}) copy-start(f32[1024,768]{1,0:T(8,128)} %get-tuple-element.106) | copy-start | bytes 9437188
  326.6 42.7 %all-to-all-start.1 = ((bf16[1,16,64,768]{3,2,0,1:T(8,128)(2,1)}), bf16[1,16,64,768]{3,2,0,1:T(8,128)(2,1)}, u32[]{:S(2)}, u32[]{:S(2)}) async-start(bf16[1,16,64,768]{3,2,0,1:T(8,128)(2,1)} %bitcast.66), calls=%async_computation.1 | async-start | bytes 3145728 | tf_op jit(solution)/shard_map/all_to_all | solution.py:1574
  423.5 173.5 %copy-start.13 = (f32[1,7,48]{2,0,1:T(1,128)S(1)}, f32[1,7,48]{2,0,1:T(1,128)}, u32[]{:S(2)}) copy-start(f32[1,7,48]{2,0,1:T(1,128)} %param.38) | copy-start | bytes 4036
  423.5 173.5 %copy-start.14 = (f32[1,7,48]{2,0,1:T(1,128)S(1)}, f32[1,7,48]{2,0,1:T(1,128)}, u32[]{:S(2)}) copy-start(f32[1,7,48]{2,0,1:T(1,128)} %param.39) | copy-start | bytes 4036
  423.5 176.0 %copy-start.10 = (f32[15,48]{1,0:T(8,128)S(1)}, f32[15,48]{1,0:T(8,128)}, u32[]{:S(2)}) copy-start(f32[15,48]{1,0:T(8,128)} %param.36) | copy-start | bytes 8644
  423.5 176.0 %copy-start.11 = (f32[15,48]{1,0:T(8,128)S(1)}, f32[15,48]{1,0:T(8,128)}, u32[]{:S(2)}) copy-start(f32[15,48]{1,0:T(8,128)} %param.35) | copy-start | bytes 8644
  601.0 20.8 %copy-start.4 = (f32[512,768]{1,0:T(8,128)S(1)}, f32[512,768]{1,0:T(8,128)}, u32[]{:S(2)}) copy-start(f32[512,768]{1,0:T(8,128)} %get-tuple-element.255) | copy-start | bytes 4718596
  621.8 2.0 copy-start.5
  621.8 3.1 copy-start.1
  (1 other events, 0.0 us)

commit v3 on v2

--- a/solution.py
+++ b/solution.py
@@ -1270,20 +1270,65 @@
     lax.fori_loop(0, queries // ROWS, take_near, 0)
 
 
+def held(*dims, dtype=F32):
+    return pltpu.VMEM(dims, dtype)
+
+
+def streams(array):
+    rows, width = array.shape
+    return rows % 16 == 0 and width % TILE == 0 and rows * width * array.dtype.itemsize >= 1 << 18
+
+
 def call(name, ident, body, inputs, outputs, scratch):
+    ins = [i for i, array in enumerate(inputs) if streams(array)]
+    outs = [i for i, array in enumerate(outputs) if streams(array)]
+    count_in, count_out = len(inputs), len(outputs)
+
+    def kernel(*refs):
+        in_refs, out_refs, rest = refs[:count_in], refs[count_in:count_in + count_out], refs[count_in + count_out:]
+        near_in, near_out = list(in_refs), list(out_refs)
+        for place, ref in zip(ins, rest[:len(ins)]):
+            near_in[place] = ref
+        rest = rest[len(ins):]
+        for place, ref in zip(outs, rest[:len(outs)]):
+            near_out[place] = ref
+        rest = rest[len(outs):]
+        in_sem, out_sem, rest = rest[0], rest[1], rest[2:]
+
+        def load(place):
+            return pltpu.make_async_copy(in_refs[place], near_in[place], in_sem.at[place])
+
+        def store(place):
+            return pltpu.make_async_copy(near_out[place], out_refs[place], out_sem.at[place])
+
+        def need(*places):
+            for place in places:
+                if place in ins:
+                    load(place).wait()
+
+        def done(*places):
+            for place in places:
+                if place in outs:
+                    store(place).start()
+
+        for place in ins:
+            load(place).start()
+        body(need, done, *near_in, *near_out, *rest)
+        for place in outs:
+            store(place).wait()
+
     return pl.pallas_call(
-        body,
+        kernel,
         out_shape=outputs,
-        in_specs=[VM] * len(inputs),
-        out_specs=[VM] * len(outputs),
-        scratch_shapes=scratch,
+        in_specs=[ANY if i in ins else VM for i in range(count_in)],
+        out_specs=[ANY if i in outs else VM for i in range(count_out)],
+        scratch_shapes=[pltpu.VMEM(inputs[i].shape, inputs[i].dtype) for i in ins]
+        + [pltpu.VMEM(outputs[i].shape, outputs[i].dtype) for i in outs]
+        + [pltpu.SemaphoreType.DMA((count_in,)), pltpu.SemaphoreType.DMA((count_out,))]
+        + scratch,
         compiler_params=params(ident),
         name=name,
     )(*inputs)
-
-
-def held(*dims, dtype=F32):
-    return pltpu.VMEM(dims, dtype)
 
 
 def encoder_forward(ident, x, wide, out_weight, up, down, shared, split, kept):
@@ -1292,18 +1337,22 @@
     tiles, span = length // ROWS, min(length, 512)
     places = bias_places(half, hidden_half)
 
-    def body(x_ref, wide_ref, out_weight_ref, up_ref, down_ref, shared_ref, split_ref, *refs):
+    def body(need, done, x_ref, wide_ref, out_weight_ref, up_ref, down_ref, shared_ref, split_ref, *refs):
         saved, fed, rest = refs[:5], refs[5:12], refs[12:]
+        need(0, 1, 2)
         Swap.greet()
         self_forward_kernel(
             False, span, x_ref, wide_ref, out_weight_ref,
             bias_row(split_ref, places, ("enc_q", None, "enc_v"), half), Rows(shared_ref, (0,)),
             *saved, *rest[:6],
         )
+        done(0, 1, 2, 3, 4)
+        need(3, 4, 5, 6)
         feed_forward_kernel(
             kept, saved[3], up_ref, down_ref, split_ref.at[:, places["enc_up"]],
             Rows(shared_ref, (1, 2, 3, 4, 5)), *fed, *rest[6:],
         )
+        done(*range(5, 12))
 
     return call(
         "encoder_forward", ident, body, [x, wide, out_weight, up, down, shared, split],
@@ -1318,26 +1367,131 @@
     )
 
 
-def decoder_self_forward(ident, x, wide, out_weight, shared, split, hidden_half):
+class Trade:
+    def __init__(self, count, into, send_sem, recv_sem, give_sem, take_sem):
+        self.count, self.into = count, into
+        self.send_sem, self.recv_sem, self.give_sem, self.take_sem = send_sem, recv_sem, give_sem, take_sem
+        self.me, self.core = lax.axis_index("dp"), lax.axis_index("tensor")
+        self.rows, self.half = into.shape[0] // count, into.shape[1] // 2
+
+    @staticmethod
+    def scratch(count):
+        return [pltpu.SemaphoreType.DMA((count,))] * 4
+
+    def greet(self):
+        barrier = pltpu.get_barrier_semaphore()
+
+        def signal(k, carry):
+            other = {"dp": lax.rem(self.me + k, self.count)}
+            pl.semaphore_signal(barrier, inc=1, device_id=other, device_id_type=MESH)
+            return carry
+
+        lax.fori_loop(1, self.count, signal, 0)
+        pl.semaphore_signal(barrier, inc=1, device_id={"tensor": 1 - self.core}, device_id_type=MESH)
+        pl.semaphore_wait(barrier, self.count)
+
+    def rows_of(self, device):
+        return pl.ds(pl.multiple_of(device * self.rows, self.rows), self.rows)
+
+    def mine(self):
+        return pl.ds(pl.multiple_of(self.core * self.half, self.half), self.half)
+
+    def send(self, source, k):
+        other = lax.rem(self.me + k, self.count)
+        return pltpu.make_async_remote_copy(
+            src_ref=source.at[self.rows_of(other), :],
+            dst_ref=self.into.at[self.rows_of(self.me), self.mine()],
+            send_sem=self.send_sem.at[k],
+            recv_sem=self.recv_sem.at[k],
+            device_id={"dp": other},
+            device_id_type=MESH,
+        )
+
+    def pass_on(self, k):
+        part = self.into.at[self.rows_of(lax.rem(self.me - k + self.count, self.count)), self.mine()]
+        return pltpu.make_async_remote_copy(
+            src_ref=part,
+            dst_ref=part,
+            send_sem=self.give_sem.at[k],
+            recv_sem=self.take_sem.at[k],
+            device_id={"tensor": 1 - self.core},
+            device_id_type=MESH,
+        )
+
+    def start(self, source):
+        def go(k, carry):
+            self.send(source, k).start()
+            return carry
+
+        lax.fori_loop(1, self.count, go, 0)
+        self.into[self.rows_of(self.me), self.mine()] = source[self.rows_of(self.me), :]
+        self.pass_on(0).start()
+
+    def finish(self, source):
+        def meet(k, carry):
+            self.send(source, k).wait_recv()
+            self.pass_on(k).start()
+            return carry
+
+        lax.fori_loop(1, self.count, meet, 0)
+
+        def end(k, carry):
+            self.pass_on(k).wait()
+            return carry
+
+        lax.fori_loop(0, self.count, end, 0)
+
+        def sent(k, carry):
+            self.send(source, k).wait_send()
+            return carry
+
+        lax.fori_loop(1, self.count, sent, 0)
+
+
+def fetch_and_self_forward(ident, stored, wanted, x, wide, out_weight, shared, split, hidden_half, count):
     length, width = x.shape
     half = out_weight.shape[0]
     span = min(length, 512)
+    fetched_rows = wanted.shape[0]
     places = bias_places(half, hidden_half)
 
-    def body(x_ref, wide_ref, out_weight_ref, shared_ref, split_ref, *refs):
-        Swap.greet()
+    def body(
+        need, done, stored_ref, wanted_ref, x_ref, wide_ref, out_weight_ref, shared_ref, split_ref,
+        mixed_ref, attended_ref, totals_ref, unit_ref, scale_ref, fetched_ref,
+        served_ref, landed_ref, send_sem, recv_sem, give_sem, take_sem, *rest,
+    ):
+        trade = Trade(count, landed_ref, send_sem, recv_sem, give_sem, take_sem)
+        need(0, 1)
+
+        def serve(t, carry):
+            want = wanted_ref[rows_of(t), :]
+            match = want == lax.broadcasted_iota(jnp.int32, (ROWS, stored_ref.shape[0]), 1)
+            pick = jnp.where(match, 1.0, 0.0).astype(BF16)
+            served_ref[rows_of(t), :] = times(pick, stored_ref[:, trade.mine()]).astype(BF16)
+            return carry
+
+        lax.fori_loop(0, fetched_rows // ROWS, serve, 0)
+        trade.greet()
+        trade.start(served_ref)
+        need(2, 3, 4)
         self_forward_kernel(
             True, span, x_ref, wide_ref, out_weight_ref,
-            bias_row(split_ref, places, ("dec_q", None, "dec_v"), half), Rows(shared_ref, (6,)), *refs,
+            bias_row(split_ref, places, ("dec_q", None, "dec_v"), half), Rows(shared_ref, (6,)),
+            mixed_ref, attended_ref, totals_ref, unit_ref, scale_ref, *rest,
         )
+        done(0, 1, 2, 3, 4)
+        trade.finish(served_ref)
+        fetched_ref[...] = landed_ref[...]
+        done(5)
 
     return call(
-        "decoder_self_forward", ident, body, [x, wide, out_weight, shared, split],
+        "fetch_and_self_forward", ident, body, [stored, wanted, x, wide, out_weight, shared, split],
         [
             shape(length, 3 * half, dtype=BF16), shape(length, half, dtype=BF16), shape(8, length),
-            shape(length, width), shape(length, 1),
+            shape(length, width), shape(length, 1), shape(fetched_rows, width, dtype=BF16),
         ],
-        [held(2, length, span), held(half, length, dtype=BF16)] + Swap.scratch(length // ROWS, width),
+        [held(fetched_rows, width // 2, dtype=BF16), held(fetched_rows, width, dtype=BF16)] + Trade.scratch(count)
+        + [held(2, length, span), held(half, length, dtype=BF16)] + Swap.scratch(length // ROWS, width),
     )
 
 
@@ -1351,7 +1505,7 @@
     places = bias_places(half, hidden_half)
 
     def body(
-        unit_ref, scale_ref, fetched_ref, cotangent_ref, query_weight_ref, wide_ref, out_weight_ref,
+        need, done, unit_ref, scale_ref, fetched_ref, cotangent_ref, query_weight_ref, wide_ref, out_weight_ref,
         up_ref, down_ref, shared_ref, split_ref,
         states_ref, low_ref, attended_ref, second_low_ref, active_ref,
         feed_low_ref, grad_up_ref, up_bias_ref, sums_after_ref, sums_before_ref,
@@ -1359,6 +1513,7 @@
         query_ref, mixed_ref, totals_ref, unit_four_ref, scale_four_ref, states_low_ref, slope_ref,
         unit_five_ref, scale_five_ref, grad_four_ref, inner_ref, score_ref, turned_ref, grad_ref, *swaps,
     ):
+        need(0, 1, 2, 4, 5, 6, 9, 10)
         Swap.greet()
         cross_forward_kernel(
             span, unit_ref, fetched_ref, query_weight_ref, wide_ref, out_weight_ref,
@@ -1367,24 +1522,30 @@
             low_ref, query_ref, mixed_ref, attended_ref, totals_ref, unit_four_ref, scale_four_ref,
             score_ref, turned_ref, *swaps[:4],
         )
+        done(1, 2)
+        need(7, 8)
         feed_forward_kernel(
             length, unit_four_ref, up_ref, down_ref, split_ref.at[:, places["dec_up"]],
             Rows(shared_ref, (10, 11, 12, 13, 14)),
             states_ref, states_low_ref, second_low_ref, active_ref, slope_ref, unit_five_ref, scale_five_ref,
             *swaps[4:8],
         )
+        done(0, 3, 4)
+        need(3)
         feed_backward_kernel(
             cotangent_ref, unit_five_ref, scale_five_ref, active_ref, slope_ref, up_ref, down_ref,
             unit_four_ref, scale_four_ref, Rows(shared_ref, (13, 10)),
             feed_low_ref, grad_up_ref, up_bias_ref, grad_four_ref, sums_after_ref, sums_before_ref,
             inner_ref, *swaps[8:12],
         )
+        done(5, 6, 7, 8, 9)
         cross_backward_kernel(
             grad_four_ref, query_ref, mixed_ref, attended_ref, totals_ref, query_weight_ref, wide_ref,
             out_weight_ref, unit_ref, scale_ref, Rows(shared_ref, (7,)),
             cross_low_ref, grad_query_ref, grad_pair_ref, returned_ref, grad_out_ref, cross_sums_ref, vec_sums_ref,
             grad_ref, turned_ref, *swaps[12:],
         )
+        done(*range(10, 17))
 
     return call(
         "decoder_core", ident, body,
@@ -1412,9 +1573,11 @@
     queries, width = grad_pre.shape
     length, half = mixed.shape[0], out_weight.shape[0]
 
-    def body(*refs):
+    def body(need, done, *refs):
+        need(*range(6))
         Swap.greet()
         self_backward_kernel(True, *refs)
+        done(*range(5))
 
     return call(
         "decoder_self_backward", ident, body, [grad_pre, mixed, attended, totals, wide, out_weight],
@@ -1434,12 +1597,13 @@
     length, half, hidden_half = mixed.shape[0], out_weight.shape[0], up.shape[1]
 
     def body(
-        grad_ref, unit_two_ref, scale_two_ref, active_ref, slope_ref, up_ref, down_ref, unit_one_ref, scale_one_ref,
+        need, done, grad_ref, unit_two_ref, scale_two_ref, active_ref, slope_ref, up_ref, down_ref, unit_one_ref, scale_one_ref,
         mixed_ref, attended_ref, totals_ref, wide_ref, out_weight_ref, shared_ref,
         feed_low_ref, grad_up_ref, up_bias_ref, sums_after_ref, sums_before_ref,
         low_ref, grad_query_ref, grad_pair_ref, grad_x_ref, sums_ref,
         grad_one_ref, inner_ref, grad_out_ref, turned_ref, *swaps,
     ):
+        need(*range(9), 14)
         Swap.greet()
         feed_backward_kernel(
             grad_ref, unit_two_ref, scale_two_ref, active_ref, slope_ref, up_ref, down_ref,
@@ -1447,10 +1611,13 @@
             feed_low_ref, grad_up_ref, up_bias_ref, grad_one_ref, sums_after_ref, sums_before_ref,
             inner_ref, *swaps[:4],
         )
+        done(0, 1, 2, 3, 4)
+        need(9, 10, 11, 12, 13)
         self_backward_kernel(
             False, grad_one_ref, mixed_ref, attended_ref, totals_ref, wide_ref, out_weight_ref,
             low_ref, grad_query_ref, grad_pair_ref, grad_x_ref, sums_ref, grad_out_ref, turned_ref, *swaps[4:],
         )
+        done(*range(5, 10))
 
     return call(
         "encoder_backward", ident, body,
@@ -1555,14 +1722,9 @@
         - KEEP * me
     ).reshape(1, -1)
     matches = (wanted == lax.broadcasted_iota(jnp.int32, (KEEP, 1), 0)).astype(BF16)
-    served = jnp.einsum("ka,kb->ab", matches, stored, preferred_element_type=F32).astype(BF16)
-    fetched = lax.all_to_all(
-        served.reshape(qblocks, device_count, per_owner, model_width),
-        "dp", split_axis=1, concat_axis=1, tiled=True,
-    ).reshape(-1, model_width)
-
-    dec_mixed, dec_attended, dec_totals, unit_three, scale_three = decoder_self_forward(
-        12, target_tokens, weights["dec_qkv"], weights["dec_out"], shared, split, hidden_half
+    dec_mixed, dec_attended, dec_totals, unit_three, scale_three, fetched = fetch_and_self_forward(
+        12, stored, wanted.reshape(-1, 1), target_tokens, weights["dec_qkv"], weights["dec_out"],
+        shared, split, hidden_half, device_count,
     )
     (decoder_states, first_low, crs_attended, second_low, dec_active,
      dec_feed_low, dec_grad_up, dec_up_bias, sums_five, sums_four,

time: 634 us -> 604 us (0.953)
  waiting for transfers between devices: 23.2 us -> 1.79 us
    all_to_all x1 -> x0, waiting for transfers between devices: 23.1 us -> none  [local(): lax.all_to_all(served.reshape(qblocks, device_count, per_owner, model_wid...]
    all_to_all x1 -> x0, starting transfers between devices: 8.33 us -> none  [local(): lax.all_to_all(served.reshape(qblocks, device_count, per_owner, model_wid...]
  transfers between devices with their start and end apart: 2 -> 1, of which waited for: 2 -> 1; matrix products, arithmetic and copies ran while one was open for 1% -> 0% of each run, Pallas kernels for 6% -> 5%
where the time goes in v3:
time: 604 us; the launch traced here: 595 us
  Pallas kernels  548 us (91%)
  other arithmetic  16.7 us (3%)
  starting transfers between devices  12.3 us (2%)
  local copies, waits for them, and re-layouts  9.51 us (2%)
    pallas_call x1, Pallas kernels, owner_update(): pl.pallas_call(functools.partial(owner_kernel, grid), out_shape=[jax.Shap...  173 us
    pallas_call x1, Pallas kernels, gather_all(): pl.pallas_call(functools.partial(ag_kernel, grid), out_shape=[jax.ShapeDt...  159 us
    pallas_call x5, Pallas kernels, call(): pl.pallas_call(kernel, out_shape=outputs, in_specs=[ANY if i in ins else...  153 us
    pallas_call x2, Pallas kernels, weight_grads(): pl.pallas_call(functools.partial(weight_grads_kernel, plan, len(arrays),...  30.4 us
    pallas_call x1, Pallas kernels, last_bases(): pl.pallas_call(last_bases_kernel, out_shape=[jax.ShapeDtypeStruct(whole,...  20.8 us
    all_to_all x1, starting transfers between devices, local(): lax.all_to_all(fetched_low.reshape(qblocks, device_count, per_owner, mode...  12.3 us
    pallas_call x1, Pallas kernels, unpack_tiles(): pl.pallas_call(functools.partial(unpack_kernel, shapes), out_shape=[jax.S...  12.3 us
  transfers between devices with their start and end apart: 1, of which 1 were waited for; matrix products, arithmetic and copies ran while one was open for 0% of the time, Pallas kernels for 5%

profile of v3, /device:TPU:0, one launch (start us, length us, event | category | flops | bytes accessed | tf_op | source)
XLA Modules:
  0.0 594.6 jit_solution(13629829935472894481)
XLA Ops:
  0.7 0.0 copy-start
  0.7 0.0 copy-start.12
  0.7 0.0 copy-start.9
  0.7 0.0 copy-start.7
  0.7 0.0 copy-done
  0.7 0.7 iota_reduce_fusion
  2.7 2.7 bitcast_convert_fusion.own_ref
  5.4 0.0 copy-done.12
  5.4 0.0 copy-done.9
  5.4 0.0 copy-done.7
  5.5 0.6 pad_maximum_fusion.small_ref
  6.1 158.5 %gather_all.1 = (bf16[4,2,2,32,128,128]{5,4,3,2,1,0:T(8,128)(2,1)}, f32[4,2,2,32,128]{4,3,2,1,0:T(8,128)}) custom-call(bf16[32,128,128]{2,1,0:T(8,128)(2,1)} %bitcast_convert_fusion.own_ref, f32[32,128]{1,0:T(8,128)} %pad_maximum_fusion.small_ref), custom_call_target="tpu_custom_call" | custom-call | tf_op jit(solution)/shard_map/gather_all/pallas_call | solution.py:609
  164.6 0.9 slice.27
  165.6 0.8 slice.30
  166.5 0.1 convert_element_type.46
  166.6 0.6 pad_convert_fusion.refs_5_.refs_9_.refs_14_
  167.2 0.7 reshape.118.refs_6_.refs_10_
  167.9 0.1 reshape.113
  168.0 0.5 broadcast.55
  168.5 0.7 fusion.11
  169.2 1.3 sub.48.refs_1_
  170.5 0.0 copy-done.6
  170.5 3.7 fusion.3.refs_0_.refs_6_
  174.2 12.3 %unpack_tiles.1 = (bf16[768,1152]{1,0:T(8,128)(2,1)}, bf16[384,768]{1,0:T(8,128)(2,1)}, bf16[768,1536]{1,0:T(8,128)(2,1)}, bf16[1536,768]{1,0:T(8,128)(2,1)}, bf...) custom-call(s32[504]{0:T(512)} %slots_ref.5, ...), custom_call_target="tpu_custom_call" | custom-call | tf_op jit(solution)/shard_map/unpack_tiles/pallas_call | solution.py:649
  186.5 34.7 %encoder_forward.1 = (bf16[1024,1152]{1,0:T(8,128)(2,1)}, bf16[1024,384]{1,0:T(8,128)(2,1)}, f32[8,1024]{1,0:T(8,128)}, f32[1024,768]{1,0:T(8,128)}, f32[1024,1]...) custom-call(bf16[1024,768]{1,0:T(8,128)(2,1)} %fusion.3.refs_0_.refs, ...), custom_call_target="tpu_custom_call" | custom-call | tf_op jit(solution)/shard_map/encoder_forward/pallas_call | solution.py:1320
  221.1 26.3 %fetch_and_self_forward.1 = (bf16[512,1152]{1,0:T(8,128)(2,1)}, bf16[512,384]{1,0:T(8,128)(2,1)}, f32[8,512]{1,0:T(8,128)}, f32[512,768]{1,0:T(8,128)}, f32[512,1]{1,0:T(8,128)}, /*index=5*/bf16[1024,768]{1,0:T(8,128)(2,1)}) custom-call(bf16[512,768]{1,0:T(8,128)(2,1)} %get-tuple-element.108.refs_0_, s32[1024,1]{1,0:T(8,128)} %sub.48.refs_1_, ...), custom_call_target="tpu_custom_call" | custom-call | tf_op jit(solution)/shard_map/fetch_and_self_forward/pallas_call | solution.py:1320
  247.4 47.2 %decoder_core.1 = (f32[512,768]{1,0:T(8,128)}, bf16[512,768]{1,0:T(8,128)(2,1)}, bf16[512,384]{1,0:T(8,128)(2,1)}, bf16[512,768]{1,0:T(8,128)(2,1)}, bf16[512,15...) custom-call(f32[512,768]{1,0:T(8,128)} %get-tuple-element.111.refs_0, ...), custom_call_target="tpu_custom_call" | custom-call | tf_op jit(solution)/shard_map/decoder_core/pallas_call | solution.py:1320
  294.7 12.3 %all-to-all-start = ((bf16[1,16,64,768]{3,2,0,1:T(8,128)(2,1)}), bf16[1,16,64,768]{3,2,0,1:T(8,128)(2,1)S(1)}, u32[]{:S(2)}, u32[]{:S(2)}) async-start(bf16[1,16,64,768]{3,2,0,1:T(8,128)(2,1)} %bitcast.61), calls=%async_computation | async-start | bytes 3145728 | tf_op jit(solution)/shard_map/all_to_all | solution.py:1736
  308.3 0.1 sub.42
  308.4 13.9 %decoder_self_backward.1 = (bf16[512,768]{1,0:T(8,128)(2,1)}, bf16[512,384]{1,0:T(8,128)(2,1)}, bf16[512,768]{1,0:T(8,128)(2,1)}, f32[512,768]{1,0:T(8,128)}, f32[1,1152]{1,0:T(1,128)}) custom-call(f32[512,768]{1,0:T(8,128)} %get-tuple-element.131.refs_0_, bf16[512,1152]{1,0:T(8,128)(2,1)} %get-tuple-element.132.refs_1_, ...), custom_call_target="tpu_custom_call" | custom-call | tf_op jit(solution)/shard_map/decoder_self_backward/pallas_call | solution.py:1320
  322.3 0.0 copy-done.8
  322.4 0.2 compare_reduce_fusion
  322.5 0.5 convert_element_type.48.refs_0_
  323.1 16.4 %weight_grads.2.refs_19_ = bf16[512,128,128]{2,1,0:T(8,128)(2,1)} custom-call(s32[504]{0:T(512)} %slots_ref.5, bf16[512,1536]{1,0:T(8,128)(2,1)} %get-tuple-element.152.refs_0_, bf16[512,768]{1,0:T(8,128)(2,1)} %get-tuple-element.153.refs_1_, bf16[512,768]{1,0:T(8,128)(2,1)} %get-tuple-element.154.refs_2_, bf16[512,1536]{1,0:T(8,128)(2,1)} %get-tuple-element.155.refs_3_, ...), custom_call_target="tpu_custom_call" | custom-call | tf_op jit(solution)/shard_map/weight_grads/pallas_call | solution.py:763
  339.4 1.8 all-to-all-done
  341.2 2.2 fusion.2.refs_0_
  343.4 31.0 %encoder_backward.1 = (bf16[512,768]{1,0:T(8,128)(2,1)}, bf16[512,1536]{1,0:T(8,128)(2,1)}, f32[1,1536]{1,0:T(1,128)}, f32[8,768]{1,0:T(8,128)}, f32[8,768]{1,0:...) custom-call(f32[512,768]{1,0:T(8,128)} %fusion.2.refs_0_, ...), custom_call_target="tpu_custom_call" | custom-call | tf_op jit(solution)/shard_map/encoder_backward/pallas_call | solution.py:1320
  374.4 14.0 %weight_grads.3 = (bf16[512,128,128]{2,1,0:T(8,128)(2,1)}, f32[24,768]{1,0:T(8,128)}) custom-call(s32[504]{0:T(512)} %slots_ref.5, bf16[512,1536]{1,0:T(8,128)(2,1)} %get-tuple-element.123.refs_3_.refs_0_, bf16[512,768]{1,0:T(8,128)(2,1)} %get-tuple-element.136.refs_1_, ...), custom_call_target="tpu_custom_call", output_to_operand_aliasing={{0}: (20, {})} | custom-call | tf_op jit(solution)/shard_map/weight_grads/pallas_call | solution.py:763
  388.4 0.0 copy-start.13
  388.5 0.0 copy-start.14
  388.5 0.0 copy-start.10
  388.5 0.0 copy-start.11
  388.5 0.0 copy-start.2
  388.5 0.0 copy-start.3
  388.5 173.2 %owner_update.1 = (f32[32,128,128]{2,1,0:T(8,128)}, f32[32,128,128]{2,1,0:T(8,128)}, f32[32,128,128]{2,1,0:T(8,128)}, f32[32,128,128]{2,1,0:T(8,128)}, f32[32,12...) custom-call(s32[32]{0:T(128)} %convert_element_type.48.refs_0_, ...), custom_call_target="tpu_custom_call" | custom-call | tf_op jit(solution)/shard_map/owner_update/pallas_call | solution.py:482
  561.7 0.0 copy-done.13
  561.7 0.0 copy-done.14
  561.7 0.8 subtract_bitcast_fusion
  562.5 0.6 copy.74
  563.1 0.6 copy.75
  563.7 0.6 copy.76
  564.3 0.0 copy-done.10
  564.3 0.0 copy-done.11
  564.3 1.4 divide_subtract_fusion
  565.7 0.0 copy-done.2
  565.7 0.0 copy-done.3
  565.7 4.8 fusion
  570.5 20.8 %last_bases.1 = (f32[32,128,128]{2,1,0:T(8,128)}, f32[32,128,128]{2,1,0:T(8,128)}, f32[32,128,128]{2,1,0:T(8,128)}, f32[32,128,128]{2,1,0:T(8,128)}, f32[32,128,...) custom-call(f32[16,128,256]{2,1,0:T(8,128)} %get-tuple-element.166.work_ref, ...), custom_call_target="tpu_custom_call" | custom-call | tf_op jit(solution)/shard_map/last_bases/pallas_call | solution.py:355
  591.3 0.0 copy-start.5
  591.3 0.0 copy-done.4
  591.3 0.0 copy-start.1
  591.3 1.1 copy.104
  592.5 0.8 copy-done.5
  593.3 1.1 copy.105
  (11 shorter events, 0.1 us)
Async XLA Ops:
  0.7 4.7 copy-start.12
  0.7 4.7 copy-start.9
  0.7 4.7 copy-start.7
  5.4 165.1 %copy-start.6 = (bf16[1024,768]{1,0:T(8,128)(2,1)S(1)}, bf16[1024,768]{1,0:T(8,128)(2,1)}, u32[]{:S(2)}) copy-start(bf16[1024,768]{1,0:T(8,128)(2,1)} %param.21) | copy-start | bytes 4718596
  294.7 46.6 %all-to-all-start = ((bf16[1,16,64,768]{3,2,0,1:T(8,128)(2,1)}), bf16[1,16,64,768]{3,2,0,1:T(8,128)(2,1)S(1)}, u32[]{:S(2)}, u32[]{:S(2)}) async-start(bf16[1,16,64,768]{3,2,0,1:T(8,128)(2,1)} %bitcast.61), calls=%async_computation | async-start | bytes 3145728 | tf_op jit(solution)/shard_map/all_to_all | solution.py:1736
  308.4 14.0 %copy-start.8 = (s32[504]{0:T(512)S(1)}, s32[504]{0:T(512)}, u32[]{:S(2)}) copy-start(s32[504]{0:T(512)} %slots_ref.5) | copy-start | bytes 6052
  388.4 173.2 %copy-start.13 = (f32[1,7,48]{2,0,1:T(1,128)S(1)}, f32[1,7,48]{2,0,1:T(1,128)}, u32[]{:S(2)}) copy-start(f32[1,7,48]{2,0,1:T(1,128)} %param.38) | copy-start | bytes 4036
  388.5 173.2 %copy-start.14 = (f32[1,7,48]{2,0,1:T(1,128)S(1)}, f32[1,7,48]{2,0,1:T(1,128)}, u32[]{:S(2)}) copy-start(f32[1,7,48]{2,0,1:T(1,128)} %param.39) | copy-start | bytes 4036
  388.5 175.8 %copy-start.10 = (f32[15,48]{1,0:T(8,128)S(1)}, f32[15,48]{1,0:T(8,128)}, u32[]{:S(2)}) copy-start(f32[15,48]{1,0:T(8,128)} %param.36) | copy-start | bytes 8644
  388.5 175.8 %copy-start.11 = (f32[15,48]{1,0:T(8,128)S(1)}, f32[15,48]{1,0:T(8,128)}, u32[]{:S(2)}) copy-start(f32[15,48]{1,0:T(8,128)} %param.35) | copy-start | bytes 8644
  388.5 177.2 %copy-start.2 = (f32[1024,768]{1,0:T(8,128)S(1)}, f32[1024,768]{1,0:T(8,128)}, u32[]{:S(2)}) copy-start(f32[1024,768]{1,0:T(8,128)} %get-tuple-element.107) | copy-start | bytes 9437188
  388.5 177.2 %copy-start.3 = (f32[1024,768]{1,0:T(8,128)S(1)}, f32[1024,768]{1,0:T(8,128)}, u32[]{:S(2)}) copy-start(f32[1024,768]{1,0:T(8,128)} %get-tuple-element.130) | copy-start | bytes 9437188
  570.5 20.8 %copy-start.4 = (f32[512,768]{1,0:T(8,128)S(1)}, f32[512,768]{1,0:T(8,128)}, u32[]{:S(2)}) copy-start(f32[512,768]{1,0:T(8,128)} %get-tuple-element.295) | copy-start | bytes 4718596
  591.3 2.0 copy-start.5
  591.3 3.1 copy-start.1
  (1 other events, 0.0 us)

commit v4 on v3

--- a/solution.py
+++ b/solution.py
@@ -492,7 +492,7 @@
     return last_bases(results[8], results[:7]), results[7]
 
 
-def ag_kernel(grid, own_ref, small_ref, out_ref, small_out_ref,
+def ag_kernel(grid, wide_ref, small_ref, out_ref, small_out_ref, own_ref,
               load_sem, z_send, z_recv, b_send0, b_send1, b_recv0, b_recv1, a_send0, a_send1, a_recv0, a_recv1,
               s_load, ssz, ssy, ssx, srz, sry, srx):
     zs, ys, xs = grid
@@ -528,6 +528,7 @@
             source = target = small_out_ref.at[:, y, x] if axis == 1 else small_out_ref.at[:, :, x]
         return remote(source, target, s_send[axis].at[k - 1], s_recv[axis].at[k - 1], tos[axis](k))
 
+    own_ref[...] = wide_ref[...].astype(BF16)
     keep = pltpu.make_async_copy(own_ref, out_ref.at[z, y, x], load_sem)
     keep_small = pltpu.make_async_copy(small_ref, small_out_ref.at[z, y, x], s_load)
     keep.start()
@@ -600,7 +601,7 @@
     dma = pltpu.SemaphoreType.DMA
     firsts, seconds = (xs, ys), (ys, xs)
     scratch = (
-        [dma, dma(some((2, chunks, zs - 1))), dma(some((2, chunks, zs - 1)))]
+        [pltpu.VMEM(own.shape, BF16), dma, dma(some((2, chunks, zs - 1))), dma(some((2, chunks, zs - 1)))]
         + [dma(some((chunks, seconds[g] - 1))) for g in range(2)] * 2
         + [dma(some((chunks, firsts[g] - 1))) for g in range(2)] * 2
         + [dma]
@@ -608,11 +609,11 @@
     )
     blocks, smalls = pl.pallas_call(
         functools.partial(ag_kernel, grid),
-        out_shape=[jax.ShapeDtypeStruct(grid + own.shape, own.dtype), jax.ShapeDtypeStruct(grid + small.shape, small.dtype)],
+        out_shape=[jax.ShapeDtypeStruct(grid + own.shape, BF16), jax.ShapeDtypeStruct(grid + small.shape, small.dtype)],
         in_specs=[pl.BlockSpec(memory_space=pltpu.VMEM)] * 2,
         out_specs=[ANY, ANY],
         scratch_shapes=scratch,
-        compiler_params=pltpu.CompilerParams(collective_id=2, has_side_effects=True),
+        compiler_params=pltpu.CompilerParams(collective_id=2, has_side_effects=True, vmem_limit_bytes=56 << 20),
         name="gather_all",
     )(own, small)
     return blocks.reshape((-1,) + own.shape[1:]), smalls.reshape((-1,) + small.shape)
@@ -1065,7 +1066,7 @@
 
 
 def feed_forward_kernel(
-    kept, unit_ref, up_ref, down_ref, bias_ref, vec_ref,
+    kept, between, unit_ref, up_ref, down_ref, bias_ref, vec_ref,
     states_ref, states_low_ref, low_ref, active_ref, slope_ref, unit_out_ref, scale_ref, *swap_refs,
 ):
     swap = Swap(*swap_refs)
@@ -1092,10 +1093,6 @@
         swap.give(t, total)
         return carry
 
-    lax.fori_loop(0, kept_tiles, functools.partial(feed, keep=True), 0)
-    if kept_tiles < tiles:
-        lax.fori_loop(kept_tiles, tiles, functools.partial(feed, keep=False), 0)
-
     def take(t, carry, keep):
         rows = rows_of(t)
         hidden = unit_ref[rows, :] * vec_ref[0:1, :] + vec_ref[1:2, :]
@@ -1108,8 +1105,11 @@
             scale_ref[rows, :] = scale
         return carry
 
+    lax.fori_loop(0, kept_tiles, functools.partial(feed, keep=True), 0)
     lax.fori_loop(0, kept_tiles, functools.partial(take, keep=True), 0)
+    between()
     if kept_tiles < tiles:
+        lax.fori_loop(kept_tiles, tiles, functools.partial(feed, keep=False), 0)
         lax.fori_loop(kept_tiles, tiles, functools.partial(take, keep=False), 0)
 
 
@@ -1218,7 +1218,7 @@
 
 
 def cross_backward_kernel(
-    grad_pre_ref, query_ref, mixed_ref, attended_ref, totals_ref, query_weight_ref, wide_ref, out_weight_ref,
+    between, grad_pre_ref, query_ref, mixed_ref, attended_ref, totals_ref, query_weight_ref, wide_ref, out_weight_ref,
     unit_ref, scale_ref, vec_ref,
     low_ref, grad_query_ref, grad_pair_ref, fetched_ref, grad_out_ref, sums_ref, vec_sums_ref,
     grad_ref, turned_ref, *swap_refs,
@@ -1257,6 +1257,7 @@
         return carry
 
     lax.fori_loop(0, keys // ROWS, take_far, 0)
+    between()
 
     def take_near(t, carry):
         rows = rows_of(t)
@@ -1279,7 +1280,7 @@
     return rows % 16 == 0 and width % TILE == 0 and rows * width * array.dtype.itemsize >= 1 << 18
 
 
-def call(name, ident, body, inputs, outputs, scratch):
+def call(name, ident, body, inputs, outputs, scratch, mib=56):
     ins = [i for i, array in enumerate(inputs) if streams(array)]
     outs = [i for i, array in enumerate(outputs) if streams(array)]
     count_in, count_out = len(inputs), len(outputs)
@@ -1326,45 +1327,9 @@
         + [pltpu.VMEM(outputs[i].shape, outputs[i].dtype) for i in outs]
         + [pltpu.SemaphoreType.DMA((count_in,)), pltpu.SemaphoreType.DMA((count_out,))]
         + scratch,
-        compiler_params=params(ident),
+        compiler_params=params(ident, mib),
         name=name,
     )(*inputs)
-
-
-def encoder_forward(ident, x, wide, out_weight, up, down, shared, split, kept):
-    length, width = x.shape
-    half, hidden_half = out_weight.shape[0], up.shape[1]
-    tiles, span = length // ROWS, min(length, 512)
-    places = bias_places(half, hidden_half)
-
-    def body(need, done, x_ref, wide_ref, out_weight_ref, up_ref, down_ref, shared_ref, split_ref, *refs):
-        saved, fed, rest = refs[:5], refs[5:12], refs[12:]
-        need(0, 1, 2)
-        Swap.greet()
-        self_forward_kernel(
-            False, span, x_ref, wide_ref, out_weight_ref,
-            bias_row(split_ref, places, ("enc_q", None, "enc_v"), half), Rows(shared_ref, (0,)),
-            *saved, *rest[:6],
-        )
-        done(0, 1, 2, 3, 4)
-        need(3, 4, 5, 6)
-        feed_forward_kernel(
-            kept, saved[3], up_ref, down_ref, split_ref.at[:, places["enc_up"]],
-            Rows(shared_ref, (1, 2, 3, 4, 5)), *fed, *rest[6:],
-        )
-        done(*range(5, 12))
-
-    return call(
-        "encoder_forward", ident, body, [x, wide, out_weight, up, down, shared, split],
-        [
-            shape(length, 3 * half, dtype=BF16), shape(length, half, dtype=BF16), shape(8, length),
-            shape(length, width), shape(length, 1),
-            shape(length, width), shape(kept, width, dtype=BF16), shape(kept, width, dtype=BF16),
-            shape(kept, hidden_half, dtype=BF16), shape(kept, hidden_half, dtype=BF16),
-            shape(kept, width), shape(kept, 1),
-        ],
-        [held(2, length, span), held(half, length, dtype=BF16)] + Swap.scratch(tiles, width) * 2,
-    )
 
 
 class Trade:
@@ -1396,10 +1361,13 @@
     def mine(self):
         return pl.ds(pl.multiple_of(self.core * self.half, self.half), self.half)
 
+    def lanes_of(self, source):
+        return self.mine() if source.shape[1] == self.into.shape[1] else slice(None)
+
     def send(self, source, k):
         other = lax.rem(self.me + k, self.count)
         return pltpu.make_async_remote_copy(
-            src_ref=source.at[self.rows_of(other), :],
+            src_ref=source.at[self.rows_of(other), self.lanes_of(source)],
             dst_ref=self.into.at[self.rows_of(self.me), self.mine()],
             send_sem=self.send_sem.at[k],
             recv_sem=self.recv_sem.at[k],
@@ -1424,7 +1392,7 @@
             return carry
 
         lax.fori_loop(1, self.count, go, 0)
-        self.into[self.rows_of(self.me), self.mine()] = source[self.rows_of(self.me), :]
+        self.into[self.rows_of(self.me), self.mine()] = source[self.rows_of(self.me), self.lanes_of(source)]
         self.pass_on(0).start()
 
     def finish(self, source):
@@ -1448,55 +1416,84 @@
         lax.fori_loop(1, self.count, sent, 0)
 
 
-def fetch_and_self_forward(ident, stored, wanted, x, wide, out_weight, shared, split, hidden_half, count):
+def encoder_and_fetch(
+    ident, x, wide, out_weight, up, down, shared, split, kept, wanted, target, dec_wide, dec_out_weight, count
+):
     length, width = x.shape
-    half = out_weight.shape[0]
-    span = min(length, 512)
+    half, hidden_half = out_weight.shape[0], up.shape[1]
+    tiles, span = length // ROWS, min(length, 512)
+    target_length = target.shape[0]
+    target_span = min(target_length, span)
     fetched_rows = wanted.shape[0]
     places = bias_places(half, hidden_half)
 
     def body(
-        need, done, stored_ref, wanted_ref, x_ref, wide_ref, out_weight_ref, shared_ref, split_ref,
-        mixed_ref, attended_ref, totals_ref, unit_ref, scale_ref, fetched_ref,
-        served_ref, landed_ref, send_sem, recv_sem, give_sem, take_sem, *rest,
+        need, done, x_ref, wide_ref, out_weight_ref, up_ref, down_ref, shared_ref, split_ref, wanted_ref,
+        target_ref, dec_wide_ref, dec_out_weight_ref, *refs,
     ):
-        trade = Trade(count, landed_ref, send_sem, recv_sem, give_sem, take_sem)
-        need(0, 1)
+        saved, fed, dec_saved, fetched_ref, rest = refs[:5], refs[5:12], refs[12:17], refs[17], refs[18:]
+        served_ref, trade_sems, rest = rest[0], rest[1:5], rest[5:]
+        score_ref, turned_ref, rest = rest[0], rest[1], rest[2:]
+        trade = Trade(count, fetched_ref, *trade_sems)
+        stored_ref = fed[1]
+        need(0, 1, 2)
+        trade.greet()
+        self_forward_kernel(
+            False, span, x_ref, wide_ref, out_weight_ref,
+            bias_row(split_ref, places, ("enc_q", None, "enc_v"), half), Rows(shared_ref, (0,)),
+            *saved, score_ref, turned_ref, *rest[:4],
+        )
+        done(0, 1, 2, 3, 4)
+        need(3, 4, 5, 6, 7)
 
         def serve(t, carry):
             want = wanted_ref[rows_of(t), :]
-            match = want == lax.broadcasted_iota(jnp.int32, (ROWS, stored_ref.shape[0]), 1)
+            match = want == lax.broadcasted_iota(jnp.int32, (ROWS, kept), 1)
             pick = jnp.where(match, 1.0, 0.0).astype(BF16)
             served_ref[rows_of(t), :] = times(pick, stored_ref[:, trade.mine()]).astype(BF16)
             return carry
 
-        lax.fori_loop(0, fetched_rows // ROWS, serve, 0)
-        trade.greet()
-        trade.start(served_ref)
-        need(2, 3, 4)
+        def between():
+            lax.fori_loop(0, fetched_rows // ROWS, serve, 0)
+            trade.start(served_ref)
+            done(6, 7, 8, 9, 10, 11)
+
+        feed_forward_kernel(
+            kept, between, saved[3], up_ref, down_ref, split_ref.at[:, places["enc_up"]],
+            Rows(shared_ref, (1, 2, 3, 4, 5)), *fed, *rest[4:8],
+        )
+        done(5)
+        need(8, 9, 10)
         self_forward_kernel(
-            True, span, x_ref, wide_ref, out_weight_ref,
+            True, target_span, target_ref, dec_wide_ref, dec_out_weight_ref,
             bias_row(split_ref, places, ("dec_q", None, "dec_v"), half), Rows(shared_ref, (6,)),
-            mixed_ref, attended_ref, totals_ref, unit_ref, scale_ref, *rest,
+            *dec_saved, score_ref.at[:, :, :target_span], turned_ref.at[:, :target_length], *rest[8:],
         )
-        done(0, 1, 2, 3, 4)
+        done(12, 13, 14, 15, 16)
         trade.finish(served_ref)
-        fetched_ref[...] = landed_ref[...]
-        done(5)
+        done(17)
 
     return call(
-        "fetch_and_self_forward", ident, body, [stored, wanted, x, wide, out_weight, shared, split],
+        "encoder_and_fetch", ident, body,
+        [x, wide, out_weight, up, down, shared, split, wanted, target, dec_wide, dec_out_weight],
         [
             shape(length, 3 * half, dtype=BF16), shape(length, half, dtype=BF16), shape(8, length),
-            shape(length, width), shape(length, 1), shape(fetched_rows, width, dtype=BF16),
+            shape(length, width), shape(length, 1),
+            shape(length, width), shape(kept, width, dtype=BF16), shape(kept, width, dtype=BF16),
+            shape(kept, hidden_half, dtype=BF16), shape(kept, hidden_half, dtype=BF16),
+            shape(kept, width), shape(kept, 1),
+            shape(target_length, 3 * half, dtype=BF16), shape(target_length, half, dtype=BF16), shape(8, target_length),
+            shape(target_length, width), shape(target_length, 1), shape(fetched_rows, width, dtype=BF16),
         ],
-        [held(fetched_rows, width // 2, dtype=BF16), held(fetched_rows, width, dtype=BF16)] + Trade.scratch(count)
-        + [held(2, length, span), held(half, length, dtype=BF16)] + Swap.scratch(length // ROWS, width),
+        [held(fetched_rows, width // 2, dtype=BF16)] + Trade.scratch(count)
+        + [held(2, length, span), held(half, length, dtype=BF16)]
+        + Swap.scratch(tiles, width) * 2 + Swap.scratch(target_length // ROWS, width),
     )
 
 
 def decoder_core(
-    ident, unit, scale, fetched, cotangent, query_weight, wide, out_weight, up, down, shared, split
+    ident, unit, scale, fetched, cotangent, query_weight, wide, out_weight, up, down, shared, split,
+    mixed, attended, totals, self_wide, self_out_weight, count,
 ):
     length, width = unit.shape
     keys = fetched.shape[0]
@@ -1507,14 +1504,18 @@
     def body(
         need, done, unit_ref, scale_ref, fetched_ref, cotangent_ref, query_weight_ref, wide_ref, out_weight_ref,
         up_ref, down_ref, shared_ref, split_ref,
+        self_mixed_ref, self_attended_ref, self_totals_ref, self_wide_ref, self_out_weight_ref,
         states_ref, low_ref, attended_ref, second_low_ref, active_ref,
         feed_low_ref, grad_up_ref, up_bias_ref, sums_after_ref, sums_before_ref,
-        cross_low_ref, grad_query_ref, grad_pair_ref, returned_ref, grad_out_ref, cross_sums_ref, vec_sums_ref,
-        query_ref, mixed_ref, totals_ref, unit_four_ref, scale_four_ref, states_low_ref, slope_ref,
-        unit_five_ref, scale_five_ref, grad_four_ref, inner_ref, score_ref, turned_ref, grad_ref, *swaps,
+        cross_low_ref, grad_query_ref, grad_pair_ref, landed_ref, cross_sums_ref, vec_sums_ref,
+        self_low_ref, self_query_ref, self_pair_ref, grad_x_ref, self_sums_ref,
+        query_ref, mixed_ref, totals_ref, unit_four_ref, scale_four_ref, slope_ref,
+        unit_five_ref, scale_five_ref, grad_four_ref, inner_ref, score_ref, turned_ref, grad_ref, returned_ref, grad_out_ref,
+        send_sem, recv_sem, give_sem, take_sem, *swaps,
     ):
         need(0, 1, 2, 4, 5, 6, 9, 10)
-        Swap.greet()
+        trade = Trade(count, landed_ref, send_sem, recv_sem, give_sem, take_sem)
+        trade.greet()
         cross_forward_kernel(
             span, unit_ref, fetched_ref, query_weight_ref, wide_ref, out_weight_ref,
             split_ref.at[:, places["crs_q"]], bias_row(split_ref, places, (None, "crs_v"), half),
@@ -1525,9 +1526,9 @@
         done(1, 2)
         need(7, 8)
         feed_forward_kernel(
-            length, unit_four_ref, up_ref, down_ref, split_ref.at[:, places["dec_up"]],
+            length, lambda: None, unit_four_ref, up_ref, down_ref, split_ref.at[:, places["dec_up"]],
             Rows(shared_ref, (10, 11, 12, 13, 14)),
-            states_ref, states_low_ref, second_low_ref, active_ref, slope_ref, unit_five_ref, scale_five_ref,
+            states_ref, cross_low_ref, second_low_ref, active_ref, slope_ref, unit_five_ref, scale_five_ref,
             *swaps[4:8],
         )
         done(0, 3, 4)
@@ -1540,70 +1541,75 @@
         )
         done(5, 6, 7, 8, 9)
         cross_backward_kernel(
-            grad_four_ref, query_ref, mixed_ref, attended_ref, totals_ref, query_weight_ref, wide_ref,
+            lambda: trade.start(returned_ref), grad_four_ref, query_ref, mixed_ref, attended_ref, totals_ref, query_weight_ref, wide_ref,
             out_weight_ref, unit_ref, scale_ref, Rows(shared_ref, (7,)),
             cross_low_ref, grad_query_ref, grad_pair_ref, returned_ref, grad_out_ref, cross_sums_ref, vec_sums_ref,
-            grad_ref, turned_ref, *swaps[12:],
+            grad_ref, turned_ref, *swaps[12:20],
         )
-        done(*range(10, 17))
+        done(10, 11, 12, 14, 15)
+        need(11, 12, 13, 14, 15)
+        self_backward_kernel(
+            True, grad_out_ref, self_mixed_ref, self_attended_ref, self_totals_ref, self_wide_ref, self_out_weight_ref,
+            self_low_ref, self_query_ref, self_pair_ref, grad_x_ref, self_sums_ref,
+            grad_ref, turned_ref.at[:, :length], *swaps[20:],
+        )
+        done(16, 17, 18, 19, 20)
+        trade.finish(returned_ref)
+        done(13)
 
     return call(
         "decoder_core", ident, body,
-        [unit, scale, fetched, cotangent, query_weight, wide, out_weight, up, down, shared, split],
+        [
+            unit, scale, fetched, cotangent, query_weight, wide, out_weight, up, down, shared, split,
+            mixed, attended, totals, self_wide, self_out_weight,
+        ],
         [
             shape(length, width), shape(length, width, dtype=BF16), shape(length, half, dtype=BF16),
             shape(length, width, dtype=BF16), shape(length, hidden_half, dtype=BF16),
             shape(length, width, dtype=BF16), shape(length, hidden_half, dtype=BF16), shape(1, hidden_half),
             shape(8, width), shape(8, width),
             shape(length, width, dtype=BF16), shape(length, half, dtype=BF16), shape(keys, 2 * half, dtype=BF16),
-            shape(keys, width, dtype=BF16), shape(length, width), shape(1, 3 * half), shape(8, width),
+            shape(keys, width, dtype=BF16), shape(1, 3 * half), shape(8, width),
+            shape(length, width, dtype=BF16), shape(length, half, dtype=BF16), shape(length, 2 * half, dtype=BF16),
+            shape(length, width), shape(1, 3 * half),
         ],
         [
             held(length, half, dtype=BF16), held(keys, 2 * half, dtype=BF16), held(8, length),
-            held(length, width), held(length, 1), held(length, width, dtype=BF16),
+            held(length, width), held(length, 1),
             held(length, hidden_half, dtype=BF16), held(length, width), held(length, 1),
             held(length, width), held(length, width), held(2, keys, span), held(half, keys, dtype=BF16),
-            held(length, half, dtype=BF16),
+            held(length, half, dtype=BF16), held(keys, width, dtype=BF16), held(length, width),
         ]
-        + Swap.scratch(tiles, width) * 4 + Swap.scratch(keys // ROWS, width),
-    )
-
-
-def decoder_self_backward(ident, grad_pre, mixed, attended, totals, wide, out_weight):
-    queries, width = grad_pre.shape
-    length, half = mixed.shape[0], out_weight.shape[0]
-
-    def body(need, done, *refs):
-        need(*range(6))
-        Swap.greet()
-        self_backward_kernel(True, *refs)
-        done(*range(5))
-
-    return call(
-        "decoder_self_backward", ident, body, [grad_pre, mixed, attended, totals, wide, out_weight],
-        [
-            shape(queries, width, dtype=BF16), shape(queries, half, dtype=BF16), shape(length, 2 * half, dtype=BF16),
-            shape(length, width), shape(1, 3 * half),
-        ],
-        [held(queries, half, dtype=BF16), held(half, length, dtype=BF16)] + Swap.scratch(length // ROWS, width),
+        + Trade.scratch(count)
+        + Swap.scratch(tiles, width) * 4 + Swap.scratch(keys // ROWS, width) + Swap.scratch(tiles, width),
+        60,
     )
 
 
 def encoder_backward(
-    ident, grad, unit_two, scale_two, active, slope, up, down, unit_one, scale_one,
+    ident, returned, wanted, unit_two, scale_two, active, slope, up, down, unit_one, scale_one,
     mixed, attended, totals, wide, out_weight, shared,
 ):
-    queries, width = grad.shape
+    queries, width = unit_two.shape
     length, half, hidden_half = mixed.shape[0], out_weight.shape[0], up.shape[1]
 
     def body(
-        need, done, grad_ref, unit_two_ref, scale_two_ref, active_ref, slope_ref, up_ref, down_ref, unit_one_ref, scale_one_ref,
+        need, done, returned_ref, wanted_ref, unit_two_ref, scale_two_ref, active_ref, slope_ref, up_ref, down_ref, unit_one_ref, scale_one_ref,
         mixed_ref, attended_ref, totals_ref, wide_ref, out_weight_ref, shared_ref,
         feed_low_ref, grad_up_ref, up_bias_ref, sums_after_ref, sums_before_ref,
         low_ref, grad_query_ref, grad_pair_ref, grad_x_ref, sums_ref,
-        grad_one_ref, inner_ref, grad_out_ref, turned_ref, *swaps,
+        grad_ref, grad_one_ref, inner_ref, grad_out_ref, turned_ref, *swaps,
     ):
-        need(*range(9), 14)
+        need(0, 1)
+
+        def collect(t, carry):
+            place = t * ROWS + lax.broadcasted_iota(jnp.int32, (ROWS, returned_ref.shape[0]), 0)
+            match = jnp.where(wanted_ref[...] == place, 1.0, 0.0).astype(BF16)
+            grad_ref[rows_of(t), :] = times(match, returned_ref[...])
+            return carry
+
+        lax.fori_loop(0, queries // ROWS, collect, 0)
+        need(*range(2, 10), 15)
         Swap.greet()
         feed_backward_kernel(
             grad_ref, unit_two_ref, scale_two_ref, active_ref, slope_ref, up_ref, down_ref,
@@ -1612,7 +1618,7 @@
             inner_ref, *swaps[:4],
         )
         done(0, 1, 2, 3, 4)
-        need(9, 10, 11, 12, 13)
+        need(10, 11, 12, 13, 14)
         self_backward_kernel(
             False, grad_one_ref, mixed_ref, attended_ref, totals_ref, wide_ref, out_weight_ref,
             low_ref, grad_query_ref, grad_pair_ref, grad_x_ref, sums_ref, grad_out_ref, turned_ref, *swaps[4:],
@@ -1622,7 +1628,7 @@
     return call(
         "encoder_backward", ident, body,
         [
-            grad, unit_two, scale_two, active, slope, up, down, unit_one, scale_one,
+            returned, wanted, unit_two, scale_two, active, slope, up, down, unit_one, scale_one,
             mixed, attended, totals, wide, out_weight, shared,
         ],
         [
@@ -1632,7 +1638,7 @@
             shape(length, width), shape(1, 3 * half),
         ],
         [
-            held(queries, width), held(queries, width), held(queries, half, dtype=BF16),
+            held(queries, width), held(queries, width), held(queries, width), held(queries, half, dtype=BF16),
             held(half, length, dtype=BF16),
         ]
         + Swap.scratch(queries // ROWS, width) + Swap.scratch(length // ROWS, width),
@@ -1691,7 +1697,7 @@
         ],
         0,
     )
-    gathered, smalls = gather_all(master[0].astype(jnp.bfloat16), small, device_count)
+    gathered, smalls = gather_all(master[0], small, device_count)
     whole = (
         smalls[:, :vector_count, :vector_width]
         .transpose(1, 0, 2)
@@ -1708,12 +1714,6 @@
     start_row = jnp.argmax(kept_mask)
     turned = jnp.roll(source_tokens, -start_row, 0)
 
-    (enc_mixed, enc_attended, enc_totals, unit_one, scale_one,
-     states, stored, hidden_low, enc_active, enc_slope, unit_two, scale_two) = encoder_forward(
-        10, turned, weights["enc_qkv"], weights["enc_out"], weights["enc_up"], weights["enc_down"],
-        shared, split, KEEP,
-    )
-    encoder_states = jnp.roll(states, start_row, 0)
 
     wanted = (
         smalls[:, padded:].reshape(device_count, qblocks, device_count, per_owner)[:, :, me]
@@ -1721,31 +1721,24 @@
         .astype(jnp.int32)
         - KEEP * me
     ).reshape(1, -1)
-    matches = (wanted == lax.broadcasted_iota(jnp.int32, (KEEP, 1), 0)).astype(BF16)
-    dec_mixed, dec_attended, dec_totals, unit_three, scale_three, fetched = fetch_and_self_forward(
-        12, stored, wanted.reshape(-1, 1), target_tokens, weights["dec_qkv"], weights["dec_out"],
-        shared, split, hidden_half, device_count,
-    )
+    (enc_mixed, enc_attended, enc_totals, unit_one, scale_one,
+     states, _, hidden_low, enc_active, enc_slope, unit_two, scale_two,
+     dec_mixed, dec_attended, dec_totals, unit_three, scale_three, fetched) = encoder_and_fetch(
+        10, turned, weights["enc_qkv"], weights["enc_out"], weights["enc_up"], weights["enc_down"],
+        shared, split, KEEP, wanted.reshape(-1, 1), target_tokens, weights["dec_qkv"], weights["dec_out"], device_count,
+    )
+    encoder_states = jnp.roll(states, start_row, 0)
     (decoder_states, first_low, crs_attended, second_low, dec_active,
      dec_feed_low, dec_grad_up, dec_up_bias, sums_five, sums_four,
-     crs_low, crs_grad_query, crs_grad_pair, fetched_low, grad_three, crs_sums, sums_three) = decoder_core(
+     crs_low, crs_grad_query, crs_grad_pair, returned, crs_sums, sums_three,
+     dec_low, dec_grad_query, dec_grad_pair, target_grad, dec_sums) = decoder_core(
         13, unit_three, scale_three, fetched, target_cotangent,
         weights["crs_q"], weights["crs_kv"], weights["crs_out"], weights["dec_up"], weights["dec_down"],
-        shared, split,
-    )
-    returned = lax.all_to_all(
-        fetched_low.reshape(qblocks, device_count, per_owner, model_width),
-        "dp", split_axis=1, concat_axis=1, tiled=True,
-    )
-    dec_low, dec_grad_query, dec_grad_pair, target_grad, dec_sums = decoder_self_backward(
-        17, grad_three, dec_mixed, dec_attended, dec_totals, weights["dec_qkv"], weights["dec_out"]
-    )
-    stored_grad = jnp.einsum(
-        "ka,ab->kb", matches, returned.reshape(-1, model_width), preferred_element_type=F32
+        shared, split, dec_mixed, dec_attended, dec_totals, weights["dec_qkv"], weights["dec_out"], device_count,
     )
     (enc_feed_low, enc_grad_up, enc_up_bias, sums_two, sums_one,
      enc_low, enc_grad_query, enc_grad_pair, grad_turned, enc_sums) = encoder_backward(
-        18, stored_grad, unit_two, scale_two, enc_active, enc_slope, weights["enc_up"], weights["enc_down"],
+        18, returned, wanted, unit_two, scale_two, enc_active, enc_slope, weights["enc_up"], weights["enc_down"],
         unit_one, scale_one, enc_mixed, enc_attended, enc_totals, weights["enc_qkv"], weights["enc_out"], shared,
     )
     source_grad = jnp.roll(grad_turned, start_row, 0)

time: 604 us -> 590 us (0.977)
  starting transfers between devices: 12.3 us -> 0 us
    all_to_all x1 -> x0, starting transfers between devices: 12.3 us -> none  [local(): lax.all_to_all(fetched_low.reshape(qblocks, device_count, per_owner, mode...]
    pallas_call x5 -> x3, Pallas kernels: 153 us -> 151 us  [call(): pl.pallas_call(kernel, out_shape=outputs, in_specs=[ANY if i in ins else...]
  transfers between devices with their start and end apart: 1 -> 0, of which waited for: 1 -> 0; matrix products, arithmetic and copies ran while one was open for 0% -> 0% of each run, Pallas kernels for 5% -> 0%
where the time goes in v4:
time: 590 us; the launch traced here: 582 us
  Pallas kernels  551 us (93%)
  other arithmetic  18.6 us (3%)
  local copies, waits for them, and re-layouts  8.2 us (1%)
    pallas_call x1, Pallas kernels, owner_update(): pl.pallas_call(functools.partial(owner_kernel, grid), out_shape=[jax.Shap...  178 us
    pallas_call x1, Pallas kernels, gather_all(): pl.pallas_call(functools.partial(ag_kernel, grid), out_shape=[jax.ShapeDt...  159 us
    pallas_call x3, Pallas kernels, call(): pl.pallas_call(kernel, out_shape=outputs, in_specs=[ANY if i in ins else...  151 us
    pallas_call x2, Pallas kernels, weight_grads(): pl.pallas_call(functools.partial(weight_grads_kernel, plan, len(arrays),...  30.4 us
    pallas_call x1, Pallas kernels, last_bases(): pl.pallas_call(last_bases_kernel, out_shape=[jax.ShapeDtypeStruct(whole,...  20.8 us
    pallas_call x1, Pallas kernels, unpack_tiles(): pl.pallas_call(functools.partial(unpack_kernel, shapes), out_shape=[jax.S...  12.3 us

profile of v4, /device:TPU:0, one launch (start us, length us, event | category | flops | bytes accessed | tf_op | source)
XLA Modules:
  0.0 581.8 jit_solution(18396347949826352574)
XLA Ops:
  0.7 0.0 copy-start
  0.7 0.9 compare_reduce_fusion
  1.6 0.5 convert_element_type.46.refs_0_
  2.1 0.0 copy-done
  2.1 0.7 iota_reduce_fusion
  5.4 0.7 convert_element_type.42
  6.0 0.7 copy.89
  6.7 0.7 select_maximum_fusion
  7.4 0.6 pad_maximum_fusion.small_ref
  8.0 4.0 fusion.2.refs_0_.refs_6_
  12.1 159.3 %gather_all.1 = (bf16[4,2,2,32,128,128]{5,4,3,2,1,0:T(8,128)(2,1)}, f32[4,2,2,32,128]{4,3,2,1,0:T(8,128)}) custom-call(f32[32,128,128]{2,1,0:T(8,128)} %bitcast.48, f32[32,128]{1,0:T(8,128)} %pad_maximum_fusion.small_ref), custom_call_target="tpu_custom_call" | custom-call | tf_op jit(solution)/shard_map/gather_all/pallas_call | solution.py:610
  171.4 0.0 copy-start.5
  171.4 12.3 %unpack_tiles.1 = (bf16[768,1152]{1,0:T(8,128)(2,1)}, bf16[384,768]{1,0:T(8,128)(2,1)}, bf16[768,1536]{1,0:T(8,128)(2,1)}, bf16[1536,768]{1,0:T(8,128)(2,1)}, bf...) custom-call(s32[504]{0:T(512)} %slots_ref.5, ...), custom_call_target="tpu_custom_call" | custom-call | tf_op jit(solution)/shard_map/unpack_tiles/pallas_call | solution.py:650
  183.7 0.0 copy-done.5
  183.8 0.7 reshape.117.refs_6_.refs_10_
  184.5 0.1 convert_element_type.44
  184.7 0.6 pad_convert_fusion.refs_5_.refs_9_.refs_15_
  185.3 0.1 reshape.114
  185.4 0.5 broadcast.58
  185.9 0.7 fusion.9
  186.6 0.7 sub.45.refs_1_
  187.2 1.3 sub.51.refs_7_
  188.5 52.3 %encoder_and_fetch.1 = (bf16[1024,1152]{1,0:T(8,128)(2,1)}, bf16[1024,384]{1,0:T(8,128)(2,1)}, f32[8,1024]{1,0:T(8,128)}, f32[1024,768]{1,0:T(8,128)}, f32[1024,...) custom-call(bf16[1024,768]{1,0:T(8,128)(2,1)} %fusion.2.refs_0_.refs, ...), custom_call_target="tpu_custom_call" | custom-call | tf_op jit(solution)/shard_map/encoder_and_fetch/pallas_call | solution.py:1321
  240.8 67.5 %decoder_core.1 = (f32[512,768]{1,0:T(8,128)}, bf16[512,768]{1,0:T(8,128)(2,1)}, bf16[512,384]{1,0:T(8,128)(2,1)}, bf16[512,768]{1,0:T(8,128)(2,1)}, bf16[512,15...) custom-call(f32[512,768]{1,0:T(8,128)} %get-tuple-element.108.refs_0, ...), custom_call_target="tpu_custom_call" | custom-call | tf_op jit(solution)/shard_map/decoder_core/pallas_call | solution.py:1321
  308.3 0.0 copy-start.2
  308.4 31.0 %encoder_backward.1 = (bf16[512,768]{1,0:T(8,128)(2,1)}, bf16[512,1536]{1,0:T(8,128)(2,1)}, f32[1,1536]{1,0:T(1,128)}, f32[8,768]{1,0:T(8,128)}, f32[8,768]{1,0:...) custom-call(bf16[1024,768]{1,0:T(8,128)(2,1)} %get-tuple-element.120, ...), custom_call_target="tpu_custom_call" | custom-call | tf_op jit(solution)/shard_map/encoder_backward/pallas_call | solution.py:1321
  339.3 0.0 copy-done.2
  339.3 6.9 %fusion = (f32[1024,768]{1,0:T(8,128)}, f32[1024,768]{1,0:T(8,128)}) fusion(s32[]{:T(128)S(6)} %select_n.37, f32[1024,768]{1,0:T(8,128)} %get-tuple-element.130, f32[1024,768]{1,0:T(8,128)S(1)} %copy-done.2), kind=kLoop, calls=%fused_computation.4 | loop fusion | flops 1572864 | bytes 12582916 | tf_op jit(solution)/shard_map/jit(_roll_dynamic)/concatenate | solution.py:1744
  346.2 16.4 %weight_grads.2.refs_19_ = bf16[512,128,128]{2,1,0:T(8,128)(2,1)} custom-call(s32[504]{0:T(512)} %slots_ref.5, bf16[512,1536]{1,0:T(8,128)(2,1)} %get-tuple-element.148.refs_0_, bf16[512,768]{1,0:T(8,128)(2,1)} %get-tuple-element.149.refs_1_, bf16[512,768]{1,0:T(8,128)(2,1)} %get-tuple-element.150.refs_2_, bf16[512,1536]{1,0:T(8,128)(2,1)} %get-tuple-element.151.refs_3_, ...), custom_call_target="tpu_custom_call" | custom-call | tf_op jit(solution)/shard_map/weight_grads/pallas_call | solution.py:764
  362.6 14.0 %weight_grads.3 = (bf16[512,128,128]{2,1,0:T(8,128)(2,1)}, f32[24,768]{1,0:T(8,128)}) custom-call(s32[504]{0:T(512)} %slots_ref.5, bf16[512,1536]{1,0:T(8,128)(2,1)} %get-tuple-element.123.refs_4_.refs_0_, bf16[512,768]{1,0:T(8,128)(2,1)} %get-tuple-element.132.refs_1_, ...), custom_call_target="tpu_custom_call", output_to_operand_aliasing={{0}: (20, {})} | custom-call | tf_op jit(solution)/shard_map/weight_grads/pallas_call | solution.py:764
  376.6 177.7 %owner_update.1 = (f32[32,128,128]{2,1,0:T(8,128)}, f32[32,128,128]{2,1,0:T(8,128)}, f32[32,128,128]{2,1,0:T(8,128)}, f32[32,128,128]{2,1,0:T(8,128)}, f32[32,12...) custom-call(s32[32]{0:T(128)} %convert_element_type.46.refs_0_, ...), custom_call_target="tpu_custom_call" | custom-call | tf_op jit(solution)/shard_map/owner_update/pallas_call | solution.py:482
  554.3 0.0 copy-start.7
  554.3 0.0 copy-start.10
  554.3 0.0 copy-start.11
  554.3 0.0 copy-start.6
  554.3 0.0 copy-start.8
  554.3 0.0 copy-start.9
  554.3 0.0 copy-start.4
  554.3 20.8 %last_bases.1 = (f32[32,128,128]{2,1,0:T(8,128)}, f32[32,128,128]{2,1,0:T(8,128)}, f32[32,128,128]{2,1,0:T(8,128)}, f32[32,128,128]{2,1,0:T(8,128)}, f32[32,128,...) custom-call(f32[16,128,256]{2,1,0:T(8,128)} %get-tuple-element.162.work_ref, ...), custom_call_target="tpu_custom_call" | custom-call | tf_op jit(solution)/shard_map/last_bases/pallas_call | solution.py:355
  575.2 0.0 copy-start.3
  575.2 0.0 copy-done.7
  575.2 0.0 copy-done.10
  575.2 0.0 copy-done.11
  575.2 0.9 subtract_bitcast_fusion
  576.1 0.0 copy-done.6
  576.1 0.0 copy-done.8
  576.1 0.0 copy-done.9
  576.2 1.4 divide_subtract_fusion
  577.6 0.6 copy.65
  578.2 0.6 copy.64
  578.7 0.6 copy.63
  579.3 0.0 copy-done.4
  579.3 0.0 copy-start.1
  579.3 1.1 copy.93
  580.5 0.0 copy-done.3
  580.5 1.1 copy.94
  581.6 0.0 copy-done.1
  (6 shorter events, 0.1 us)
Async XLA Ops:
  0.7 1.4 copy-start
  171.4 12.4 %copy-start.5 = (f32[4,2,2,32,128]{4,3,2,1,0:T(8,128)S(1)}, f32[4,2,2,32,128]{4,3,2,1,0:T(8,128)}, u32[]{:S(2)}) copy-start(f32[4,2,2,32,128]{4,3,2,1,0:T(8,128)} %get-tuple-element.104) | copy-start | bytes 786436
  308.3 31.0 %copy-start.2 = (f32[1024,768]{1,0:T(8,128)S(1)}, f32[1024,768]{1,0:T(8,128)}, u32[]{:S(2)}) copy-start(f32[1024,768]{1,0:T(8,128)} %get-tuple-element.107) | copy-start | bytes 9437188
  554.3 20.9 %copy-start.7 = (f32[1,7,48]{2,0,1:T(1,128)S(1)}, f32[1,7,48]{2,0,1:T(1,128)}, u32[]{:S(2)}) copy-start(f32[1,7,48]{2,0,1:T(1,128)} %param.37) | copy-start | bytes 4036
  554.3 20.9 %copy-start.10 = (f32[1,7,48]{2,0,1:T(1,128)S(1)}, f32[1,7,48]{2,0,1:T(1,128)}, u32[]{:S(2)}) copy-start(f32[1,7,48]{2,0,1:T(1,128)} %param.38) | copy-start | bytes 4036
  554.3 20.9 %copy-start.11 = (f32[1,7,48]{2,0,1:T(1,128)S(1)}, f32[1,7,48]{2,0,1:T(1,128)}, u32[]{:S(2)}) copy-start(f32[1,7,48]{2,0,1:T(1,128)} %param.39) | copy-start | bytes 4036
  554.3 21.8 %copy-start.6 = (f32[15,48]{1,0:T(8,128)S(1)}, f32[15,48]{1,0:T(8,128)}, u32[]{:S(2)}) copy-start(f32[15,48]{1,0:T(8,128)} %param.34) | copy-start | bytes 8644
  554.3 21.8 %copy-start.8 = (f32[15,48]{1,0:T(8,128)S(1)}, f32[15,48]{1,0:T(8,128)}, u32[]{:S(2)}) copy-start(f32[15,48]{1,0:T(8,128)} %param.36) | copy-start | bytes 8644
  554.3 21.8 %copy-start.9 = (f32[15,48]{1,0:T(8,128)S(1)}, f32[15,48]{1,0:T(8,128)}, u32[]{:S(2)}) copy-start(f32[15,48]{1,0:T(8,128)} %param.35) | copy-start | bytes 8644
  554.3 25.0 %copy-start.4 = (f32[512,768]{1,0:T(8,128)S(1)}, f32[512,768]{1,0:T(8,128)}, u32[]{:S(2)}) copy-start(f32[512,768]{1,0:T(8,128)} %get-tuple-element.274) | copy-start | bytes 4718596
  575.2 5.3 copy-start.3
  579.3 2.3 copy-start.1

commit v5 on v4

--- a/solution.py
+++ b/solution.py
@@ -285,11 +285,14 @@
 
                 @pl.when((r >= 1) & (r < half // 4))
                 def _(s=s):
-                    b = r - 1
-                    for p in ((0,), (1,), (2, 3))[s - 1]:
-                        panel_step(work, lax.rem(b, 2), p)
-                    if s == 3:
-                        finish(b)
+                    panel_step(work, lax.rem(r - 1, 2), s - 1)
+
+            else:
+
+                @pl.when((r >= 2) & (r <= half // 4))
+                def _():
+                    panel_step(work, lax.rem(r - 2, 2), TILE // PANEL - 1)
+                    finish(r - 2)
 
         return carry
 
@@ -619,43 +622,73 @@
     return blocks.reshape((-1,) + own.shape[1:]), smalls.reshape((-1,) + small.shape)
 
 
-def unpack_kernel(shapes, slots_ref, packed, *refs):
-    count = len(shapes)
-    mats, held, sems = refs[:count], refs[count:-1], refs[-1]
-
-    def whole(index):
-        return pltpu.make_async_copy(held[index], mats[index], sems.at[1, index])
-
-    offset = 0
-    for index, (height, breadth) in enumerate(shapes):
-        down, across = height // TILE, breadth // TILE
-
-        def start(i, carry, index=index, offset=offset, across=across):
-            for j in range(across):
-                tile = held[index].at[pl.ds(pl.multiple_of(i * TILE, TILE), TILE), j * TILE:(j + 1) * TILE]
-                slot = packed.at[slots_ref[offset + i * across + j]]
-                pltpu.make_async_copy(slot, tile, sems.at[0, index]).start()
-            return carry
-
-        lax.fori_loop(0, down, start, 0)
-        offset += down * across
-    for index in range(count):
-        pltpu.make_async_copy(held[index], held[index], sems.at[0, index]).wait()
-        whole(index).start()
-    for index in range(count):
-        whole(index).wait()
-
-
-def unpack_tiles(packed, slots, shapes):
-    return pl.pallas_call(
-        functools.partial(unpack_kernel, shapes),
-        out_shape=[jax.ShapeDtypeStruct(s, packed.dtype) for s in shapes],
-        in_specs=[pl.BlockSpec(memory_space=pltpu.SMEM), ANY],
-        out_specs=[ANY] * len(shapes),
-        scratch_shapes=[pltpu.VMEM(s, packed.dtype) for s in shapes] + [pltpu.SemaphoreType.DMA((2, len(shapes)))],
+def unpack_and_attend(packed, slots, shapes, x, split, places, half):
+    length, width = x.shape
+    span, count = min(length, 512), len(shapes)
+
+    def kernel(slots_ref, split_ref, packed_ref, x_ref, *refs):
+        mats, mixed_out, attended_out, totals_ref = refs[:count], refs[count], refs[count + 1], refs[count + 2]
+        near, rest = refs[count + 3:2 * count + 3], refs[2 * count + 3:]
+        x_near, mixed_ref, attended_ref, score_ref, turned_ref, sems, own_sems = rest
+
+        def whole(index):
+            return pltpu.make_async_copy(near[index], mats[index], sems.at[1, index])
+
+        load_x = pltpu.make_async_copy(x_ref, x_near, own_sems.at[0])
+        load_x.start()
+        offset = 0
+        for index, (height, breadth) in enumerate(shapes):
+            down, across = height // TILE, breadth // TILE
+
+            def start(i, carry, index=index, offset=offset, across=across):
+                for j in range(across):
+                    tile = near[index].at[pl.ds(pl.multiple_of(i * TILE, TILE), TILE), j * TILE:(j + 1) * TILE]
+                    slot = packed_ref.at[slots_ref[offset + i * across + j]]
+                    pltpu.make_async_copy(slot, tile, sems.at[0, index]).start()
+                return carry
+
+            lax.fori_loop(0, down, start, 0)
+            offset += down * across
+
+        def landed(index):
+            pltpu.make_async_copy(near[index], near[index], sems.at[0, index]).wait()
+            whole(index).start()
+
+        load_x.wait()
+        landed(0)
+        mix(x_near, near[0], bias_row(split_ref, places, ("enc_q", None, "enc_v"), half), mixed_ref)
+        keep_mixed = pltpu.make_async_copy(mixed_ref, mixed_out, own_sems.at[1])
+        keep_mixed.start()
+        for index in range(1, count):
+            landed(index)
+        totals_ref[...] = jnp.zeros_like(totals_ref)
+        attend(
+            mixed_ref.at[:, :half], mixed_ref.at[:, half:2 * half], mixed_ref.at[:, 2 * half:],
+            attended_ref, totals_ref, score_ref, turned_ref, False, span,
+        )
+        keep_attended = pltpu.make_async_copy(attended_ref, attended_out, own_sems.at[2])
+        keep_attended.start()
+        for index in range(count):
+            whole(index).wait()
+        keep_mixed.wait()
+        keep_attended.wait()
+
+    results = pl.pallas_call(
+        kernel,
+        out_shape=[jax.ShapeDtypeStruct(s, BF16) for s in shapes]
+        + [shape(length, 3 * half, dtype=BF16), shape(length, half, dtype=BF16), shape(8, length)],
+        in_specs=[pl.BlockSpec(memory_space=pltpu.SMEM), VM, ANY, ANY],
+        out_specs=[ANY] * (count + 2) + [VM],
+        scratch_shapes=[held(*s, dtype=BF16) for s in shapes]
+        + [
+            held(length, width, dtype=BF16), held(length, 3 * half, dtype=BF16), held(length, half, dtype=BF16),
+            held(2, length, span), held(half, length, dtype=BF16),
+            pltpu.SemaphoreType.DMA((2, count)), pltpu.SemaphoreType.DMA((3,)),
+        ],
         compiler_params=pltpu.CompilerParams(vmem_limit_bytes=56 << 20),
-        name="unpack_tiles",
-    )(slots, packed)
+        name="unpack_and_attend",
+    )(slots, split, packed, x)
+    return results[:count], results[count:]
 
 
 def weight_grads_kernel(plan, used, vectors, passed, slots_ref, *refs):
@@ -971,26 +1004,17 @@
     lax.fori_loop(0, pairs, pair, 0)
 
 
-def self_forward_kernel(
-    causal, span, x_ref, wide_ref, out_weight_ref, bias_ref, vec_ref,
-    mixed_ref, attended_ref, totals_ref, unit_ref, scale_ref,
-    score_ref, turned_ref, *swap_refs,
-):
+def mix(x_ref, wide_ref, bias, mixed_ref):
+    def one(t, carry):
+        mixed_ref[rows_of(t), :] = (times(x_ref[rows_of(t), :], wide_ref[...]) + bias).astype(BF16)
+        return carry
+
+    lax.fori_loop(0, x_ref.shape[0] // ROWS, one, 0)
+
+
+def close_branch(x_ref, attended_ref, out_weight_ref, vec_ref, unit_ref, scale_ref, *swap_refs):
     swap = Swap(*swap_refs)
-    length, width = x_ref.shape
-    half = out_weight_ref.shape[0]
-    tiles = length // ROWS
-    totals_ref[...] = jnp.zeros_like(totals_ref)
-
-    def mix(t, carry):
-        mixed_ref[rows_of(t), :] = (times(x_ref[rows_of(t), :], wide_ref[...]) + bias_ref[...]).astype(BF16)
-        return carry
-
-    lax.fori_loop(0, tiles, mix, 0)
-    attend(
-        mixed_ref.at[:, :half], mixed_ref.at[:, half:2 * half], mixed_ref.at[:, 2 * half:],
-        attended_ref, totals_ref, score_ref, turned_ref, causal, span,
-    )
+    tiles = x_ref.shape[0] // ROWS
 
     def give(t, carry):
         swap.give(t, times(attended_ref[rows_of(t), :], out_weight_ref[...]))
@@ -1006,6 +1030,21 @@
         return carry
 
     lax.fori_loop(0, tiles, take, 0)
+
+
+def self_forward_kernel(
+    causal, span, x_ref, wide_ref, out_weight_ref, bias, vec_ref,
+    mixed_ref, attended_ref, totals_ref, unit_ref, scale_ref,
+    score_ref, turned_ref, *swap_refs,
+):
+    half = out_weight_ref.shape[0]
+    totals_ref[...] = jnp.zeros_like(totals_ref)
+    mix(x_ref, wide_ref, bias, mixed_ref)
+    attend(
+        mixed_ref.at[:, :half], mixed_ref.at[:, half:2 * half], mixed_ref.at[:, 2 * half:],
+        attended_ref, totals_ref, score_ref, turned_ref, causal, span,
+    )
+    close_branch(x_ref, attended_ref, out_weight_ref, vec_ref, unit_ref, scale_ref, *swap_refs)
 
 
 def shape(*dims, dtype=F32):
@@ -1417,33 +1456,28 @@
 
 
 def encoder_and_fetch(
-    ident, x, wide, out_weight, up, down, shared, split, kept, wanted, target, dec_wide, dec_out_weight, count
+    ident, x, attended, out_weight, up, down, shared, split, kept, wanted, target, dec_wide, dec_out_weight, count
 ):
     length, width = x.shape
     half, hidden_half = out_weight.shape[0], up.shape[1]
-    tiles, span = length // ROWS, min(length, 512)
-    target_length = target.shape[0]
-    target_span = min(target_length, span)
+    tiles, target_length = length // ROWS, target.shape[0]
+    span = min(target_length, 512)
     fetched_rows = wanted.shape[0]
     places = bias_places(half, hidden_half)
 
     def body(
-        need, done, x_ref, wide_ref, out_weight_ref, up_ref, down_ref, shared_ref, split_ref, wanted_ref,
+        need, done, x_ref, attended_ref, out_weight_ref, up_ref, down_ref, shared_ref, split_ref, wanted_ref,
         target_ref, dec_wide_ref, dec_out_weight_ref, *refs,
     ):
-        saved, fed, dec_saved, fetched_ref, rest = refs[:5], refs[5:12], refs[12:17], refs[17], refs[18:]
+        saved, fed, dec_saved, fetched_ref, rest = refs[:2], refs[2:9], refs[9:14], refs[14], refs[15:]
         served_ref, trade_sems, rest = rest[0], rest[1:5], rest[5:]
         score_ref, turned_ref, rest = rest[0], rest[1], rest[2:]
         trade = Trade(count, fetched_ref, *trade_sems)
         stored_ref = fed[1]
         need(0, 1, 2)
         trade.greet()
-        self_forward_kernel(
-            False, span, x_ref, wide_ref, out_weight_ref,
-            bias_row(split_ref, places, ("enc_q", None, "enc_v"), half), Rows(shared_ref, (0,)),
-            *saved, score_ref, turned_ref, *rest[:4],
-        )
-        done(0, 1, 2, 3, 4)
+        close_branch(x_ref, attended_ref, out_weight_ref, Rows(shared_ref, (0,)), *saved, *rest[:4])
+        done(0, 1)
         need(3, 4, 5, 6, 7)
 
         def serve(t, carry):
@@ -1456,28 +1490,27 @@
         def between():
             lax.fori_loop(0, fetched_rows // ROWS, serve, 0)
             trade.start(served_ref)
-            done(6, 7, 8, 9, 10, 11)
+            done(3, 4, 5, 6, 7, 8)
 
         feed_forward_kernel(
-            kept, between, saved[3], up_ref, down_ref, split_ref.at[:, places["enc_up"]],
+            kept, between, saved[0], up_ref, down_ref, split_ref.at[:, places["enc_up"]],
             Rows(shared_ref, (1, 2, 3, 4, 5)), *fed, *rest[4:8],
         )
-        done(5)
+        done(2)
         need(8, 9, 10)
         self_forward_kernel(
-            True, target_span, target_ref, dec_wide_ref, dec_out_weight_ref,
+            True, span, target_ref, dec_wide_ref, dec_out_weight_ref,
             bias_row(split_ref, places, ("dec_q", None, "dec_v"), half), Rows(shared_ref, (6,)),
-            *dec_saved, score_ref.at[:, :, :target_span], turned_ref.at[:, :target_length], *rest[8:],
+            *dec_saved, score_ref, turned_ref, *rest[8:],
         )
-        done(12, 13, 14, 15, 16)
+        done(9, 10, 11, 12, 13)
         trade.finish(served_ref)
-        done(17)
+        done(14)
 
     return call(
         "encoder_and_fetch", ident, body,
-        [x, wide, out_weight, up, down, shared, split, wanted, target, dec_wide, dec_out_weight],
+        [x, attended, out_weight, up, down, shared, split, wanted, target, dec_wide, dec_out_weight],
         [
-            shape(length, 3 * half, dtype=BF16), shape(length, half, dtype=BF16), shape(8, length),
             shape(length, width), shape(length, 1),
             shape(length, width), shape(kept, width, dtype=BF16), shape(kept, width, dtype=BF16),
             shape(kept, hidden_half, dtype=BF16), shape(kept, hidden_half, dtype=BF16),
@@ -1486,7 +1519,7 @@
             shape(target_length, width), shape(target_length, 1), shape(fetched_rows, width, dtype=BF16),
         ],
         [held(fetched_rows, width // 2, dtype=BF16)] + Trade.scratch(count)
-        + [held(2, length, span), held(half, length, dtype=BF16)]
+        + [held(2, target_length, span), held(half, target_length, dtype=BF16)]
         + Swap.scratch(tiles, width) * 2 + Swap.scratch(target_length // ROWS, width),
     )
 
@@ -1708,7 +1741,6 @@
     shared_whole, split_whole = whole[:shared_count], whole[shared_count:]
     shapes = [s[1:] for s in matrix_list(model_width, hidden_width, tensor_count)]
     names = [s[0] for s in matrix_list(model_width, hidden_width, tensor_count)]
-    weights = dict(zip(names, unpack_tiles(gathered, owner_slots, shapes)))
     shared = jnp.pad(shared_whole.astype(F32), ((0, 16 - shared_count), (0, 0)))
     split = split_whole.astype(F32).reshape(1, -1)
     start_row = jnp.argmax(kept_mask)
@@ -1721,10 +1753,14 @@
         .astype(jnp.int32)
         - KEEP * me
     ).reshape(1, -1)
-    (enc_mixed, enc_attended, enc_totals, unit_one, scale_one,
+    matrices, (enc_mixed, enc_attended, enc_totals) = unpack_and_attend(
+        gathered, owner_slots, shapes, turned, split, bias_places(half_width, hidden_half), half_width
+    )
+    weights = dict(zip(names, matrices))
+    (unit_one, scale_one,
      states, _, hidden_low, enc_active, enc_slope, unit_two, scale_two,
      dec_mixed, dec_attended, dec_totals, unit_three, scale_three, fetched) = encoder_and_fetch(
-        10, turned, weights["enc_qkv"], weights["enc_out"], weights["enc_up"], weights["enc_down"],
+        10, turned, enc_attended, weights["enc_out"], weights["enc_up"], weights["enc_down"],
         shared, split, KEEP, wanted.reshape(-1, 1), target_tokens, weights["dec_qkv"], weights["dec_out"], device_count,
     )
     encoder_states = jnp.roll(states, start_row, 0)

time: 590 us -> 584 us (0.990)
  Pallas kernels: 551 us -> 543 us
    pallas_call x3, Pallas kernels: 151 us -> 137 us  [call(): pl.pallas_call(kernel, out_shape=outputs, in_specs=[ANY if i in ins else...]
    pallas_call x1, Pallas kernels: 12.3 us -> 22.9 us  [unpack_and_attend(): pl.pallas_call(kernel, out_shape=[jax.ShapeDtypeStruct(s, BF16) for s in...]
where the time goes in v5:
time: 584 us; the launch traced here: 575 us
  Pallas kernels  543 us (93%)
  other arithmetic  18.6 us (3%)
  local copies, waits for them, and re-layouts  9.98 us (2%)
    pallas_call x1, Pallas kernels, owner_update(): pl.pallas_call(functools.partial(owner_kernel, grid), out_shape=[jax.Shap...  173 us
    pallas_call x1, Pallas kernels, gather_all(): pl.pallas_call(functools.partial(ag_kernel, grid), out_shape=[jax.ShapeDt...  159 us
    pallas_call x3, Pallas kernels, call(): pl.pallas_call(kernel, out_shape=outputs, in_specs=[ANY if i in ins else...  137 us
    pallas_call x2, Pallas kernels, weight_grads(): pl.pallas_call(functools.partial(weight_grads_kernel, plan, len(arrays),...  30.5 us
    pallas_call x1, Pallas kernels, unpack_and_attend(): pl.pallas_call(kernel, out_shape=[jax.ShapeDtypeStruct(s, BF16) for s in...  22.9 us
    pallas_call x1, Pallas kernels, last_bases(): pl.pallas_call(last_bases_kernel, out_shape=[jax.ShapeDtypeStruct(whole,...  20.8 us

profile of v5, /device:TPU:0, one launch (start us, length us, event | category | flops | bytes accessed | tf_op | source)
XLA Modules:
  0.0 575.4 jit_solution(2999831998038264590)
XLA Ops:
  0.7 0.0 copy-start
  0.7 0.9 compare_reduce_fusion
  1.6 0.5 convert_element_type.46.refs_0_
  2.1 0.0 copy-done
  2.1 0.7 iota_reduce_fusion
  5.4 0.7 convert_element_type.42
  6.0 0.7 copy.89
  6.7 0.7 select_maximum_fusion
  7.4 0.6 pad_maximum_fusion.small_ref
  8.0 4.0 fusion.2.x_ref.refs_0_.refs_6_
  12.1 159.3 %gather_all.1 = (bf16[4,2,2,32,128,128]{5,4,3,2,1,0:T(8,128)(2,1)}, f32[4,2,2,32,128]{4,3,2,1,0:T(8,128)}) custom-call(f32[32,128,128]{2,1,0:T(8,128)} %bitcast.48, f32[32,128]{1,0:T(8,128)} %pad_maximum_fusion.small_ref), custom_call_target="tpu_custom_call" | custom-call | tf_op jit(solution)/shard_map/gather_all/pallas_call | solution.py:613
  171.4 0.8 slice.30
  172.2 0.9 slice.27
  173.2 0.7 reshape.117.split_ref.refs_6_.refs_10_
  173.9 0.1 convert_element_type.44
  174.0 0.6 pad_convert_fusion.refs_5_.refs_9_.refs_15_
  174.7 0.1 reshape.114
  174.8 0.5 broadcast.58
  175.3 0.7 fusion.9
  176.0 0.7 sub.45.refs_1_
  176.6 1.3 sub.51.refs_7_
  177.9 22.9 %unpack_and_attend.1 = (bf16[768,1152]{1,0:T(8,128)(2,1)}, bf16[384,768]{1,0:T(8,128)(2,1)}, bf16[768,1536]{1,0:T(8,128)(2,1)}, bf16[1536,768]{1,0:T(8,128)(2,1)...) custom-call(s32[504]{0:T(512)} %slots_ref.5, ...), custom_call_target="tpu_custom_call" | custom-call | tf_op jit(solution)/shard_map/unpack_and_attend/pallas_call | solution.py:676
  200.8 38.4 %encoder_and_fetch.1 = (f32[1024,768]{1,0:T(8,128)}, f32[1024,1]{1,0:T(8,128)}, f32[1024,768]{1,0:T(8,128)}, bf16[512,768]{1,0:T(8,128)(2,1)}, bf16[512,768]{1,0...) custom-call(bf16[1024,768]{1,0:T(8,128)(2,1)} %fusion.2.x_ref.refs_0, ...), custom_call_target="tpu_custom_call" | custom-call | tf_op jit(solution)/shard_map/encoder_and_fetch/pallas_call | solution.py:1360
  239.3 67.4 %decoder_core.1 = (f32[512,768]{1,0:T(8,128)}, bf16[512,768]{1,0:T(8,128)(2,1)}, bf16[512,384]{1,0:T(8,128)(2,1)}, bf16[512,768]{1,0:T(8,128)(2,1)}, bf16[512,15...) custom-call(f32[512,768]{1,0:T(8,128)} %get-tuple-element.108.refs_0, ...), custom_call_target="tpu_custom_call" | custom-call | tf_op jit(solution)/shard_map/decoder_core/pallas_call | solution.py:1360
  306.7 0.0 copy-start.2
  306.7 31.0 %encoder_backward.1 = (bf16[512,768]{1,0:T(8,128)(2,1)}, bf16[512,1536]{1,0:T(8,128)(2,1)}, f32[1,1536]{1,0:T(1,128)}, f32[8,768]{1,0:T(8,128)}, f32[8,768]{1,0:...) custom-call(bf16[1024,768]{1,0:T(8,128)(2,1)} %get-tuple-element.120, ...), custom_call_target="tpu_custom_call" | custom-call | tf_op jit(solution)/shard_map/encoder_backward/pallas_call | solution.py:1360
  337.7 0.0 copy-done.2
  337.7 6.9 %fusion = (f32[1024,768]{1,0:T(8,128)}, f32[1024,768]{1,0:T(8,128)}) fusion(s32[]{:T(128)S(6)} %select_n.37, f32[1024,768]{1,0:T(8,128)} %get-tuple-element.130, f32[1024,768]{1,0:T(8,128)S(1)} %copy-done.2), kind=kLoop, calls=%fused_computation.4 | loop fusion | flops 1572864 | bytes 12582916 | tf_op jit(solution)/shard_map/jit(_roll_dynamic)/concatenate | solution.py:1780
  344.5 16.4 %weight_grads.2.refs_19_ = bf16[512,128,128]{2,1,0:T(8,128)(2,1)} custom-call(s32[504]{0:T(512)} %slots_ref.5, bf16[512,1536]{1,0:T(8,128)(2,1)} %get-tuple-element.148.refs_0_, bf16[512,768]{1,0:T(8,128)(2,1)} %get-tuple-element.149.refs_1_, bf16[512,768]{1,0:T(8,128)(2,1)} %get-tuple-element.150.refs_2_, bf16[512,1536]{1,0:T(8,128)(2,1)} %get-tuple-element.151.refs_3_, ...), custom_call_target="tpu_custom_call" | custom-call | tf_op jit(solution)/shard_map/weight_grads/pallas_call | solution.py:797
  360.9 14.1 %weight_grads.3 = (bf16[512,128,128]{2,1,0:T(8,128)(2,1)}, f32[24,768]{1,0:T(8,128)}) custom-call(s32[504]{0:T(512)} %slots_ref.5, bf16[512,1536]{1,0:T(8,128)(2,1)} %get-tuple-element.123.refs_4_.refs_0_, bf16[512,768]{1,0:T(8,128)(2,1)} %get-tuple-element.132.refs_1_, ...), custom_call_target="tpu_custom_call", output_to_operand_aliasing={{0}: (20, {})} | custom-call | tf_op jit(solution)/shard_map/weight_grads/pallas_call | solution.py:797
  375.0 172.9 %owner_update.1 = (f32[32,128,128]{2,1,0:T(8,128)}, f32[32,128,128]{2,1,0:T(8,128)}, f32[32,128,128]{2,1,0:T(8,128)}, f32[32,128,128]{2,1,0:T(8,128)}, f32[32,12...) custom-call(s32[32]{0:T(128)} %convert_element_type.46.refs_0_, ...), custom_call_target="tpu_custom_call" | custom-call | tf_op jit(solution)/shard_map/owner_update/pallas_call | solution.py:485
  547.9 0.0 copy-start.6
  547.9 0.0 copy-start.9
  547.9 0.0 copy-start.10
  547.9 0.0 copy-start.5
  547.9 0.0 copy-start.7
  547.9 0.0 copy-start.8
  548.0 0.0 copy-start.4
  548.0 20.8 %last_bases.1 = (f32[32,128,128]{2,1,0:T(8,128)}, f32[32,128,128]{2,1,0:T(8,128)}, f32[32,128,128]{2,1,0:T(8,128)}, f32[32,128,128]{2,1,0:T(8,128)}, f32[32,128,...) custom-call(f32[16,128,256]{2,1,0:T(8,128)} %get-tuple-element.162.work_ref, ...), custom_call_target="tpu_custom_call" | custom-call | tf_op jit(solution)/shard_map/last_bases/pallas_call | solution.py:358
  568.8 0.0 copy-start.3
  568.8 0.0 copy-done.6
  568.8 0.0 copy-done.9
  568.8 0.0 copy-done.10
  568.8 0.9 subtract_bitcast_fusion
  569.8 0.0 copy-done.5
  569.8 0.0 copy-done.7
  569.8 0.0 copy-done.8
  569.8 1.4 divide_subtract_fusion
  571.2 0.6 copy.65
  571.8 0.6 copy.64
  572.4 0.6 copy.63
  573.0 0.0 copy-done.4
  573.0 0.0 copy-start.1
  573.0 1.1 copy.93
  574.1 0.0 copy-done.3
  574.1 1.1 copy.94
  575.2 0.0 copy-done.1
  (4 shorter events, 0.0 us)
Async XLA Ops:
  0.7 1.4 copy-start
  306.7 31.0 %copy-start.2 = (f32[1024,768]{1,0:T(8,128)S(1)}, f32[1024,768]{1,0:T(8,128)}, u32[]{:S(2)}) copy-start(f32[1024,768]{1,0:T(8,128)} %get-tuple-element.107) | copy-start | bytes 9437188
  547.9 20.9 %copy-start.6 = (f32[1,7,48]{2,0,1:T(1,128)S(1)}, f32[1,7,48]{2,0,1:T(1,128)}, u32[]{:S(2)}) copy-start(f32[1,7,48]{2,0,1:T(1,128)} %param.37) | copy-start | bytes 4036
  547.9 20.9 %copy-start.9 = (f32[1,7,48]{2,0,1:T(1,128)S(1)}, f32[1,7,48]{2,0,1:T(1,128)}, u32[]{:S(2)}) copy-start(f32[1,7,48]{2,0,1:T(1,128)} %param.38) | copy-start | bytes 4036
  547.9 20.9 %copy-start.10 = (f32[1,7,48]{2,0,1:T(1,128)S(1)}, f32[1,7,48]{2,0,1:T(1,128)}, u32[]{:S(2)}) copy-start(f32[1,7,48]{2,0,1:T(1,128)} %param.39) | copy-start | bytes 4036
  547.9 21.8 %copy-start.5 = (f32[15,48]{1,0:T(8,128)S(1)}, f32[15,48]{1,0:T(8,128)}, u32[]{:S(2)}) copy-start(f32[15,48]{1,0:T(8,128)} %param.34) | copy-start | bytes 8644
  547.9 21.8 %copy-start.7 = (f32[15,48]{1,0:T(8,128)S(1)}, f32[15,48]{1,0:T(8,128)}, u32[]{:S(2)}) copy-start(f32[15,48]{1,0:T(8,128)} %param.36) | copy-start | bytes 8644
  547.9 21.8 %copy-start.8 = (f32[15,48]{1,0:T(8,128)S(1)}, f32[15,48]{1,0:T(8,128)}, u32[]{:S(2)}) copy-start(f32[15,48]{1,0:T(8,128)} %param.35) | copy-start | bytes 8644
  548.0 25.0 %copy-start.4 = (f32[512,768]{1,0:T(8,128)S(1)}, f32[512,768]{1,0:T(8,128)}, u32[]{:S(2)}) copy-start(f32[512,768]{1,0:T(8,128)} %get-tuple-element.274) | copy-start | bytes 4718596
  568.8 5.3 copy-start.3
  573.0 2.3 copy-start.1

commit v6 on v5

--- a/solution.py
+++ b/solution.py
@@ -636,19 +636,20 @@
 
         load_x = pltpu.make_async_copy(x_ref, x_near, own_sems.at[0])
         load_x.start()
-        offset = 0
-        for index, (height, breadth) in enumerate(shapes):
-            down, across = height // TILE, breadth // TILE
-
-            def start(i, carry, index=index, offset=offset, across=across):
+        offsets = [0]
+        for height, breadth in shapes:
+            offsets.append(offsets[-1] + height // TILE * (breadth // TILE))
+
+        def start(index):
+            height, breadth = shapes[index]
+            across = breadth // TILE
+            for i in range(height // TILE):
                 for j in range(across):
-                    tile = near[index].at[pl.ds(pl.multiple_of(i * TILE, TILE), TILE), j * TILE:(j + 1) * TILE]
-                    slot = packed_ref.at[slots_ref[offset + i * across + j]]
+                    tile = near[index].at[i * TILE:(i + 1) * TILE, j * TILE:(j + 1) * TILE]
+                    slot = packed_ref.at[slots_ref[offsets[index] + i * across + j]]
                     pltpu.make_async_copy(slot, tile, sems.at[0, index]).start()
-                return carry
-
-            lax.fori_loop(0, down, start, 0)
-            offset += down * across
+
+        start(0)
 
         def landed(index):
             pltpu.make_async_copy(near[index], near[index], sems.at[0, index]).wait()
@@ -659,12 +660,21 @@
         mix(x_near, near[0], bias_row(split_ref, places, ("enc_q", None, "enc_v"), half), mixed_ref)
         keep_mixed = pltpu.make_async_copy(mixed_ref, mixed_out, own_sems.at[1])
         keep_mixed.start()
-        for index in range(1, count):
-            landed(index)
+
+        def beside(part, parts):
+            lead = parts // 2
+            share = -(-(count - 1) // lead)
+            place = part if part < lead else part - lead
+            for index in range(1 + place * share, min(count, 1 + (place + 1) * share)):
+                if part < lead:
+                    start(index)
+                elif part < 2 * lead:
+                    landed(index)
+
         totals_ref[...] = jnp.zeros_like(totals_ref)
         attend(
             mixed_ref.at[:, :half], mixed_ref.at[:, half:2 * half], mixed_ref.at[:, 2 * half:],
-            attended_ref, totals_ref, score_ref, turned_ref, False, span,
+            attended_ref, totals_ref, score_ref, turned_ref, False, span, beside,
         )
         keep_attended = pltpu.make_async_copy(attended_ref, attended_out, own_sems.at[2])
         keep_attended.start()
@@ -728,6 +738,15 @@
                     begin, at = begin + size, at + size
     ready = set()
     last = None
+    ready_columns = []
+
+    def send(result, index, offset, stride, down, group, n):
+        for i in range(down):
+            for j in range(n * group, (n + 1) * group):
+                tile = result.at[i * TILE:(i + 1) * TILE, j * TILE:(j + 1) * TILE]
+                slot = packed.at[slots_ref[offset + i * stride + j]]
+                pltpu.make_async_copy(tile, slot, store_sem.at[index]).start()
+
     for index, (left, tokens, right, offset, stride, down, across) in enumerate(plan):
         for i in (left, right):
             if i not in ready:
@@ -743,25 +762,14 @@
         result = results[index]
         group = 3 if across % 3 == 0 else 1
 
-        def columns(n, carry, right=right, tokens=tokens, height=height, result=result, offset=offset,
-                    stride=stride, down=down, group=group, index=index):
-            lanes = pl.ds(pl.multiple_of(n * group * TILE, TILE), group * TILE)
+        for n in range(across // group):
+            lanes = slice(n * group * TILE, (n + 1) * group * TILE)
             result[:, lanes] = times(turned[:height, :tokens], held[right][:tokens, lanes]).astype(BF16)
-
-            def send(i, carry):
-                for j in range(group):
-                    tile = result.at[
-                        pl.ds(pl.multiple_of(i * TILE, TILE), TILE),
-                        pl.ds(pl.multiple_of((n * group + j) * TILE, TILE), TILE),
-                    ]
-                    slot = packed.at[slots_ref[offset + i * stride + n * group + j]]
-                    pltpu.make_async_copy(tile, slot, store_sem.at[index]).start()
-                return carry
-
-            lax.fori_loop(0, down, send, 0)
-            return carry
-
-        lax.fori_loop(0, across // group, columns, 0)
+            ready_columns.append((result, index, offset, stride, down, group, n))
+            if len(ready_columns) > 1:
+                send(*ready_columns.pop(0))
+    for columns in ready_columns:
+        send(*columns)
     for index in range(len(plan)):
         pltpu.make_async_copy(results[index], results[index], store_sem.at[index]).wait()
 
@@ -903,7 +911,7 @@
     return lax.broadcasted_iota(jnp.int32, shape, 1) < HD
 
 
-def attend(query_ref, key_ref, value_ref, attended_ref, totals_ref, score_ref, turned_ref, causal, span):
+def attend(query_ref, key_ref, value_ref, attended_ref, totals_ref, score_ref, turned_ref, causal, span, beside=None):
     queries, keys = query_ref.shape[0], key_ref.shape[0]
     pairs = query_ref.shape[1] // PAIR
     chunks = keys // KEYS
@@ -915,7 +923,7 @@
         mine = slice(i * span, (i + 1) * span)
 
         def pair(j, carry, i=i, mine=mine):
-            lanes = pl.ds(pl.multiple_of(j * PAIR, PAIR), PAIR)
+            lanes = pl.ds(j * PAIR if isinstance(j, int) else pl.multiple_of(j * PAIR, PAIR), PAIR)
             query = query_ref[mine, lanes] * jnp.asarray(HD**-0.5, BF16)
             first = head_mask(query.shape)
             parts = []
@@ -934,7 +942,7 @@
                     top = jnp.maximum(top, jnp.max(scores, 0, keepdims=True))
                 total = jnp.zeros((1, span), F32)
                 mixed = jnp.zeros((HD, span), F32)
-                value_rows = pl.ds(pl.multiple_of(j * PAIR + h * HD, HD), HD)
+                value_rows = pl.ds(j * PAIR + h * HD if isinstance(j, int) else pl.multiple_of(j * PAIR + h * HD, HD), HD)
                 for c in range(chunks):
                     if causal and c * KEYS >= (i + 1) * span:
                         continue
@@ -946,7 +954,12 @@
             attended_ref[mine, lanes] = jnp.concatenate(parts, 0).T.astype(BF16)
             return carry
 
-        lax.fori_loop(0, pairs, pair, 0)
+        if beside is None:
+            lax.fori_loop(0, pairs, pair, 0)
+        else:
+            for j in range(pairs):
+                beside(i * pairs + j, queries // span * pairs)
+                pair(j, 0)
 
 
 def attend_back(

time: 584 us -> 570 us (0.976)
  Pallas kernels: 543 us -> 533 us
    pallas_call x2, Pallas kernels: 30.5 us -> 23.9 us  [weight_grads(): pl.pallas_call(functools.partial(weight_grads_kernel, plan, len(arrays),...]
where the time goes in v6:
time: 570 us; the launch traced here: 565 us
  Pallas kernels  533 us (94%)
  other arithmetic  18.6 us (3%)
  local copies, waits for them, and re-layouts  9.98 us (2%)
    pallas_call x1, Pallas kernels, owner_update(): pl.pallas_call(functools.partial(owner_kernel, grid), out_shape=[jax.Shap...  173 us
    pallas_call x1, Pallas kernels, gather_all(): pl.pallas_call(functools.partial(ag_kernel, grid), out_shape=[jax.ShapeDt...  159 us
    pallas_call x3, Pallas kernels, call(): pl.pallas_call(kernel, out_shape=outputs, in_specs=[ANY if i in ins else...  137 us
    pallas_call x2, Pallas kernels, weight_grads(): pl.pallas_call(functools.partial(weight_grads_kernel, plan, len(arrays),...  23.9 us
    pallas_call x1, Pallas kernels, last_bases(): pl.pallas_call(last_bases_kernel, out_shape=[jax.ShapeDtypeStruct(whole,...  20.8 us
    pallas_call x1, Pallas kernels, unpack_and_attend(): pl.pallas_call(kernel, out_shape=[jax.ShapeDtypeStruct(s, BF16) for s in...  19.5 us

profile of v6, /device:TPU:0, one launch (start us, length us, event | category | flops | bytes accessed | tf_op | source)
XLA Modules:
  0.0 565.3 jit_solution(4351134164045152989)
XLA Ops:
  0.7 0.0 copy-start
  0.7 0.9 compare_reduce_fusion
  1.6 0.5 convert_element_type.46.refs_0_
  2.1 0.0 copy-done
  2.1 0.7 iota_reduce_fusion
  5.4 0.7 convert_element_type.42
  6.0 0.7 copy.89
  6.7 0.7 select_maximum_fusion
  7.4 0.6 pad_maximum_fusion.small_ref
  8.0 4.0 fusion.2.x_ref.refs_0_.refs_6_
  12.1 159.3 %gather_all.1 = (bf16[4,2,2,32,128,128]{5,4,3,2,1,0:T(8,128)(2,1)}, f32[4,2,2,32,128]{4,3,2,1,0:T(8,128)}) custom-call(f32[32,128,128]{2,1,0:T(8,128)} %bitcast.48, f32[32,128]{1,0:T(8,128)} %pad_maximum_fusion.small_ref), custom_call_target="tpu_custom_call" | custom-call | tf_op jit(solution)/shard_map/gather_all/pallas_call | solution.py:613
  171.4 0.8 slice.30
  172.2 0.9 slice.27
  173.2 0.7 reshape.117.split_ref.refs_6_.refs_10_
  173.9 0.1 convert_element_type.44
  174.0 0.6 pad_convert_fusion.refs_5_.refs_9_.refs_15_
  174.7 0.1 reshape.114
  174.7 0.5 broadcast.58
  175.3 0.7 fusion.9
  176.0 0.7 sub.45.refs_1_
  176.6 1.3 sub.51.refs_7_
  177.9 19.5 %unpack_and_attend.1 = (bf16[768,1152]{1,0:T(8,128)(2,1)}, bf16[384,768]{1,0:T(8,128)(2,1)}, bf16[768,1536]{1,0:T(8,128)(2,1)}, bf16[1536,768]{1,0:T(8,128)(2,1)...) custom-call(s32[504]{0:T(512)} %slots_ref.5, ...), custom_call_target="tpu_custom_call" | custom-call | tf_op jit(solution)/shard_map/unpack_and_attend/pallas_call | solution.py:686
  197.4 38.6 %encoder_and_fetch.1 = (f32[1024,768]{1,0:T(8,128)}, f32[1024,1]{1,0:T(8,128)}, f32[1024,768]{1,0:T(8,128)}, bf16[512,768]{1,0:T(8,128)(2,1)}, bf16[512,768]{1,0...) custom-call(bf16[1024,768]{1,0:T(8,128)(2,1)} %fusion.2.x_ref.refs_0, ...), custom_call_target="tpu_custom_call" | custom-call | tf_op jit(solution)/shard_map/encoder_and_fetch/pallas_call | solution.py:1373
  236.0 67.3 %decoder_core.1 = (f32[512,768]{1,0:T(8,128)}, bf16[512,768]{1,0:T(8,128)(2,1)}, bf16[512,384]{1,0:T(8,128)(2,1)}, bf16[512,768]{1,0:T(8,128)(2,1)}, bf16[512,15...) custom-call(f32[512,768]{1,0:T(8,128)} %get-tuple-element.108.refs_0, ...), custom_call_target="tpu_custom_call" | custom-call | tf_op jit(solution)/shard_map/decoder_core/pallas_call | solution.py:1373
  303.3 0.0 copy-start.2
  303.3 30.8 %encoder_backward.1 = (bf16[512,768]{1,0:T(8,128)(2,1)}, bf16[512,1536]{1,0:T(8,128)(2,1)}, f32[1,1536]{1,0:T(1,128)}, f32[8,768]{1,0:T(8,128)}, f32[8,768]{1,0:...) custom-call(bf16[1024,768]{1,0:T(8,128)(2,1)} %get-tuple-element.120, ...), custom_call_target="tpu_custom_call" | custom-call | tf_op jit(solution)/shard_map/encoder_backward/pallas_call | solution.py:1373
  334.1 0.0 copy-done.2
  334.1 6.9 %fusion = (f32[1024,768]{1,0:T(8,128)}, f32[1024,768]{1,0:T(8,128)}) fusion(s32[]{:T(128)S(6)} %select_n.37, f32[1024,768]{1,0:T(8,128)} %get-tuple-element.130, f32[1024,768]{1,0:T(8,128)S(1)} %copy-done.2), kind=kLoop, calls=%fused_computation.4 | loop fusion | flops 1572864 | bytes 12582916 | tf_op jit(solution)/shard_map/jit(_roll_dynamic)/concatenate | solution.py:1793
  341.0 12.7 %weight_grads.2.refs_19_ = bf16[512,128,128]{2,1,0:T(8,128)(2,1)} custom-call(s32[504]{0:T(512)} %slots_ref.5, bf16[512,1536]{1,0:T(8,128)(2,1)} %get-tuple-element.148.refs_0_, bf16[512,768]{1,0:T(8,128)(2,1)} %get-tuple-element.149.refs_1_, bf16[512,768]{1,0:T(8,128)(2,1)} %get-tuple-element.150.refs_2_, bf16[512,1536]{1,0:T(8,128)(2,1)} %get-tuple-element.151.refs_3_, ...), custom_call_target="tpu_custom_call" | custom-call | tf_op jit(solution)/shard_map/weight_grads/pallas_call | solution.py:805
  353.7 11.2 %weight_grads.3 = (bf16[512,128,128]{2,1,0:T(8,128)(2,1)}, f32[24,768]{1,0:T(8,128)}) custom-call(s32[504]{0:T(512)} %slots_ref.5, bf16[512,1536]{1,0:T(8,128)(2,1)} %get-tuple-element.123.refs_4_.refs_0_, bf16[512,768]{1,0:T(8,128)(2,1)} %get-tuple-element.132.refs_1_, ...), custom_call_target="tpu_custom_call", output_to_operand_aliasing={{0}: (20, {})} | custom-call | tf_op jit(solution)/shard_map/weight_grads/pallas_call | solution.py:805
  364.9 172.8 %owner_update.1 = (f32[32,128,128]{2,1,0:T(8,128)}, f32[32,128,128]{2,1,0:T(8,128)}, f32[32,128,128]{2,1,0:T(8,128)}, f32[32,128,128]{2,1,0:T(8,128)}, f32[32,12...) custom-call(s32[32]{0:T(128)} %convert_element_type.46.refs_0_, ...), custom_call_target="tpu_custom_call" | custom-call | tf_op jit(solution)/shard_map/owner_update/pallas_call | solution.py:485
  537.7 0.0 copy-start.6
  537.8 0.0 copy-start.9
  537.8 0.0 copy-start.10
  537.8 0.0 copy-start.5
  537.8 0.0 copy-start.7
  537.8 0.0 copy-start.8
  537.8 0.0 copy-start.4
  537.8 20.8 %last_bases.1 = (f32[32,128,128]{2,1,0:T(8,128)}, f32[32,128,128]{2,1,0:T(8,128)}, f32[32,128,128]{2,1,0:T(8,128)}, f32[32,128,128]{2,1,0:T(8,128)}, f32[32,128,...) custom-call(f32[16,128,256]{2,1,0:T(8,128)} %get-tuple-element.162.work_ref, ...), custom_call_target="tpu_custom_call" | custom-call | tf_op jit(solution)/shard_map/last_bases/pallas_call | solution.py:358
  558.7 0.0 copy-start.3
  558.7 0.0 copy-done.6
  558.7 0.0 copy-done.9
  558.7 0.0 copy-done.10
  558.7 0.9 subtract_bitcast_fusion
  559.6 0.0 copy-done.5
  559.6 0.0 copy-done.7
  559.6 0.0 copy-done.8
  559.6 1.4 divide_subtract_fusion
  561.1 0.6 copy.65
  561.7 0.6 copy.64
  562.2 0.6 copy.63
  562.8 0.0 copy-done.4
  562.8 0.0 copy-start.1
  562.8 1.1 copy.93
  564.0 0.0 copy-done.3
  564.0 1.1 copy.94
  565.1 0.0 copy-done.1
  (4 shorter events, 0.0 us)
Async XLA Ops:
  0.7 1.4 copy-start
  303.3 30.8 %copy-start.2 = (f32[1024,768]{1,0:T(8,128)S(1)}, f32[1024,768]{1,0:T(8,128)}, u32[]{:S(2)}) copy-start(f32[1024,768]{1,0:T(8,128)} %get-tuple-element.107) | copy-start | bytes 9437188
  537.7 20.9 %copy-start.6 = (f32[1,7,48]{2,0,1:T(1,128)S(1)}, f32[1,7,48]{2,0,1:T(1,128)}, u32[]{:S(2)}) copy-start(f32[1,7,48]{2,0,1:T(1,128)} %param.37) | copy-start | bytes 4036
  537.8 20.9 %copy-start.9 = (f32[1,7,48]{2,0,1:T(1,128)S(1)}, f32[1,7,48]{2,0,1:T(1,128)}, u32[]{:S(2)}) copy-start(f32[1,7,48]{2,0,1:T(1,128)} %param.38) | copy-start | bytes 4036
  537.8 20.9 %copy-start.10 = (f32[1,7,48]{2,0,1:T(1,128)S(1)}, f32[1,7,48]{2,0,1:T(1,128)}, u32[]{:S(2)}) copy-start(f32[1,7,48]{2,0,1:T(1,128)} %param.39) | copy-start | bytes 4036
  537.8 21.8 %copy-start.5 = (f32[15,48]{1,0:T(8,128)S(1)}, f32[15,48]{1,0:T(8,128)}, u32[]{:S(2)}) copy-start(f32[15,48]{1,0:T(8,128)} %param.34) | copy-start | bytes 8644
  537.8 21.8 %copy-start.7 = (f32[15,48]{1,0:T(8,128)S(1)}, f32[15,48]{1,0:T(8,128)}, u32[]{:S(2)}) copy-start(f32[15,48]{1,0:T(8,128)} %param.36) | copy-start | bytes 8644
  537.8 21.8 %copy-start.8 = (f32[15,48]{1,0:T(8,128)S(1)}, f32[15,48]{1,0:T(8,128)}, u32[]{:S(2)}) copy-start(f32[15,48]{1,0:T(8,128)} %param.35) | copy-start | bytes 8644
  537.8 25.0 %copy-start.4 = (f32[512,768]{1,0:T(8,128)S(1)}, f32[512,768]{1,0:T(8,128)}, u32[]{:S(2)}) copy-start(f32[512,768]{1,0:T(8,128)} %get-tuple-element.274) | copy-start | bytes 4718596
  558.7 5.3 copy-start.3
  562.8 2.3 copy-start.1

commit v7 on v6

--- a/solution.py
+++ b/solution.py
@@ -1014,7 +1014,7 @@
         grad_query_ref[:, lanes] = (jnp.concatenate(grad_query, 0) * scale).T.astype(BF16)
         return carry
 
-    lax.fori_loop(0, pairs, pair, 0)
+    lax.fori_loop(0, pairs, pair, 0, unroll=True)
 
 
 def mix(x_ref, wide_ref, bias, mixed_ref):

time: 570 us -> 569 us (level)
  no operation moved by 1% of the time
where the time goes in v7:
time: 569 us; the launch traced here: 564 us
  Pallas kernels  532 us (93%)
  other arithmetic  18.6 us (3%)
  local copies, waits for them, and re-layouts  9.98 us (2%)
    pallas_call x1, Pallas kernels, owner_update(): pl.pallas_call(functools.partial(owner_kernel, grid), out_shape=[jax.Shap...  173 us
    pallas_call x1, Pallas kernels, gather_all(): pl.pallas_call(functools.partial(ag_kernel, grid), out_shape=[jax.ShapeDt...  159 us
    pallas_call x3, Pallas kernels, call(): pl.pallas_call(kernel, out_shape=outputs, in_specs=[ANY if i in ins else...  136 us
    pallas_call x2, Pallas kernels, weight_grads(): pl.pallas_call(functools.partial(weight_grads_kernel, plan, len(arrays),...  23.9 us
    pallas_call x1, Pallas kernels, last_bases(): pl.pallas_call(last_bases_kernel, out_shape=[jax.ShapeDtypeStruct(whole,...  20.8 us
    pallas_call x1, Pallas kernels, unpack_and_attend(): pl.pallas_call(kernel, out_shape=[jax.ShapeDtypeStruct(s, BF16) for s in...  19.5 us

profile of v7, /device:TPU:0, one launch (start us, length us, event | category | flops | bytes accessed | tf_op | source)
XLA Modules:
  0.0 564.3 jit_solution(186292234591824594)
XLA Ops:
  0.7 0.0 copy-start
  0.7 0.9 compare_reduce_fusion
  1.6 0.5 convert_element_type.46.refs_0_
  2.1 0.0 copy-done
  2.1 0.7 iota_reduce_fusion
  5.4 0.7 convert_element_type.42
  6.0 0.7 copy.89
  6.7 0.7 select_maximum_fusion
  7.4 0.6 pad_maximum_fusion.small_ref
  8.0 4.0 fusion.2.x_ref.refs_0_.refs_6_
  12.1 159.3 %gather_all.1 = (bf16[4,2,2,32,128,128]{5,4,3,2,1,0:T(8,128)(2,1)}, f32[4,2,2,32,128]{4,3,2,1,0:T(8,128)}) custom-call(f32[32,128,128]{2,1,0:T(8,128)} %bitcast.48, f32[32,128]{1,0:T(8,128)} %pad_maximum_fusion.small_ref), custom_call_target="tpu_custom_call" | custom-call | tf_op jit(solution)/shard_map/gather_all/pallas_call | solution.py:613
  171.4 0.8 slice.30
  172.2 0.9 slice.27
  173.2 0.7 reshape.117.split_ref.refs_6_.refs_10_
  173.9 0.1 convert_element_type.44
  174.0 0.6 pad_convert_fusion.refs_5_.refs_9_.refs_15_
  174.7 0.1 reshape.114
  174.7 0.5 broadcast.58
  175.3 0.7 fusion.9
  176.0 0.7 sub.45.refs_1_
  176.6 1.3 sub.51.refs_7_
  177.9 19.5 %unpack_and_attend.1 = (bf16[768,1152]{1,0:T(8,128)(2,1)}, bf16[384,768]{1,0:T(8,128)(2,1)}, bf16[768,1536]{1,0:T(8,128)(2,1)}, bf16[1536,768]{1,0:T(8,128)(2,1)...) custom-call(s32[504]{0:T(512)} %slots_ref.5, ...), custom_call_target="tpu_custom_call" | custom-call | tf_op jit(solution)/shard_map/unpack_and_attend/pallas_call | solution.py:686
  197.4 38.4 %encoder_and_fetch.1 = (f32[1024,768]{1,0:T(8,128)}, f32[1024,1]{1,0:T(8,128)}, f32[1024,768]{1,0:T(8,128)}, bf16[512,768]{1,0:T(8,128)(2,1)}, bf16[512,768]{1,0...) custom-call(bf16[1024,768]{1,0:T(8,128)(2,1)} %fusion.2.x_ref.refs_0, ...), custom_call_target="tpu_custom_call" | custom-call | tf_op jit(solution)/shard_map/encoder_and_fetch/pallas_call | solution.py:1373
  235.8 67.0 %decoder_core.1 = (f32[512,768]{1,0:T(8,128)}, bf16[512,768]{1,0:T(8,128)(2,1)}, bf16[512,384]{1,0:T(8,128)(2,1)}, bf16[512,768]{1,0:T(8,128)(2,1)}, bf16[512,15...) custom-call(f32[512,768]{1,0:T(8,128)} %get-tuple-element.108.refs_0, ...), custom_call_target="tpu_custom_call" | custom-call | tf_op jit(solution)/shard_map/decoder_core/pallas_call | solution.py:1373
  302.8 0.0 copy-start.2
  302.8 30.4 %encoder_backward.1 = (bf16[512,768]{1,0:T(8,128)(2,1)}, bf16[512,1536]{1,0:T(8,128)(2,1)}, f32[1,1536]{1,0:T(1,128)}, f32[8,768]{1,0:T(8,128)}, f32[8,768]{1,0:...) custom-call(bf16[1024,768]{1,0:T(8,128)(2,1)} %get-tuple-element.120, ...), custom_call_target="tpu_custom_call" | custom-call | tf_op jit(solution)/shard_map/encoder_backward/pallas_call | solution.py:1373
  333.2 0.0 copy-done.2
  333.2 6.9 %fusion = (f32[1024,768]{1,0:T(8,128)}, f32[1024,768]{1,0:T(8,128)}) fusion(s32[]{:T(128)S(6)} %select_n.37, f32[1024,768]{1,0:T(8,128)} %get-tuple-element.130, f32[1024,768]{1,0:T(8,128)S(1)} %copy-done.2), kind=kLoop, calls=%fused_computation.4 | loop fusion | flops 1572864 | bytes 12582916 | tf_op jit(solution)/shard_map/jit(_roll_dynamic)/concatenate | solution.py:1793
  340.1 12.8 %weight_grads.2.refs_19_ = bf16[512,128,128]{2,1,0:T(8,128)(2,1)} custom-call(s32[504]{0:T(512)} %slots_ref.5, bf16[512,1536]{1,0:T(8,128)(2,1)} %get-tuple-element.148.refs_0_, bf16[512,768]{1,0:T(8,128)(2,1)} %get-tuple-element.149.refs_1_, bf16[512,768]{1,0:T(8,128)(2,1)} %get-tuple-element.150.refs_2_, bf16[512,1536]{1,0:T(8,128)(2,1)} %get-tuple-element.151.refs_3_, ...), custom_call_target="tpu_custom_call" | custom-call | tf_op jit(solution)/shard_map/weight_grads/pallas_call | solution.py:805
  352.8 11.2 %weight_grads.3 = (bf16[512,128,128]{2,1,0:T(8,128)(2,1)}, f32[24,768]{1,0:T(8,128)}) custom-call(s32[504]{0:T(512)} %slots_ref.5, bf16[512,1536]{1,0:T(8,128)(2,1)} %get-tuple-element.123.refs_4_.refs_0_, bf16[512,768]{1,0:T(8,128)(2,1)} %get-tuple-element.132.refs_1_, ...), custom_call_target="tpu_custom_call", output_to_operand_aliasing={{0}: (20, {})} | custom-call | tf_op jit(solution)/shard_map/weight_grads/pallas_call | solution.py:805
  364.0 172.7 %owner_update.1 = (f32[32,128,128]{2,1,0:T(8,128)}, f32[32,128,128]{2,1,0:T(8,128)}, f32[32,128,128]{2,1,0:T(8,128)}, f32[32,128,128]{2,1,0:T(8,128)}, f32[32,12...) custom-call(s32[32]{0:T(128)} %convert_element_type.46.refs_0_, ...), custom_call_target="tpu_custom_call" | custom-call | tf_op jit(solution)/shard_map/owner_update/pallas_call | solution.py:485
  536.7 0.0 copy-start.6
  536.7 0.0 copy-start.9
  536.8 0.0 copy-start.10
  536.8 0.0 copy-start.5
  536.8 0.0 copy-start.7
  536.8 0.0 copy-start.8
  536.8 0.0 copy-start.4
  536.8 20.8 %last_bases.1 = (f32[32,128,128]{2,1,0:T(8,128)}, f32[32,128,128]{2,1,0:T(8,128)}, f32[32,128,128]{2,1,0:T(8,128)}, f32[32,128,128]{2,1,0:T(8,128)}, f32[32,128,...) custom-call(f32[16,128,256]{2,1,0:T(8,128)} %get-tuple-element.162.work_ref, ...), custom_call_target="tpu_custom_call" | custom-call | tf_op jit(solution)/shard_map/last_bases/pallas_call | solution.py:358
  557.6 0.0 copy-start.3
  557.6 0.0 copy-done.6
  557.7 0.0 copy-done.9
  557.7 0.0 copy-done.10
  557.7 0.9 subtract_bitcast_fusion
  558.6 0.0 copy-done.5
  558.6 0.0 copy-done.7
  558.6 0.0 copy-done.8
  558.6 1.4 divide_subtract_fusion
  560.0 0.6 copy.65
  560.6 0.6 copy.64
  561.2 0.6 copy.63
  561.8 0.0 copy-done.4
  561.8 0.0 copy-start.1
  561.8 1.1 copy.93
  562.9 0.0 copy-done.3
  562.9 1.1 copy.94
  564.1 0.0 copy-done.1
  (4 shorter events, 0.0 us)
Async XLA Ops:
  0.7 1.4 copy-start
  302.8 30.4 %copy-start.2 = (f32[1024,768]{1,0:T(8,128)S(1)}, f32[1024,768]{1,0:T(8,128)}, u32[]{:S(2)}) copy-start(f32[1024,768]{1,0:T(8,128)} %get-tuple-element.107) | copy-start | bytes 9437188
  536.7 20.9 %copy-start.6 = (f32[1,7,48]{2,0,1:T(1,128)S(1)}, f32[1,7,48]{2,0,1:T(1,128)}, u32[]{:S(2)}) copy-start(f32[1,7,48]{2,0,1:T(1,128)} %param.37) | copy-start | bytes 4036
  536.7 20.9 %copy-start.9 = (f32[1,7,48]{2,0,1:T(1,128)S(1)}, f32[1,7,48]{2,0,1:T(1,128)}, u32[]{:S(2)}) copy-start(f32[1,7,48]{2,0,1:T(1,128)} %param.38) | copy-start | bytes 4036
  536.8 20.9 %copy-start.10 = (f32[1,7,48]{2,0,1:T(1,128)S(1)}, f32[1,7,48]{2,0,1:T(1,128)}, u32[]{:S(2)}) copy-start(f32[1,7,48]{2,0,1:T(1,128)} %param.39) | copy-start | bytes 4036
  536.8 21.8 %copy-start.5 = (f32[15,48]{1,0:T(8,128)S(1)}, f32[15,48]{1,0:T(8,128)}, u32[]{:S(2)}) copy-start(f32[15,48]{1,0:T(8,128)} %param.34) | copy-start | bytes 8644
  536.8 21.8 %copy-start.7 = (f32[15,48]{1,0:T(8,128)S(1)}, f32[15,48]{1,0:T(8,128)}, u32[]{:S(2)}) copy-start(f32[15,48]{1,0:T(8,128)} %param.36) | copy-start | bytes 8644
  536.8 21.8 %copy-start.8 = (f32[15,48]{1,0:T(8,128)S(1)}, f32[15,48]{1,0:T(8,128)}, u32[]{:S(2)}) copy-start(f32[15,48]{1,0:T(8,128)} %param.35) | copy-start | bytes 8644
  536.8 25.0 %copy-start.4 = (f32[512,768]{1,0:T(8,128)S(1)}, f32[512,768]{1,0:T(8,128)}, u32[]{:S(2)}) copy-start(f32[512,768]{1,0:T(8,128)} %get-tuple-element.274) | copy-start | bytes 4718596
  557.6 5.3 copy-start.3
  561.8 2.3 copy-start.1
